TPU v7x, 32 devices: a whole 2x2x4 slice. The times are simulated.
32 devices in a mesh: rows: 4 (over x, core), cols: 8 (over z, y).
Axes of the slice: x: 2, y: 2, z: 4, core: 2. Of those that a mesh axis runs over, the one named last changes fastest.
Arguments:
- search_vectors: bfloat16 [4096, 1024], P(('rows', 'cols')), may hold values from -6 to 6
- tile_values: bfloat16 [64, 64, 512], P('rows'), may hold values from -0.25 to 0.25
- block_columns: int32 [64, 8], P('rows'), may hold values from -4 to 67, as said below
Outputs:
- filtered: bfloat16 [4096, 1024], P(('rows', 'cols'))
- gram: float32 [1024, 1024], P('cols')
Inputs may be any that keep to these rules, and one draw needn't show every extreme that they name: `block_columns`: row b names 8 distinct block columns, each within 4 of b, always including b - 4, b and b + 4; block columns outside 0 to 63 stand for zero tiles.
All inputs are finite; a program needn't handle non-finite values.
Results may differ from a plain program's by a relative error of at most 0.023.
Values may be sent and summed in bfloat16 or wider, within the bound.
No kernel may reach another device: no remote copies, remote signals or barrier semaphores. Data moves between devices by JAX's collectives and lax.ppermute only.
A program may use at most 64 MiB of HBM per device.

v0:
```python
import jax
import jax.numpy as jnp
from jax import lax
from jax.sharding import PartitionSpec as P

HALO = 4
DEGREE = 8


shift_value = 0.1
half_width = 2.0


def extended(shard, sides, width):
    for axis, dim in sides:
        size, length = (lax.axis_size(axis), shard.shape[dim])
        up = [(i, (i + 1) % size) for i in range(size - 1)]
        down = [(j, i) for i, j in up]
        last = lax.slice_in_dim(shard, length - width, length, axis=dim)
        first = lax.slice_in_dim(shard, 0, width, axis=dim)
        before = lax.ppermute(last, axis, up)
        after = lax.ppermute(first, axis, down)
        shard = jnp.concatenate([before, shard, after], axis=dim)
    return shard


def per_device(search_vectors, tile_values, block_columns):
    group_count = lax.axis_size("cols")
    row_part = lax.axis_index("rows")
    block_rows = tile_values.shape[0]
    tile_size = tile_values.shape[1]
    tile_count = block_columns.shape[1]
    columns = lax.all_to_all(search_vectors, "cols", split_axis=1, concat_axis=0, tiled=True)
    anchors = row_part * block_rows + jnp.arange(block_rows, dtype=jnp.int32)
    offsets = block_columns - anchors[:, None]
    split_tiles = tile_values.reshape(block_rows, tile_size, tile_count, tile_size)
    band_list = []
    for offset in range(-HALO, HALO + 1):
        selector = (offsets == offset).astype(jnp.float32)
        placed = jnp.einsum("bk,bikj->bij", selector, split_tiles.astype(jnp.float32))
        band_list.append(placed.astype(jnp.bfloat16))

    def filter_step(iterate):
        rounded = iterate.astype(jnp.bfloat16)
        padded = extended(rounded, (("rows", 0),), HALO * tile_size)
        stacked = padded.reshape(block_rows + 2 * HALO, tile_size, rounded.shape[1])
        product = jnp.zeros((block_rows, tile_size, rounded.shape[1]), jnp.float32)
        for position in range(2 * HALO + 1):
            window = lax.slice_in_dim(stacked, position, position + block_rows, axis=0)
            product = product + jnp.einsum(
                "bij,bjc->bic", band_list[position], window, preferred_element_type=jnp.float32
            )
        return (product.reshape(iterate.shape) - shift_value * iterate) / half_width

    previous = columns.astype(jnp.float32)
    current = filter_step(previous)
    for degree_step in range(DEGREE - 1):
        following = 2.0 * filter_step(current) - previous
        previous, current = (current, following)
    filtered = current.astype(jnp.bfloat16)
    rowwise = lax.all_to_all(filtered, "cols", split_axis=0, concat_axis=1, tiled=True)
    width = rowwise.shape[1]
    share_rows = width // group_count
    total_rows = block_rows * tile_size * lax.axis_size("rows")
    partial_value = lax.dot_general(
        rowwise, rowwise, (((0,), (0,)), ((), ())), preferred_element_type=jnp.float32
    )
    group_sum = lax.psum(partial_value.astype(jnp.bfloat16), "cols")
    summed = lax.psum(group_sum, "rows").astype(jnp.float32)
    gram = lax.dynamic_slice_in_dim(summed, lax.axis_index("cols") * share_rows, share_rows, 0)
    return (rowwise, gram * (1.0 / total_rows))


def solution(mesh):
    return jax.shard_map(
        per_device,
        mesh=mesh,
        in_specs=(P(("rows", "cols"), None), P("rows", None, None), P("rows", None)),
        out_specs=(P(("rows", "cols"), None), P("cols", None)),
        check_vma=False,
    )
```

profile of v0, /device:TPU:1, one launch (start us, length us, event | category | flops | bytes accessed | tf_op | source)
XLA Modules:
  0.0 288.3 jit_solution(12723534631785812662)
XLA Ops:
  8.9 6.4 %all-to-all-start = ((bf16[128,8,128]{2,0,1:T(8,128)(2,1)}), bf16[128,8,128]{2,0,1:T(8,128)(2,1)S(1)}, u32[]{:S(2)}, u32[]{:S(2)}) async-start(bf16[128,8,128]{2,0,1:T(8,128)(2,1)} %copy_bitcast_fusion.1), calls=%async_computation | async-start | bytes 524288 | tf_op jit(solution)/shard_map/all_to_all | solution.py:33
  16.1 2.8 reshape.153
  29.2 4.0 %collective-permute-start = (bf16[256,128]{1,0:T(8,128)(2,1)S(1)}, bf16[256,128]{1,0:T(8,128)(2,1)S(1)}, u32[]{:S(2)}, u32[]{:S(2)}) collective-permute-start(bf16[256,128]{1,0:T(8,128)(2,1)S(1)} %bitcast.494), channel_id=1, source_target_pairs={{0,8},{8,16},{16,24},{1,9},{9,17},{17,25},{2,10},{10,18},{18,26},{... | collective-permute-start | bytes 196616 | tf_op jit(solution)/shard_map/ppermute | solution.py:21
  33.2 1.9 collective-permute-start.1
  35.1 1.2 fusion.114
  36.3 2.5 collective-permute-done.1
  41.8 1.9 collective-permute-start.2
  43.8 2.4 collective-permute-start.3
  46.4 2.9 %collective-permute-done.3 = bf16[256,128]{1,0:T(8,128)(2,1)S(1)} collective-permute-done((bf16[256,128]{1,0:T(8,128)(2,1)S(1)}, bf16[256,128]{1,0:T(8,128)(2,1)S(1)}, u32[]{:S(2)}, u32[]{:S(2)}) %collective-permute-start.3) | collective-permute-done | bytes 65568 | tf_op jit(solution)/shard_map/ppermute | solution.py:22
  51.6 1.9 collective-permute-start.4
  53.6 2.6 collective-permute-start.5
  56.4 2.7 collective-permute-done.5
  61.6 1.9 collective-permute-start.6
  63.5 2.4 collective-permute-start.7
  66.1 2.9 %collective-permute-done.7 = bf16[256,128]{1,0:T(8,128)(2,1)S(1)} collective-permute-done((bf16[256,128]{1,0:T(8,128)(2,1)S(1)}, bf16[256,128]{1,0:T(8,128)(2,1)S(1)}, u32[]{:S(2)}, u32[]{:S(2)}) %collective-permute-start.7) | collective-permute-done | bytes 65568 | tf_op jit(solution)/shard_map/ppermute | solution.py:22
  71.5 1.9 collective-permute-start.8
  73.4 2.4 collective-permute-start.9
  76.1 2.9 %collective-permute-done.9 = bf16[256,128]{1,0:T(8,128)(2,1)S(1)} collective-permute-done((bf16[256,128]{1,0:T(8,128)(2,1)S(1)}, bf16[256,128]{1,0:T(8,128)(2,1)S(1)}, u32[]{:S(2)}, u32[]{:S(2)}) %collective-permute-start.9) | collective-permute-done | bytes 65568 | tf_op jit(solution)/shard_map/ppermute | solution.py:22
  81.2 1.9 collective-permute-start.10
  83.2 2.4 collective-permute-start.11
  85.8 2.9 %collective-permute-done.11 = bf16[256,128]{1,0:T(8,128)(2,1)S(1)} collective-permute-done((bf16[256,128]{1,0:T(8,128)(2,1)S(1)}, bf16[256,128]{1,0:T(8,128)(2,1)S(1)}, u32[]{:S(2)}, u32[]{:S(2)}) %collective-permute-start.11) | collective-permute-done | bytes 65568 | tf_op jit(solution)/shard_map/ppermute | solution.py:22
  91.0 1.9 collective-permute-start.12
  92.9 2.4 collective-permute-start.13
  95.6 2.9 %collective-permute-done.13 = bf16[256,128]{1,0:T(8,128)(2,1)S(1)} collective-permute-done((bf16[256,128]{1,0:T(8,128)(2,1)S(1)}, bf16[256,128]{1,0:T(8,128)(2,1)S(1)}, u32[]{:S(2)}, u32[]{:S(2)}) %collective-permute-start.13) | collective-permute-done | bytes 65568 | tf_op jit(solution)/shard_map/ppermute | solution.py:22
  100.8 1.9 collective-permute-start.14
  102.7 2.6 collective-permute-start.15
  105.7 2.6 collective-permute-done.15
  110.9 13.4 %all_to_all.35 = bf16[8,128,128]{2,1,0:T(8,128)(2,1)S(1)} all-to-all(bf16[8,128,128]{2,1,0:T(8,128)(2,1)S(1)} %fusion.19), channel_id=1, replica_groups=mesh['rows'=4,'cols'=8] {'cols'}, dimensions={0} | all-to-all | bytes 524288 | tf_op jit(solution)/shard_map/all_to_all | solution.py:61
  124.4 2.1 convolution_convert_fusion
  126.5 99.4 %all-reduce.3.cloned.1.call-done = bf16[1024,1024]{1,0:T(8,128)(2,1)} async-done(((bf16[1024,1024]{1,0:T(8,128)(2,1)}), bf16[1024,1024]{1,0:T(8,128)(2,1)}) %all-reduce.3.cloned.1.call-update) | async-done | bytes 2097168 | tf_op jit(solution)/shard_map/psum | solution.py:68
  226.0 53.6 %all-reduce.5.cloned.1.call-done = bf16[1024,1024]{1,0:T(8,128)(2,1)} async-done(((bf16[1024,1024]{1,0:T(8,128)(2,1)}), bf16[1024,1024]{1,0:T(8,128)(2,1)}) %all-reduce.5.cloned.1.call-update) | async-done | bytes 2097168 | tf_op jit(solution)/shard_map/psum | solution.py:69
  279.6 1.8 convert_multiply_fusion.3
  (153 shorter events, 33.5 us)
Async XLA Ops:
  7.2 1.0 copy-start
  8.9 20.4 %all-to-all-start = ((bf16[128,8,128]{2,0,1:T(8,128)(2,1)}), bf16[128,8,128]{2,0,1:T(8,128)(2,1)S(1)}, u32[]{:S(2)}, u32[]{:S(2)}) async-start(bf16[128,8,128]{2,0,1:T(8,128)(2,1)} %copy_bitcast_fusion.1), calls=%async_computation | async-start | bytes 524288 | tf_op jit(solution)/shard_map/all_to_all | solution.py:33
  15.3 210.7 %all-reduce.3.cloned.1.call-start = ((), (), s32[]{:S(2)}) async-start(), calls=%async_computation.2 | async-start | bytes 4194304 | tf_op jit(solution)/shard_map/psum | solution.py:68
  29.2 7.1 %collective-permute-start = (bf16[256,128]{1,0:T(8,128)(2,1)S(1)}, bf16[256,128]{1,0:T(8,128)(2,1)S(1)}, u32[]{:S(2)}, u32[]{:S(2)}) collective-permute-start(bf16[256,128]{1,0:T(8,128)(2,1)S(1)} %bitcast.494), channel_id=1, source_target_pairs={{0,8},{8,16},{16,24},{1,9},{9,17},{17,25},{2,10},{10,18},{18,26},{... | collective-permute-start | bytes 196616 | tf_op jit(solution)/shard_map/ppermute | solution.py:21
  33.2 5.6 %collective-permute-start.1 = (bf16[256,128]{1,0:T(8,128)(2,1)S(1)}, bf16[256,128]{1,0:T(8,128)(2,1)S(1)}, u32[]{:S(2)}, u32[]{:S(2)}) collective-permute-start(bf16[256,128]{1,0:T(8,128)(2,1)S(1)} %bitcast.493), channel_id=1, source_target_pairs={{8,0},{16,8},{24,16},{9,1},{17,9},{25,17},{10,2},{18,10},{26,18},{... | collective-permute-start | bytes 196616 | tf_op jit(solution)/shard_map/ppermute | solution.py:22
  39.1 1.0 copy-start.5
  39.8 1.0 copy-start.2
  40.3 1.0 copy-start.3
  41.3 4.9 %copy-start.4 = (bf16[16,64,64]{2,1,0:T(8,128)(2,1)S(1)}, bf16[16,64,64]{2,1,0:T(8,128)(2,1)}, u32[]{:S(2)}) copy-start(bf16[16,64,64]{2,1,0:T(8,128)(2,1)} %convert_element_type.117) | copy-start | bytes 393220
  41.8 4.6 %collective-permute-start.2 = (bf16[256,128]{1,0:T(8,128)(2,1)S(1)}, bf16[256,128]{1,0:T(8,128)(2,1)S(1)}, u32[]{:S(2)}, u32[]{:S(2)}) collective-permute-start(bf16[256,128]{1,0:T(8,128)(2,1)S(1)} %get-tuple-element.111), channel_id=1, source_target_pairs={{0,8},{8,16},{16,24},{1,9},{9,17},{17,25},{2,10},{10,18},{18,26},{... | collective-permute-start | bytes 196616 | tf_op jit(solution)/shard_map/ppermute | solution.py:21
  43.8 5.6 %collective-permute-start.3 = (bf16[256,128]{1,0:T(8,128)(2,1)S(1)}, bf16[256,128]{1,0:T(8,128)(2,1)S(1)}, u32[]{:S(2)}, u32[]{:S(2)}) collective-permute-start(bf16[256,128]{1,0:T(8,128)(2,1)S(1)} %get-tuple-element.110), channel_id=1, source_target_pairs={{8,0},{16,8},{24,16},{9,1},{17,9},{25,17},{10,2},{18,10},{26,18},{... | collective-permute-start | bytes 196616 | tf_op jit(solution)/shard_map/ppermute | solution.py:22
  51.6 4.8 %collective-permute-start.4 = (bf16[256,128]{1,0:T(8,128)(2,1)S(1)}, bf16[256,128]{1,0:T(8,128)(2,1)S(1)}, u32[]{:S(2)}, u32[]{:S(2)}) collective-permute-start(bf16[256,128]{1,0:T(8,128)(2,1)S(1)} %get-tuple-element.105), channel_id=1, source_target_pairs={{0,8},{8,16},{16,24},{1,9},{9,17},{17,25},{2,10},{10,18},{18,26},{... | collective-permute-start | bytes 196616 | tf_op jit(solution)/shard_map/ppermute | solution.py:21
  53.6 5.6 %collective-permute-start.5 = (bf16[256,128]{1,0:T(8,128)(2,1)S(1)}, bf16[256,128]{1,0:T(8,128)(2,1)S(1)}, u32[]{:S(2)}, u32[]{:S(2)}) collective-permute-start(bf16[256,128]{1,0:T(8,128)(2,1)S(1)} %get-tuple-element.104), channel_id=1, source_target_pairs={{8,0},{16,8},{24,16},{9,1},{17,9},{25,17},{10,2},{18,10},{26,18},{... | collective-permute-start | bytes 196616 | tf_op jit(solution)/shard_map/ppermute | solution.py:22
  61.6 4.6 %collective-permute-start.6 = (bf16[256,128]{1,0:T(8,128)(2,1)S(1)}, bf16[256,128]{1,0:T(8,128)(2,1)S(1)}, u32[]{:S(2)}, u32[]{:S(2)}) collective-permute-start(bf16[256,128]{1,0:T(8,128)(2,1)S(1)} %get-tuple-element.99), channel_id=1, source_target_pairs={{0,8},{8,16},{16,24},{1,9},{9,17},{17,25},{2,10},{10,18},{18,26},{... | collective-permute-start | bytes 196616 | tf_op jit(solution)/shard_map/ppermute | solution.py:21
  63.5 5.6 %collective-permute-start.7 = (bf16[256,128]{1,0:T(8,128)(2,1)S(1)}, bf16[256,128]{1,0:T(8,128)(2,1)S(1)}, u32[]{:S(2)}, u32[]{:S(2)}) collective-permute-start(bf16[256,128]{1,0:T(8,128)(2,1)S(1)} %get-tuple-element.98), channel_id=1, source_target_pairs={{8,0},{16,8},{24,16},{9,1},{17,9},{25,17},{10,2},{18,10},{26,18},{... | collective-permute-start | bytes 196616 | tf_op jit(solution)/shard_map/ppermute | solution.py:22
  71.5 4.6 %collective-permute-start.8 = (bf16[256,128]{1,0:T(8,128)(2,1)S(1)}, bf16[256,128]{1,0:T(8,128)(2,1)S(1)}, u32[]{:S(2)}, u32[]{:S(2)}) collective-permute-start(bf16[256,128]{1,0:T(8,128)(2,1)S(1)} %get-tuple-element.93), channel_id=1, source_target_pairs={{0,8},{8,16},{16,24},{1,9},{9,17},{17,25},{2,10},{10,18},{18,26},{... | collective-permute-start | bytes 196616 | tf_op jit(solution)/shard_map/ppermute | solution.py:21
  73.4 5.6 %collective-permute-start.9 = (bf16[256,128]{1,0:T(8,128)(2,1)S(1)}, bf16[256,128]{1,0:T(8,128)(2,1)S(1)}, u32[]{:S(2)}, u32[]{:S(2)}) collective-permute-start(bf16[256,128]{1,0:T(8,128)(2,1)S(1)} %get-tuple-element.92), channel_id=1, source_target_pairs={{8,0},{16,8},{24,16},{9,1},{17,9},{25,17},{10,2},{18,10},{26,18},{... | collective-permute-start | bytes 196616 | tf_op jit(solution)/shard_map/ppermute | solution.py:22
  81.2 4.6 %collective-permute-start.10 = (bf16[256,128]{1,0:T(8,128)(2,1)S(1)}, bf16[256,128]{1,0:T(8,128)(2,1)S(1)}, u32[]{:S(2)}, u32[]{:S(2)}) collective-permute-start(bf16[256,128]{1,0:T(8,128)(2,1)S(1)} %get-tuple-element.87), channel_id=1, source_target_pairs={{0,8},{8,16},{16,24},{1,9},{9,17},{17,25},{2,10},{10,18},{18,26},{... | collective-permute-start | bytes 196616 | tf_op jit(solution)/shard_map/ppermute | solution.py:21
  83.2 5.6 %collective-permute-start.11 = (bf16[256,128]{1,0:T(8,128)(2,1)S(1)}, bf16[256,128]{1,0:T(8,128)(2,1)S(1)}, u32[]{:S(2)}, u32[]{:S(2)}) collective-permute-start(bf16[256,128]{1,0:T(8,128)(2,1)S(1)} %get-tuple-element.86), channel_id=1, source_target_pairs={{8,0},{16,8},{24,16},{9,1},{17,9},{25,17},{10,2},{18,10},{26,18},{... | collective-permute-start | bytes 196616 | tf_op jit(solution)/shard_map/ppermute | solution.py:22
  91.0 4.6 %collective-permute-start.12 = (bf16[256,128]{1,0:T(8,128)(2,1)S(1)}, bf16[256,128]{1,0:T(8,128)(2,1)S(1)}, u32[]{:S(2)}, u32[]{:S(2)}) collective-permute-start(bf16[256,128]{1,0:T(8,128)(2,1)S(1)} %get-tuple-element.81), channel_id=1, source_target_pairs={{0,8},{8,16},{16,24},{1,9},{9,17},{17,25},{2,10},{10,18},{18,26},{... | collective-permute-start | bytes 196616 | tf_op jit(solution)/shard_map/ppermute | solution.py:21
  92.9 5.6 %collective-permute-start.13 = (bf16[256,128]{1,0:T(8,128)(2,1)S(1)}, bf16[256,128]{1,0:T(8,128)(2,1)S(1)}, u32[]{:S(2)}, u32[]{:S(2)}) collective-permute-start(bf16[256,128]{1,0:T(8,128)(2,1)S(1)} %get-tuple-element.80), channel_id=1, source_target_pairs={{8,0},{16,8},{24,16},{9,1},{17,9},{25,17},{10,2},{18,10},{26,18},{... | collective-permute-start | bytes 196616 | tf_op jit(solution)/shard_map/ppermute | solution.py:22
  100.8 4.9 %collective-permute-start.14 = (bf16[256,128]{1,0:T(8,128)(2,1)S(1)}, bf16[256,128]{1,0:T(8,128)(2,1)S(1)}, u32[]{:S(2)}, u32[]{:S(2)}) collective-permute-start(bf16[256,128]{1,0:T(8,128)(2,1)S(1)} %get-tuple-element.75), channel_id=1, source_target_pairs={{0,8},{8,16},{16,24},{1,9},{9,17},{17,25},{2,10},{10,18},{18,26},{... | collective-permute-start | bytes 196616 | tf_op jit(solution)/shard_map/ppermute | solution.py:21
  102.7 5.6 %collective-permute-start.15 = (bf16[256,128]{1,0:T(8,128)(2,1)S(1)}, bf16[256,128]{1,0:T(8,128)(2,1)S(1)}, u32[]{:S(2)}, u32[]{:S(2)}) collective-permute-start(bf16[256,128]{1,0:T(8,128)(2,1)S(1)} %get-tuple-element.74), channel_id=1, source_target_pairs={{8,0},{16,8},{24,16},{9,1},{17,9},{25,17},{10,2},{18,10},{26,18},{... | collective-permute-start | bytes 196616 | tf_op jit(solution)/shard_map/ppermute | solution.py:22
  124.4 2.1 copy-start.6
  126.4 155.0 %copy-start.1 = (bf16[128,1024]{1,0:T(8,128)(2,1)S(1)}, bf16[128,1024]{1,0:T(8,128)(2,1)}, u32[]{:S(2)}) copy-start(bf16[128,1024]{1,0:T(8,128)(2,1)} %param.3) | copy-start | bytes 786436
  126.5 153.1 %all-reduce.5.cloned.1.call-start = ((), (), s32[]{:S(2)}) async-start(), calls=%async_computation.3 | async-start | bytes 4194304 | tf_op jit(solution)/shard_map/psum | solution.py:69
Sparse Core Ops, SparseCore 0:
  126.6 99.3 all-reduce.2
  228.3 51.2 all-reduce.4
where the time goes:
time: 290 us; the launch traced here: 288 us
  waiting for transfers between devices  176 us (61%)
  starting transfers between devices  43 us (15%)
  matrix products  25.2 us (9%)
  between operations  15 us (5%)
  blocking collectives  13.4 us (5%)
  other arithmetic  9.77 us (3%)
  local copies, waits for them, and re-layouts  6.25 us (2%)
    psum x1, waiting for transfers between devices, per_device(): group_sum = lax.psum(partial_value.astype(jnp.bfloat16), 'cols')  99.4 us
    psum x1, waiting for transfers between devices, per_device(): summed = lax.psum(group_sum, 'rows').astype(jnp.float32)  53.6 us
    ppermute x8, waiting for transfers between devices, extended(): after = lax.ppermute(first, axis, down)  22.5 us
    ppermute x8, starting transfers between devices, extended(): after = lax.ppermute(first, axis, down)  19.2 us
    ppermute x8, starting transfers between devices, extended(): before = lax.ppermute(last, axis, up)  17.4 us
    dot_general x72, matrix products, filter_step(): jnp.einsum('bij,bjc->bic', band_list[position], window, preferred_element...  16.9 us
    all_to_all x1, blocking collectives, per_device(): lax.all_to_all(filtered, 'cols', split_axis=0, concat_axis=1, tiled=True)  13.4 us
    all_to_all x1, starting transfers between devices, per_device(): lax.all_to_all(search_vectors, 'cols', split_axis=1, concat_axis=0, tiled...  6.38 us
  transfers between devices with their start and end apart: 19, of which 10 were waited for; matrix products, arithmetic and copies ran while one was open for 6% of the time, Pallas kernels for 0%

commit v1 on v0

v1 whole, which is shorter than its diff:
```python
import functools

import functools

import jax
import jax.numpy as jnp
from jax import lax
from jax.experimental import pallas as pl
from jax.experimental.pallas import tpu as pltpu
from jax.sharding import PartitionSpec as P

HALO = 4
DEGREE = 8
STAGE = 4
REACH = HALO * STAGE
TILES_REACH = REACH - HALO
SPAN = 3

shift_value = 0.1
half_width = 2.0

SMEM = pl.BlockSpec(memory_space=pltpu.SMEM)
VMEM = pl.BlockSpec(memory_space=pltpu.VMEM)


def params(mebibytes):
    return pltpu.CompilerParams(vmem_limit_bytes=mebibytes * 1024 * 1024)


def with_core(value):
    return lax.ppermute(value, "rows", [(i, i ^ 1) for i in range(lax.axis_size("rows"))])


def with_chip(value):
    odds = range(1, lax.axis_size("rows") - 1, 2)
    return lax.ppermute(value, "rows", [p for k in odds for p in ((k, k + 1), (k + 1, k))])


def place_group(offsets, ahead, tiles, start, bands, band, doubled, slot):
    kt = offsets.shape[0]
    tile = tiles.shape[1]
    blank = kt
    nothing = jnp.zeros((tile, tile), doubled.dtype)
    for i in range(HALO):
        values = tiles[start + i]
        for k in range(kt):
            one = values[:, k * tile:(k + 1) * tile]
            doubled[i, k] = jnp.concatenate([one, one], axis=1)
        for place in range(2 * HALO + 1):
            slot[i, place] = blank
        for k in range(kt):
            slot[i, offsets[k, ahead + start + i] + HALO] = k
    for i in range(HALO):
        rows = slice(i * tile, (i + 1) * tile)
        for pair in range(SPAN * HALO // 2):
            halves = []
            for side in range(2):
                place = 2 * pair + side - i
                if 0 <= place <= 2 * HALO:
                    both = doubled[i, slot[i, place]]
                    halves.append(both[:, side * tile:(side + 1) * tile])
                else:
                    halves.append(nothing)
            columns = slice(2 * pair * tile, 2 * (pair + 1) * tile)
            bands[band, rows, columns] = jnp.concatenate(halves, axis=1)


def clear(doubled):
    doubled[:, doubled.shape[1] - 1] = jnp.zeros(
        doubled.shape[:1] + doubled.shape[2:], doubled.dtype
    )


def split_columns(vectors, pieces):
    width = pieces.shape[2]
    for i in range(pieces.shape[0]):
        pieces[i] = vectors[:, i * width:(i + 1) * width]


def own_bands(odd, offsets, columns, tiles, _, bands, to_first, columns_out, doubled, slot):
    count = tiles.shape[0]
    sent = to_first.shape[0]
    to_first[...] = tiles[pl.ds((1 - odd[0]) * (count - sent), sent)]
    columns_out[...] = columns[...]
    clear(doubled)

    @pl.loop(0, count // HALO)
    def _(g):
        place_group(offsets, 0, tiles, g * HALO, bands, g, doubled, slot)


def edge_bands(odd, at_first, at_second, first, second, bands, doubled, slot):
    count = at_first.shape[1]
    edge = TILES_REACH // HALO
    clear(doubled)
    for offsets, tiles, behind in ((at_first, first, odd[0]), (at_second, second, 1 - odd[0])):
        begin = behind * (count - TILES_REACH)
        band = (1 - behind) * edge
        skipped = begin * (tiles.shape[0] // count)

        @pl.loop(0, edge)
        def _(g, offsets=offsets, tiles=tiles, begin=begin, band=band, skipped=skipped):
            place_group(offsets, begin - skipped, tiles, skipped + g * HALO, bands, band + g,
                        doubled, slot)


def run_steps(own, edges, w, y, degree):
    middle, size, span = own.shape
    edge = edges.shape[0] // 2
    bands = [edges.at[j] for j in range(edge)]
    bands += [own.at[j] for j in range(middle)]
    bands += [edges.at[edge + j] for j in range(edge)]
    groups = len(bands)
    cur, new = y
    src, dst = w
    for step in range(STAGE):
        for j in range(step, groups - step):
            start = j * size
            here = slice(start + size, start + 2 * size)
            product = dot(bands[j][...], src[start:start + span])
            value = product - shift_value * cur[here]
            value = value / half_width if degree + step == 0 else value - new[here]
            new[here] = value
            dst[here] = value.astype(jnp.bfloat16)
        cur, new = new, cur
        src, dst = dst, src
    return cur, new, src


def placed(behind, rows):
    return pl.multiple_of((1 - behind) * 2 * rows, rows)


def first_stage(odd, own, edges, x_first, x_own, x_second, now_out, last_out, sent_out,
                w0, w1, y0, y1):
    rows = x_own.shape[0]
    size = own.shape[1]
    starts = (placed(odd[0], rows), rows, placed(1 - odd[0], rows))
    for start, ref in zip(starts, (x_first, x_own, x_second)):
        w0[pl.ds(start, rows)] = ref[...]
        y0[pl.ds(start, rows)] = ref[...].astype(jnp.float32)
    cur, prev, rounded = run_steps(own, edges, (w0, w1), (y0, y1), 0)
    now_out[...] = cur[rows:2 * rows]
    last_out[...] = prev[rows - size:2 * rows + size]
    sent_out[:rows] = rounded[rows:2 * rows]
    sent_out[rows:] = prev[rows + size:2 * rows - size].astype(jnp.bfloat16)


def second_stage(odd, own, edges, now, last, got_first, got_second, out, w0, w1, y0, y1):
    rows = now.shape[0]
    size = own.shape[1]
    here = slice(rows, 2 * rows)
    w0[here] = now[...].astype(jnp.bfloat16)
    y0[here] = now[...]
    y1[rows - size:2 * rows + size] = last[...]
    for got, behind in ((got_first, odd[0]), (got_second, 1 - odd[0])):
        start = placed(behind, rows)
        w0[pl.ds(start, rows)] = got[:rows]
        y0[pl.ds(start, rows)] = got[:rows].astype(jnp.float32)
        y1[pl.ds(pl.multiple_of(start + size, size), rows - 2 * size)] = (
            got[rows:].astype(jnp.float32)
        )
    _, _, rounded = run_steps(own, edges, (w0, w1), (y0, y1), STAGE)
    out[...] = rounded[here]


def dot(a, b):
    return jnp.dot(a, b, preferred_element_type=jnp.float32)


def columns_at(ref, group, width):
    if len(ref.shape) == 2:
        return slice(None), pl.ds(pl.multiple_of(group * width, width), width)
    return (group,)


def whole(chunk):
    low, high = chunk
    return jnp.concatenate([low[...], high[...]], axis=0)


def in_pairs(chunks):
    return [chunks[t:t + 2] for t in range(0, len(chunks), 2)]


def early_gram(mine, *refs):
    *chunks, partial, lefts = refs
    half = mine.shape[0] // 2
    left = mine[...].T
    lefts[0] = left
    for t, chunk in enumerate([(mine.at[:half], mine.at[half:])] + in_pairs(chunks)):
        block = whole(chunk)
        if t:
            lefts[t] = block.T
        partial[t] = dot(left, block)


def rows_of(chunk, device, share, put):
    low, high = chunk
    half = low.shape[0]
    start = pl.multiple_of(device * share, share)

    @pl.when(start < half)
    def _():
        put(low[pl.ds(start, share)])

    @pl.when(start >= half)
    def _():
        put(high[pl.ds(start - half, share)])


def late_gram(where, lefts, *refs):
    back, front = refs[:2], refs[2:4]
    partial, *messages = refs[4:]
    width = partial.shape[1]
    share = messages[0].shape[0] - width
    reach = lefts.shape[0] // 2 + 1
    far_back, far_front = whole(back), whole(front)
    partial[0] = dot(lefts[0], far_back)
    partial[1] = dot(lefts[0], far_front)
    made = []
    for t in range(1, reach):
        made.append((dot(lefts[2 * t], far_back), back, where[2 * t]))
        made.append((dot(lefts[2 * t - 1], far_front), front, where[2 * t - 1]))
    made.append((dot(far_back.T, far_front), front, where[2 * reach - 1]))
    for message, (block, chunk, device) in zip(messages, made):
        message[:width] = block.astype(message.dtype)

        def put(rows, message=message):
            message[width:] = rows

        rows_of(chunk, device, share, put)


def assemble(where, early, late, *refs):
    *messages, partial = refs
    width = early.shape[1]
    held = early.shape[0]
    blocks = [early[t] for t in range(held)] + [late[0], late[1]]
    blocks += [message[:width].astype(jnp.float32) for message in messages]
    for t, block in enumerate(blocks):
        partial[columns_at(partial, where[t], width)] = block


def filtered_rows(number, where, mine, *refs):
    chunks, messages, rowwise = refs[:number], refs[number:-1], refs[-1]
    rows, width = mine.shape
    half = rows // 2
    share = rowwise.shape[-2]
    for t, chunk in enumerate([(mine.at[:half], mine.at[half:])] + in_pairs(chunks)):

        def put(rows, t=t):
            rowwise[columns_at(rowwise, where[t], width)] = rows

        rows_of(chunk, where[0], share, put)
    for t, message in enumerate(messages):
        at = columns_at(rowwise, where[1 + number // 2 + t], width)
        rowwise[at] = message[width:]


def ring_of(size):
    return list(range(0, size, 2)) + list(range(size - 1, 0, -2))


def gram_and_rows(mine):
    size = lax.axis_size("cols")
    device = lax.axis_index("cols")
    assert size % 4 == 0
    reach = size // 4
    order = ring_of(size)
    rows, width = mine.shape
    half = rows // 2
    share = rows // size

    def move(value, by):
        return lax.ppermute(
            value, "cols", [(order[i], order[(i + by) % size]) for i in range(size)]
        )

    low_ahead = low_behind = mine[:half]
    high_ahead = high_behind = mine[half:]
    chunks, steps = [], [0]
    for t in range(1, reach + 1):
        low_ahead, high_behind = move(low_ahead, 1), move(high_behind, -1)
        high_ahead, low_behind = move(high_ahead, 1), move(low_behind, -1)
        chunks += [low_ahead, high_ahead, low_behind, high_behind]
        steps += [-t, t]
    sends = [by for t in range(1, reach) for by in (t, -t)] + [-reach]
    steps += [-(by + reach) if by > 0 else reach - by for by in sends]

    place = jnp.where(device % 2 == 0, device // 2, size - 1 - device // 2)
    where = (place + jnp.array(steps, jnp.int32)) % size
    where = jnp.where(where < size // 2, 2 * where, 2 * (size - 1 - where) + 1)

    held = 2 * reach - 1
    early, lefts = pl.pallas_call(
        early_gram,
        out_shape=(
            jax.ShapeDtypeStruct((held, width, width), jnp.float32),
            jax.ShapeDtypeStruct((held, width, rows), mine.dtype),
        ),
        in_specs=[VMEM] * (1 + 4 * (reach - 1)),
        out_specs=(VMEM, VMEM),
        compiler_params=params(16),
    )(mine, *chunks[:-4])
    message = jax.ShapeDtypeStruct((width + share, width), mine.dtype)
    late, *messages = pl.pallas_call(
        late_gram,
        out_shape=(jax.ShapeDtypeStruct((2, width, width), jnp.float32),)
        + (message,) * len(sends),
        in_specs=[SMEM] + [VMEM] * 5,
        out_specs=(VMEM,) * (1 + len(sends)),
        compiler_params=params(16),
    )(where, lefts, *chunks[-4:])
    messages = [move(value, by) for value, by in zip(messages, sends)]

    flat = width % 128 == 0
    shape = (lambda n: (n, size * width)) if flat else (lambda n: (size, n, width))
    partial = pl.pallas_call(
        assemble,
        out_shape=jax.ShapeDtypeStruct(shape(width), jnp.float32),
        in_specs=[SMEM] + [VMEM] * (2 + len(messages)),
        out_specs=VMEM,
        compiler_params=params(16),
    )(where, early, late, *messages)
    rowwise = pl.pallas_call(
        functools.partial(filtered_rows, len(chunks)),
        out_shape=jax.ShapeDtypeStruct(shape(share), mine.dtype),
        in_specs=[SMEM] + [VMEM] * (1 + len(chunks) + len(messages)),
        out_specs=VMEM,
        compiler_params=params(16),
    )(where, mine, *chunks, *messages)
    if not flat:
        partial = partial.transpose(1, 0, 2).reshape(width, size * width)
        rowwise = rowwise.transpose(1, 0, 2).reshape(share, size * width)
    return partial, rowwise


def sum_over_rows(partial):
    size = lax.axis_size("rows")
    me = lax.axis_index("rows")
    half = partial.shape[0] // 2
    odd = me & 1
    partner = [(i, i ^ 1) for i in range(size)]
    halves = partial.reshape(2, half, partial.shape[1])
    keep = lax.dynamic_index_in_dim(halves, odd, 0, keepdims=False)
    give = lax.dynamic_index_in_dim(halves, 1 - odd, 0, keepdims=False)
    total = keep + lax.ppermute(give, "rows", partner)
    bit = 2
    while bit < size:
        sent = total.astype(jnp.bfloat16)
        got = lax.ppermute(sent, "rows", [(i, i ^ bit) for i in range(size)])
        total = sent.astype(jnp.float32) + got.astype(jnp.float32)
        bit *= 2
    other = lax.ppermute(total, "rows", partner)
    low = jnp.where(odd == 0, total, other)
    high = jnp.where(odd == 0, other, total)
    return jnp.concatenate([low, high], axis=0)


def per_device(search_vectors, tile_values, block_columns):
    row_part = lax.axis_index("rows")
    row_parts = lax.axis_size("rows")
    col_parts = lax.axis_size("cols")
    count, tile, depth = tile_values.shape
    kt = block_columns.shape[1]
    assert REACH == count
    share = search_vectors.shape[0]
    width = search_vectors.shape[1] // col_parts
    rows = share * col_parts
    second = with_chip(tile_values)
    pieces = pl.pallas_call(
        split_columns,
        out_shape=jax.ShapeDtypeStruct((col_parts, share, width), search_vectors.dtype),
        in_specs=[VMEM],
        out_specs=VMEM,
        compiler_params=params(4),
    )(search_vectors)
    columns = lax.all_to_all(pieces, "cols", split_axis=0, concat_axis=0, tiled=True)
    columns = columns.reshape(rows, width)

    size = HALO * tile
    odd = row_part & 1
    block_columns = block_columns.T
    inner = jnp.arange(count, dtype=jnp.int32)

    def offsets_of(columns, part):
        return jnp.clip(columns - (part * count + inner), -HALO, HALO)

    scratch = [
        pltpu.VMEM((HALO, kt + 1, tile, 2 * tile), jnp.bfloat16),
        pltpu.SMEM((HALO, 2 * HALO + 1), jnp.int32),
    ]
    bands, to_first, sent_columns = pl.pallas_call(
        own_bands,
        out_shape=(
            jax.ShapeDtypeStruct((count // HALO, size, SPAN * size), jnp.bfloat16),
            jax.ShapeDtypeStruct((TILES_REACH, tile, depth), jnp.bfloat16),
            jax.ShapeDtypeStruct((kt, count), jnp.int32),
        ),
        in_specs=[SMEM, SMEM, VMEM, VMEM, pl.BlockSpec(memory_space=pl.ANY)],
        out_specs=(VMEM,) * 3,
        scratch_shapes=scratch,
        compiler_params=params(16),
    )(odd[None], offsets_of(block_columns, row_part), block_columns, tile_values, pieces)
    first = with_core(to_first)
    at_first = with_core(sent_columns)
    at_second = with_chip(sent_columns)
    edges = pl.pallas_call(
        edge_bands,
        out_shape=jax.ShapeDtypeStruct(
            (2 * TILES_REACH // HALO, size, SPAN * size), jnp.bfloat16
        ),
        in_specs=[SMEM] * 3 + [VMEM] * 2,
        out_specs=VMEM,
        scratch_shapes=scratch,
        compiler_params=params(16),
    )(
        odd[None],
        offsets_of(at_first, row_part ^ 1),
        offsets_of(at_second, row_part - 1 + 2 * odd),
        first,
        second,
    )
    x_second = with_chip(columns)
    x_first = with_core(columns)

    window = [
        pltpu.VMEM((3 * rows, width), dtype)
        for dtype in (jnp.bfloat16, jnp.bfloat16, jnp.float32, jnp.float32)
    ]
    now, last, sent = pl.pallas_call(
        first_stage,
        out_shape=(
            jax.ShapeDtypeStruct((rows, width), jnp.float32),
            jax.ShapeDtypeStruct((rows + 2 * size, width), jnp.float32),
            jax.ShapeDtypeStruct((2 * rows - 2 * size, width), jnp.bfloat16),
        ),
        in_specs=[SMEM] + [VMEM] * 5,
        out_specs=(VMEM,) * 3,
        scratch_shapes=window,
        compiler_params=params(24),
    )(odd[None], bands, edges, x_first, columns, x_second)
    got_second = with_chip(sent)
    got_first = with_core(sent)
    filtered = pl.pallas_call(
        second_stage,
        out_shape=jax.ShapeDtypeStruct((rows, width), jnp.bfloat16),
        in_specs=[SMEM] + [VMEM] * 6,
        out_specs=VMEM,
        scratch_shapes=window,
        compiler_params=params(24),
    )(odd[None], bands, edges, now, last, got_first, got_second)

    partial, rowwise = gram_and_rows(filtered)
    gram = sum_over_rows(partial)
    return rowwise, gram * (1.0 / (rows * row_parts))


def solution(mesh):
    return jax.shard_map(
        per_device,
        mesh=mesh,
        in_specs=(P(("rows", "cols"), None), P("rows", None, None), P("rows", None)),
        out_specs=(P(("rows", "cols"), None), P("cols", None)),
        check_vma=False,
    )
```

time: 290 us -> 78 us (0.27)
  waiting for transfers between devices: 176 us -> 24.1 us
  matrix products: 25.2 us -> 0 us
  Pallas kernels: 0 us -> 15.6 us
  between operations: 15 us -> 0.89 us
  blocking collectives: 13.4 us -> 0 us
  starting transfers between devices: 43 us -> 32.3 us
  other arithmetic: 9.77 us -> 1.69 us
  local copies, waits for them, and re-layouts: 6.25 us -> 2.9 us
    psum x2 -> x0, waiting for transfers between devices: 153 us -> none  [the longest x1 99.4 us: per_device(): group_sum = lax.psum(partial_value.astype(jnp.bfloat16), 'cols')]
    dot_general x82 -> x0, matrix products: 25.2 us -> none  [the longest x72 16.9 us: filter_step(): jnp.einsum('bij,bjc->bic', band_list[position], window, preferred_element...]
    pallas_call x0 -> x9, Pallas kernels: none -> 15.6 us  [the longest x1 3.38 us: per_device(): pl.pallas_call(second_stage, out_shape=jax.ShapeDtypeStruct((rows, width)...]
    all_to_all x1 -> x0, blocking collectives: 13.4 us -> none  [per_device(): lax.all_to_all(filtered, 'cols', split_axis=0, concat_axis=1, tiled=True)]
    ppermute x16 -> x22, starting transfers between devices: 36.6 us -> 26.8 us  [the longest x4 13.4 us: with_chip(): lax.ppermute(value, 'rows', [p for k in odds for p in ((k, k + 1), (k + 1...]
    convert_element_type x17 -> x1, other arithmetic: 4.83 us -> 0.04 us  [sum_over_rows(): sent = total.astype(jnp.bfloat16)]
    ppermute x16 -> x22, waiting for transfers between devices: 22.5 us -> 24.1 us  [the longest x11 11.1 us: move(): lax.ppermute(value, 'cols', [(order[i], order[(i + by) % size]) for i in...]
  transfers between devices with their start and end apart: 19 -> 23, of which waited for: 10 -> 14; matrix products, arithmetic and copies ran while one was open for 6% -> 1% of each run, Pallas kernels for 0% -> 9%
where the time goes in v1:
time: 78 us; the launch traced here: 77.5 us
  starting transfers between devices  32.3 us (41%)
  waiting for transfers between devices  24.1 us (31%)
  Pallas kernels  15.6 us (20%)
  local copies, waits for them, and re-layouts  2.9 us (4%)
  other arithmetic  1.69 us (2%)
  between operations  0.89 us (1%)
    ppermute x4, starting transfers between devices, with_chip(): lax.ppermute(value, 'rows', [p for k in odds for p in ((k, k + 1), (k + 1...  13.4 us
    ppermute x11, waiting for transfers between devices, move(): lax.ppermute(value, 'cols', [(order[i], order[(i + by) % size]) for i in...  11.1 us
    ppermute x11, starting transfers between devices, move(): lax.ppermute(value, 'cols', [(order[i], order[(i + by) % size]) for i in...  8.64 us
    ppermute x4, waiting for transfers between devices, with_chip(): lax.ppermute(value, 'rows', [p for k in odds for p in ((k, k + 1), (k + 1...  7.9 us
    all_to_all x1, starting transfers between devices, per_device(): lax.all_to_all(pieces, 'cols', split_axis=0, concat_axis=0, tiled=True)  5.55 us
    ppermute x1, waiting for transfers between devices, sum_over_rows(): got = lax.ppermute(sent, 'rows', [(i, i ^ bit) for i in range(size)])  3.57 us
    pallas_call x1, Pallas kernels, per_device(): pl.pallas_call(second_stage, out_shape=jax.ShapeDtypeStruct((rows, width)...  3.38 us
    pallas_call x1, Pallas kernels, per_device(): pl.pallas_call(first_stage, out_shape=(jax.ShapeDtypeStruct((rows, width)...  3.28 us
  transfers between devices with their start and end apart: 23, of which 14 were waited for; matrix products, arithmetic and copies ran while one was open for 1% of the time, Pallas kernels for 9%

profile of v1, /device:TPU:1, one launch (start us, length us, event | category | flops | bytes accessed | tf_op | source)
XLA Modules:
  0.0 77.5 jit_solution(18198710579105848153)
XLA Ops:
  0.6 4.5 %collective-permute-start.3 = (bf16[16,64,512]{2,1,0:T(8,128)(2,1)}, bf16[16,64,512]{2,1,0:T(8,128)(2,1)S(1)}, u32[]{:S(2)}, u32[]{:S(2)}) collective-permute-start(bf16[16,64,512]{2,1,0:T(8,128)(2,1)} %tiles.1), channel_id=1, source_target_pairs={{8,16},{16,8},{9,17},{17,9},{10,18},{18,10},{11,19},{19,11},{12,20... | collective-permute-start | bytes 3145736 | tf_op jit(solution)/shard_map/ppermute | solution.py:36
  5.2 0.9 %copy-done.1 = bf16[128,1024]{1,0:T(8,128)(2,1)S(1)} copy-done((bf16[128,1024]{1,0:T(8,128)(2,1)S(1)}, bf16[128,1024]{1,0:T(8,128)(2,1)}, u32[]{:S(2)}) %copy-start.1) | copy-done | bytes 262168
  6.8 5.6 %all-to-all-start = ((bf16[8,128,128]{2,1,0:T(8,128)(2,1)}), bf16[8,128,128]{2,1,0:T(8,128)(2,1)S(1)}, u32[]{:S(2)}, u32[]{:S(2)}) async-start(bf16[8,128,128]{2,1,0:T(8,128)(2,1)} %shard_map.59._), calls=%async_computation | async-start | bytes 524288 | tf_op jit(solution)/shard_map/all_to_all | solution.py:379
  13.1 1.2 %copy-done = bf16[16,64,512]{2,1,0:T(8,128)(2,1)S(1)} copy-done((bf16[16,64,512]{2,1,0:T(8,128)(2,1)S(1)}, bf16[16,64,512]{2,1,0:T(8,128)(2,1)}, u32[]{:S(2)}) %copy-start) | copy-done | bytes 1048600
  15.0 2.4 %shard_map.60 = (bf16[4,256,768]{2,1,0:T(8,128)(2,1)S(1)}, bf16[12,64,512]{2,1,0:T(8,128)(2,1)}, s32[8,16]{1,0:T(8,128)S(1)}) custom-call(s32[1]{0:T(128)} %bitcast.odd, s32[8,16]{1,0:T(8,128)S(1)} %subtract_clamp_fusion.2.offsets, s32[8,16]{1,0:T(8,128)S(1)} %bitcast.16, bf16[16,64,512]{2,1,0:T(8,128)(2,1)S(1)} %copy-done, bf16[8,128,128]{2,1,0:T(8,128)(2,1)} %shard_map.59._), custom_call_target="tpu_custom_call" | custom-call | tf_op jit(solution)/shard_map/pallas_call | solution.py:394
  17.9 2.2 %collective-permute-start.1 = (s32[8,16]{1,0:T(8,128)S(1)}, s32[8,16]{1,0:T(8,128)S(1)}, u32[]{:S(2)}, u32[]{:S(2)}) collective-permute-start(s32[8,16]{1,0:T(8,128)S(1)} %get-tuple-element.15), channel_id=1, source_target_pairs={{8,16},{16,8},{9,17},{17,9},{10,18},{18,10},{11,19},{19,11},{12,20... | collective-permute-start | bytes 1544 | tf_op jit(solution)/shard_map/ppermute | solution.py:36
  20.2 3.4 %collective-permute-start.5 = (bf16[1024,128]{1,0:T(8,128)(2,1)S(1)}, bf16[1024,128]{1,0:T(8,128)(2,1)S(1)}, u32[]{:S(2)}, u32[]{:S(2)}) collective-permute-start(bf16[1024,128]{1,0:T(8,128)(2,1)S(1)} %bitcast.14), channel_id=1, source_target_pairs={{8,16},{16,8},{9,17},{17,9},{10,18},{18,10},{11,19},{19,11},{12,20... | collective-permute-start | bytes 786440 | tf_op jit(solution)/shard_map/ppermute | solution.py:36
  23.6 2.4 %shard_map.61.edges = bf16[6,256,768]{2,1,0:T(8,128)(2,1)S(1)} custom-call(s32[1]{0:T(128)} %bitcast.odd, s32[8,16]{1,0:T(8,128)S(1)} %subtract_clamp_fusion.1.at_first, s32[8,16]{1,0:T(8,128)S(1)} %subtract_clamp_fusion.at_second, bf16[12,64,512]{2,1,0:T(8,128)(2,1)} %collective-permute-done.2.first, bf16[16,64,512]{2,1,0:T(8,128)(2,1)S(1)} %collective-permute-done.3.second), custom_call_target="tpu_custom_call" | custom-call | tf_op jit(solution)/shard_map/pallas_call | solution.py:409
  26.0 1.9 %collective-permute-done.5.x_second = bf16[1024,128]{1,0:T(8,128)(2,1)S(1)} collective-permute-done((bf16[1024,128]{1,0:T(8,128)(2,1)S(1)}, bf16[1024,128]{1,0:T(8,128)(2,1)S(1)}, u32[]{:S(2)}, u32[]{:S(2)}) %collective-permute-start.5) | collective-permute-done | bytes 262176 | tf_op jit(solution)/shard_map/ppermute | solution.py:36
  27.9 3.3 %shard_map.62 = (f32[1024,128]{1,0:T(8,128)S(1)}, f32[1536,128]{1,0:T(8,128)S(1)}, bf16[1536,128]{1,0:T(8,128)(2,1)S(1)}) custom-call(s32[1]{0:T(128)} %bitcast.odd, bf16[4,256,768]{2,1,0:T(8,128)(2,1)S(1)} %get-tuple-element.14.own, bf16[6,256,768]{2,1,0:T(8,128)(2,1)S(1)} %shard_map.61.edges, bf16[1024,128]{1,0:T(8,128)(2,1)S(1)} %collective-permute-done.4.x_first, ...), custom_call_target="tpu_custom_call" | custom-call | tf_op jit(solution)/shard_map/pallas_call | solution.py:432
  31.3 3.4 %collective-permute-start.7 = (bf16[1536,128]{1,0:T(8,128)(2,1)S(1)}, bf16[1536,128]{1,0:T(8,128)(2,1)S(1)}, u32[]{:S(2)}, u32[]{:S(2)}) collective-permute-start(bf16[1536,128]{1,0:T(8,128)(2,1)S(1)} %get-tuple-element.19), channel_id=1, source_target_pairs={{8,16},{16,8},{9,17},{17,9},{10,18},{18,10},{11,19},{19,11},{12,20... | collective-permute-start | bytes 1179656 | tf_op jit(solution)/shard_map/ppermute | solution.py:36
  34.7 6.0 %collective-permute-done.7.got_second = bf16[1536,128]{1,0:T(8,128)(2,1)S(1)} collective-permute-done((bf16[1536,128]{1,0:T(8,128)(2,1)S(1)}, bf16[1536,128]{1,0:T(8,128)(2,1)S(1)}, u32[]{:S(2)}, u32[]{:S(2)}) %collective-permute-start.7) | collective-permute-done | bytes 393248 | tf_op jit(solution)/shard_map/ppermute | solution.py:36
  40.7 3.4 %shard_map.63.mine = bf16[1024,128]{1,0:T(8,128)(2,1)S(1)} custom-call(s32[1]{0:T(128)} %bitcast.odd, bf16[4,256,768]{2,1,0:T(8,128)(2,1)S(1)} %get-tuple-element.14.own, bf16[6,256,768]{2,1,0:T(8,128)(2,1)S(1)} %shard_map.61.edges, f32[1024,128]{1,0:T(8,128)S(1)} %get-tuple-element.17.now, f32[1536,128]{1,0:T(8,128)S(1)} %get-tuple-element.18.last, ...), custom_call_target="tpu_custom_call" | custom-call | tf_op jit(solution)/shard_map/pallas_call | solution.py:446
  44.1 1.8 %collective-permute-start.8 = (bf16[512,128]{1,0:T(8,128)(2,1)S(1)}, bf16[512,128]{1,0:T(8,128)(2,1)S(1)}, u32[]{:S(2)}, u32[]{:S(2)}) collective-permute-start(bf16[512,128]{1,0:T(8,128)(2,1)S(1)} %get-tuple-element.29), channel_id=1, source_target_pairs={{0,2},{2,4},{4,6},{6,7},{7,5},{5,3},{3,1},{1,0},{8,10},{10,12},{12... | collective-permute-start | bytes 393224 | tf_op jit(solution)/shard_map/ppermute | solution.py:276
  45.9 1.2 %collective-permute-start.9 = (bf16[512,128]{1,0:T(8,128)(2,1)S(1)}, bf16[512,128]{1,0:T(8,128)(2,1)S(1)}, u32[]{:S(2)}, u32[]{:S(2)}) collective-permute-start(bf16[512,128]{1,0:T(8,128)(2,1)S(1)} %get-tuple-element.28), channel_id=1, source_target_pairs={{0,2},{2,4},{4,6},{6,7},{7,5},{5,3},{3,1},{1,0},{8,10},{10,12},{12... | collective-permute-start | bytes 393224 | tf_op jit(solution)/shard_map/ppermute | solution.py:276
  47.4 2.2 %collective-permute-done.8.refs_0_ = bf16[512,128]{1,0:T(8,128)(2,1)S(1)} collective-permute-done((bf16[512,128]{1,0:T(8,128)(2,1)S(1)}, bf16[512,128]{1,0:T(8,128)(2,1)S(1)}, u32[]{:S(2)}, u32[]{:S(2)}) %collective-permute-start.8) | collective-permute-done | bytes 131104 | tf_op jit(solution)/shard_map/ppermute | solution.py:276
  49.5 1.2 %collective-permute-start.12 = (bf16[512,128]{1,0:T(8,128)(2,1)S(1)}, bf16[512,128]{1,0:T(8,128)(2,1)S(1)}, u32[]{:S(2)}, u32[]{:S(2)}) collective-permute-start(bf16[512,128]{1,0:T(8,128)(2,1)S(1)} %collective-permute-done.8.refs_0_), channel_id=1, source_target_pairs={{0,2},{2,4},{4,6},{6,7},{7,5},{5,3},{3,1},{1,0},{8,10},{10,12},{12... | collective-permute-start | bytes 393224 | tf_op jit(solution)/shard_map/ppermute | solution.py:276
  51.0 1.2 %collective-permute-start.13 = (bf16[512,128]{1,0:T(8,128)(2,1)S(1)}, bf16[512,128]{1,0:T(8,128)(2,1)S(1)}, u32[]{:S(2)}, u32[]{:S(2)}) collective-permute-start(bf16[512,128]{1,0:T(8,128)(2,1)S(1)} %collective-permute-done.9.refs_1_), channel_id=1, source_target_pairs={{0,2},{2,4},{4,6},{6,7},{7,5},{5,3},{3,1},{1,0},{8,10},{10,12},{12... | collective-permute-start | bytes 393224 | tf_op jit(solution)/shard_map/ppermute | solution.py:276
  52.5 1.0 %collective-permute-done.11.refs_3_ = bf16[512,128]{1,0:T(8,128)(2,1)S(1)} collective-permute-done((bf16[512,128]{1,0:T(8,128)(2,1)S(1)}, bf16[512,128]{1,0:T(8,128)(2,1)S(1)}, u32[]{:S(2)}, u32[]{:S(2)}) %collective-permute-start.11) | collective-permute-done | bytes 131104 | tf_op jit(solution)/shard_map/ppermute | solution.py:276
  54.8 1.3 %collective-permute-done.14.refs_2_.refs_6_ = bf16[512,128]{1,0:T(8,128)(2,1)S(1)} collective-permute-done((bf16[512,128]{1,0:T(8,128)(2,1)S(1)}, bf16[512,128]{1,0:T(8,128)(2,1)S(1)}, u32[]{:S(2)}, u32[]{:S(2)}) %collective-permute-start.14) | collective-permute-done | bytes 131104 | tf_op jit(solution)/shard_map/ppermute | solution.py:276
  56.0 1.6 %collective-permute-done.15.refs_3_.refs_7_ = bf16[512,128]{1,0:T(8,128)(2,1)S(1)} collective-permute-done((bf16[512,128]{1,0:T(8,128)(2,1)S(1)}, bf16[512,128]{1,0:T(8,128)(2,1)S(1)}, u32[]{:S(2)}, u32[]{:S(2)}) %collective-permute-start.15) | collective-permute-done | bytes 131104 | tf_op jit(solution)/shard_map/ppermute | solution.py:276
  57.6 1.1 %shard_map.65 = (f32[2,128,128]{2,1,0:T(8,128)S(1)}, bf16[256,128]{1,0:T(8,128)(2,1)S(1)}, bf16[256,128]{1,0:T(8,128)(2,1)S(1)}, bf16[256,128]{1,0:T(8,128)(2,1)S(1)}) custom-call(s32[8]{0:T(128)S(1)} %compare_select_fusion.2.where, bf16[3,128,1024]{2,1,0:T(8,128)(2,1)S(1)} %get-tuple-element.20.lefts, ...), custom_call_target="tpu_custom_call" | custom-call | tf_op jit(solution)/shard_map/pallas_call | solution.py:307
  58.7 1.2 %collective-permute-start.16 = (bf16[256,128]{1,0:T(8,128)(2,1)S(1)}, bf16[256,128]{1,0:T(8,128)(2,1)S(1)}, u32[]{:S(2)}, u32[]{:S(2)}) collective-permute-start(bf16[256,128]{1,0:T(8,128)(2,1)S(1)} %get-tuple-element.21), channel_id=1, source_target_pairs={{0,2},{2,4},{4,6},{6,7},{7,5},{5,3},{3,1},{1,0},{8,10},{10,12},{12... | collective-permute-start | bytes 196616 | tf_op jit(solution)/shard_map/ppermute | solution.py:276
  60.2 0.9 %collective-permute-start.18 = (bf16[256,128]{1,0:T(8,128)(2,1)S(1)}, bf16[256,128]{1,0:T(8,128)(2,1)S(1)}, u32[]{:S(2)}, u32[]{:S(2)}) collective-permute-start(bf16[256,128]{1,0:T(8,128)(2,1)S(1)} %get-tuple-element.23), channel_id=1, source_target_pairs={{0,3},{2,1},{4,0},{6,2},{7,4},{5,6},{3,7},{1,5},{8,11},{10,9},{12,... | collective-permute-start | bytes 196616 | tf_op jit(solution)/shard_map/ppermute | solution.py:276
  61.9 1.2 %collective-permute-done.17.refs_9_.refs_1_ = bf16[256,128]{1,0:T(8,128)(2,1)S(1)} collective-permute-done((bf16[256,128]{1,0:T(8,128)(2,1)S(1)}, bf16[256,128]{1,0:T(8,128)(2,1)S(1)}, u32[]{:S(2)}, u32[]{:S(2)}) %collective-permute-start.17) | collective-permute-done | bytes 65568 | tf_op jit(solution)/shard_map/ppermute | solution.py:276
  63.0 2.3 %collective-permute-done.18.refs_10_.refs_2_ = bf16[256,128]{1,0:T(8,128)(2,1)S(1)} collective-permute-done((bf16[256,128]{1,0:T(8,128)(2,1)S(1)}, bf16[256,128]{1,0:T(8,128)(2,1)S(1)}, u32[]{:S(2)}, u32[]{:S(2)}) %collective-permute-start.18) | collective-permute-done | bytes 65568 | tf_op jit(solution)/shard_map/ppermute | solution.py:276
  66.1 1.5 %collective-permute-done.19 = f32[64,1024]{1,0:T(8,128)S(1)} collective-permute-done((f32[64,1024]{1,0:T(8,128)S(1)}, f32[64,1024]{1,0:T(8,128)S(1)}, u32[]{:S(2)}, u32[]{:S(2)}) %collective-permute-start.19) | collective-permute-done | bytes 262176 | tf_op jit(solution)/shard_map/ppermute | solution.py:348
  67.6 3.0 %collective-permute-start.20 = (bf16[64,1024]{1,0:T(8,128)(2,1)S(1)}, bf16[64,1024]{1,0:T(8,128)(2,1)S(1)}, u32[]{:S(2)}, u32[]{:S(2)}) collective-permute-start(bf16[64,1024]{1,0:T(8,128)(2,1)S(1)} %fusion), channel_id=1, source_target_pairs={{0,16},{8,24},{16,0},{24,8},{1,17},{9,25},{17,1},{25,9},{2,18},{10... | collective-permute-start | bytes 393224 | tf_op jit(solution)/shard_map/ppermute | solution.py:352
  70.7 3.6 %collective-permute-done.20 = bf16[64,1024]{1,0:T(8,128)(2,1)S(1)} collective-permute-done((bf16[64,1024]{1,0:T(8,128)(2,1)S(1)}, bf16[64,1024]{1,0:T(8,128)(2,1)S(1)}, u32[]{:S(2)}, u32[]{:S(2)}) %collective-permute-start.20) | collective-permute-done | bytes 131104 | tf_op jit(solution)/shard_map/ppermute | solution.py:352
  74.3 0.9 %collective-permute-start.21 = (f32[64,1024]{1,0:T(8,128)S(1)}, f32[64,1024]{1,0:T(8,128)S(1)}, u32[]{:S(2)}, u32[]{:S(2)}) collective-permute-start(f32[64,1024]{1,0:T(8,128)S(1)} %convert_add_fusion), channel_id=1, source_target_pairs={{0,8},{8,0},{16,24},{24,16},{1,9},{9,1},{17,25},{25,17},{2,10},{10... | collective-permute-start | bytes 786440 | tf_op jit(solution)/shard_map/ppermute | solution.py:355
  75.2 1.4 %shard_map.66 = bf16[128,1024]{1,0:T(8,128)(2,1)} custom-call(s32[8]{0:T(128)S(1)} %compare_select_fusion.2.where, bf16[1024,128]{1,0:T(8,128)(2,1)S(1)} %shard_map.63.mine, bf16[512,128]{1,0:T(8,128)(2,1)S(1)} %collective-permute-done.8.refs_0_, bf16[512,128]{1,0:T(8,128)(2,1)S(1)} %collective-permute-done.9.refs_1_, ...), custom_call_target="tpu_custom_call" | custom-call | tf_op jit(solution)/shard_map/pallas_call | solution.py:326
  76.6 0.8 %maximum_multiply_fusion = f32[128,1024]{1,0:T(8,128)} fusion(f32[64,1024]{1,0:T(8,128)S(1)} %get-tuple-element.27, f32[64,1024]{1,0:T(8,128)S(1)} %get-tuple-element.26), kind=kLoop, calls=%fused_computation | loop fusion | flops 262144 | bytes 1048576 | tf_op jit(solution)/shard_map/mul | solution.py:457
  (44 shorter events, 6.9 us)
Async XLA Ops:
  0.6 23.0 %collective-permute-start.3 = (bf16[16,64,512]{2,1,0:T(8,128)(2,1)}, bf16[16,64,512]{2,1,0:T(8,128)(2,1)S(1)}, u32[]{:S(2)}, u32[]{:S(2)}) collective-permute-start(bf16[16,64,512]{2,1,0:T(8,128)(2,1)} %tiles.1), channel_id=1, source_target_pairs={{8,16},{16,8},{9,17},{17,9},{10,18},{18,10},{11,19},{19,11},{12,20... | collective-permute-start | bytes 3145736 | tf_op jit(solution)/shard_map/ppermute | solution.py:36
  5.1 1.0 %copy-start.1 = (bf16[128,1024]{1,0:T(8,128)(2,1)S(1)}, bf16[128,1024]{1,0:T(8,128)(2,1)}, u32[]{:S(2)}) copy-start(bf16[128,1024]{1,0:T(8,128)(2,1)} %vectors.1) | copy-start | bytes 786436
  6.8 13.3 %all-to-all-start = ((bf16[8,128,128]{2,1,0:T(8,128)(2,1)}), bf16[8,128,128]{2,1,0:T(8,128)(2,1)S(1)}, u32[]{:S(2)}, u32[]{:S(2)}) async-start(bf16[8,128,128]{2,1,0:T(8,128)(2,1)} %shard_map.59._), calls=%async_computation | async-start | bytes 524288 | tf_op jit(solution)/shard_map/all_to_all | solution.py:379
  13.1 1.2 %copy-start = (bf16[16,64,512]{2,1,0:T(8,128)(2,1)S(1)}, bf16[16,64,512]{2,1,0:T(8,128)(2,1)}, u32[]{:S(2)}) copy-start(bf16[16,64,512]{2,1,0:T(8,128)(2,1)} %tiles.1) | copy-start | bytes 3145732
  14.3 0.7 copy-start.2
  17.4 6.3 %collective-permute-start.2 = (bf16[12,64,512]{2,1,0:T(8,128)(2,1)}, bf16[12,64,512]{2,1,0:T(8,128)(2,1)}, u32[]{:S(2)}, u32[]{:S(2)}) collective-permute-start(bf16[12,64,512]{2,1,0:T(8,128)(2,1)} %get-tuple-element.16), channel_id=1, source_target_pairs={{0,8},{8,0},{16,24},{24,16},{1,9},{9,1},{17,25},{25,17},{2,10},{10... | collective-permute-start | bytes 2359304 | tf_op jit(solution)/shard_map/ppermute | solution.py:31
  17.4 2.8 %collective-permute-start = (s32[8,16]{1,0:T(8,128)S(1)}, s32[8,16]{1,0:T(8,128)S(1)}, u32[]{:S(2)}, u32[]{:S(2)}) collective-permute-start(s32[8,16]{1,0:T(8,128)S(1)} %get-tuple-element.15), channel_id=1, source_target_pairs={{0,8},{8,0},{16,24},{24,16},{1,9},{9,1},{17,25},{25,17},{2,10},{10... | collective-permute-start | bytes 1544 | tf_op jit(solution)/shard_map/ppermute | solution.py:31
  17.9 5.7 %collective-permute-start.1 = (s32[8,16]{1,0:T(8,128)S(1)}, s32[8,16]{1,0:T(8,128)S(1)}, u32[]{:S(2)}, u32[]{:S(2)}) collective-permute-start(s32[8,16]{1,0:T(8,128)S(1)} %get-tuple-element.15), channel_id=1, source_target_pairs={{8,16},{16,8},{9,17},{17,9},{10,18},{18,10},{11,19},{19,11},{12,20... | collective-permute-start | bytes 1544 | tf_op jit(solution)/shard_map/ppermute | solution.py:36
  20.1 5.9 %collective-permute-start.4 = (bf16[1024,128]{1,0:T(8,128)(2,1)S(1)}, bf16[1024,128]{1,0:T(8,128)(2,1)S(1)}, u32[]{:S(2)}, u32[]{:S(2)}) collective-permute-start(bf16[1024,128]{1,0:T(8,128)(2,1)S(1)} %bitcast.13), channel_id=1, source_target_pairs={{0,8},{8,0},{16,24},{24,16},{1,9},{9,1},{17,25},{25,17},{2,10},{10... | collective-permute-start | bytes 786440 | tf_op jit(solution)/shard_map/ppermute | solution.py:31
  20.2 7.7 %collective-permute-start.5 = (bf16[1024,128]{1,0:T(8,128)(2,1)S(1)}, bf16[1024,128]{1,0:T(8,128)(2,1)S(1)}, u32[]{:S(2)}, u32[]{:S(2)}) collective-permute-start(bf16[1024,128]{1,0:T(8,128)(2,1)S(1)} %bitcast.14), channel_id=1, source_target_pairs={{8,16},{16,8},{9,17},{17,9},{10,18},{18,10},{11,19},{19,11},{12,20... | collective-permute-start | bytes 786440 | tf_op jit(solution)/shard_map/ppermute | solution.py:36
  31.2 3.5 %collective-permute-start.6 = (bf16[1536,128]{1,0:T(8,128)(2,1)S(1)}, bf16[1536,128]{1,0:T(8,128)(2,1)S(1)}, u32[]{:S(2)}, u32[]{:S(2)}) collective-permute-start(bf16[1536,128]{1,0:T(8,128)(2,1)S(1)} %get-tuple-element.19), channel_id=1, source_target_pairs={{0,8},{8,0},{16,24},{24,16},{1,9},{9,1},{17,25},{25,17},{2,10},{10... | collective-permute-start | bytes 1179656 | tf_op jit(solution)/shard_map/ppermute | solution.py:31
  31.3 9.4 %collective-permute-start.7 = (bf16[1536,128]{1,0:T(8,128)(2,1)S(1)}, bf16[1536,128]{1,0:T(8,128)(2,1)S(1)}, u32[]{:S(2)}, u32[]{:S(2)}) collective-permute-start(bf16[1536,128]{1,0:T(8,128)(2,1)S(1)} %get-tuple-element.19), channel_id=1, source_target_pairs={{8,16},{16,8},{9,17},{17,9},{10,18},{18,10},{11,19},{19,11},{12,20... | collective-permute-start | bytes 1179656 | tf_op jit(solution)/shard_map/ppermute | solution.py:36
  40.7 13.2 %copy-start.3 = (s32[8]{0:T(128)S(1)}, s32[8]{0:T(128)}, u32[]{:S(2)}) copy-start(s32[8]{0:T(128)} %constant.74.clone) | copy-start | bytes 100
  44.1 5.5 %collective-permute-start.8 = (bf16[512,128]{1,0:T(8,128)(2,1)S(1)}, bf16[512,128]{1,0:T(8,128)(2,1)S(1)}, u32[]{:S(2)}, u32[]{:S(2)}) collective-permute-start(bf16[512,128]{1,0:T(8,128)(2,1)S(1)} %get-tuple-element.29), channel_id=1, source_target_pairs={{0,2},{2,4},{4,6},{6,7},{7,5},{5,3},{3,1},{1,0},{8,10},{10,12},{12... | collective-permute-start | bytes 393224 | tf_op jit(solution)/shard_map/ppermute | solution.py:276
  45.9 5.1 %collective-permute-start.9 = (bf16[512,128]{1,0:T(8,128)(2,1)S(1)}, bf16[512,128]{1,0:T(8,128)(2,1)S(1)}, u32[]{:S(2)}, u32[]{:S(2)}) collective-permute-start(bf16[512,128]{1,0:T(8,128)(2,1)S(1)} %get-tuple-element.28), channel_id=1, source_target_pairs={{0,2},{2,4},{4,6},{6,7},{7,5},{5,3},{3,1},{1,0},{8,10},{10,12},{12... | collective-permute-start | bytes 393224 | tf_op jit(solution)/shard_map/ppermute | solution.py:276
  47.0 5.2 %collective-permute-start.10 = (bf16[512,128]{1,0:T(8,128)(2,1)S(1)}, bf16[512,128]{1,0:T(8,128)(2,1)S(1)}, u32[]{:S(2)}, u32[]{:S(2)}) collective-permute-start(bf16[512,128]{1,0:T(8,128)(2,1)S(1)} %get-tuple-element.29), channel_id=1, source_target_pairs={{0,1},{2,0},{4,2},{6,4},{7,6},{5,7},{3,5},{1,3},{8,9},{10,8},{12,1... | collective-permute-start | bytes 393224 | tf_op jit(solution)/shard_map/ppermute | solution.py:276
  47.3 6.2 %collective-permute-start.11 = (bf16[512,128]{1,0:T(8,128)(2,1)S(1)}, bf16[512,128]{1,0:T(8,128)(2,1)S(1)}, u32[]{:S(2)}, u32[]{:S(2)}) collective-permute-start(bf16[512,128]{1,0:T(8,128)(2,1)S(1)} %get-tuple-element.28), channel_id=1, source_target_pairs={{0,1},{2,0},{4,2},{6,4},{7,6},{5,7},{3,5},{1,3},{8,9},{10,8},{12,1... | collective-permute-start | bytes 393224 | tf_op jit(solution)/shard_map/ppermute | solution.py:276
  49.5 4.7 %collective-permute-start.12 = (bf16[512,128]{1,0:T(8,128)(2,1)S(1)}, bf16[512,128]{1,0:T(8,128)(2,1)S(1)}, u32[]{:S(2)}, u32[]{:S(2)}) collective-permute-start(bf16[512,128]{1,0:T(8,128)(2,1)S(1)} %collective-permute-done.8.refs_0_), channel_id=1, source_target_pairs={{0,2},{2,4},{4,6},{6,7},{7,5},{5,3},{3,1},{1,0},{8,10},{10,12},{12... | collective-permute-start | bytes 393224 | tf_op jit(solution)/shard_map/ppermute | solution.py:276
  51.0 3.8 %collective-permute-start.13 = (bf16[512,128]{1,0:T(8,128)(2,1)S(1)}, bf16[512,128]{1,0:T(8,128)(2,1)S(1)}, u32[]{:S(2)}, u32[]{:S(2)}) collective-permute-start(bf16[512,128]{1,0:T(8,128)(2,1)S(1)} %collective-permute-done.9.refs_1_), channel_id=1, source_target_pairs={{0,2},{2,4},{4,6},{6,7},{7,5},{5,3},{3,1},{1,0},{8,10},{10,12},{12... | collective-permute-start | bytes 393224 | tf_op jit(solution)/shard_map/ppermute | solution.py:276
  52.2 3.8 %collective-permute-start.14 = (bf16[512,128]{1,0:T(8,128)(2,1)S(1)}, bf16[512,128]{1,0:T(8,128)(2,1)S(1)}, u32[]{:S(2)}, u32[]{:S(2)}) collective-permute-start(bf16[512,128]{1,0:T(8,128)(2,1)S(1)} %collective-permute-done.10.refs_2_), channel_id=1, source_target_pairs={{0,1},{2,0},{4,2},{6,4},{7,6},{5,7},{3,5},{1,3},{8,9},{10,8},{12,1... | collective-permute-start | bytes 393224 | tf_op jit(solution)/shard_map/ppermute | solution.py:276
  53.5 4.1 %collective-permute-start.15 = (bf16[512,128]{1,0:T(8,128)(2,1)S(1)}, bf16[512,128]{1,0:T(8,128)(2,1)S(1)}, u32[]{:S(2)}, u32[]{:S(2)}) collective-permute-start(bf16[512,128]{1,0:T(8,128)(2,1)S(1)} %collective-permute-done.11.refs_3_), channel_id=1, source_target_pairs={{0,1},{2,0},{4,2},{6,4},{7,6},{5,7},{3,5},{1,3},{8,9},{10,8},{12,1... | collective-permute-start | bytes 393224 | tf_op jit(solution)/shard_map/ppermute | solution.py:276
  58.7 3.2 %collective-permute-start.16 = (bf16[256,128]{1,0:T(8,128)(2,1)S(1)}, bf16[256,128]{1,0:T(8,128)(2,1)S(1)}, u32[]{:S(2)}, u32[]{:S(2)}) collective-permute-start(bf16[256,128]{1,0:T(8,128)(2,1)S(1)} %get-tuple-element.21), channel_id=1, source_target_pairs={{0,2},{2,4},{4,6},{6,7},{7,5},{5,3},{3,1},{1,0},{8,10},{10,12},{12... | collective-permute-start | bytes 196616 | tf_op jit(solution)/shard_map/ppermute | solution.py:276
  59.9 3.1 %collective-permute-start.17 = (bf16[256,128]{1,0:T(8,128)(2,1)S(1)}, bf16[256,128]{1,0:T(8,128)(2,1)S(1)}, u32[]{:S(2)}, u32[]{:S(2)}) collective-permute-start(bf16[256,128]{1,0:T(8,128)(2,1)S(1)} %get-tuple-element.22), channel_id=1, source_target_pairs={{0,1},{2,0},{4,2},{6,4},{7,6},{5,7},{3,5},{1,3},{8,9},{10,8},{12,1... | collective-permute-start | bytes 196616 | tf_op jit(solution)/shard_map/ppermute | solution.py:276
  60.2 5.1 %collective-permute-start.18 = (bf16[256,128]{1,0:T(8,128)(2,1)S(1)}, bf16[256,128]{1,0:T(8,128)(2,1)S(1)}, u32[]{:S(2)}, u32[]{:S(2)}) collective-permute-start(bf16[256,128]{1,0:T(8,128)(2,1)S(1)} %get-tuple-element.23), channel_id=1, source_target_pairs={{0,3},{2,1},{4,0},{6,2},{7,4},{5,6},{3,7},{1,5},{8,11},{10,9},{12,... | collective-permute-start | bytes 196616 | tf_op jit(solution)/shard_map/ppermute | solution.py:276
  66.0 1.6 %collective-permute-start.19 = (f32[64,1024]{1,0:T(8,128)S(1)}, f32[64,1024]{1,0:T(8,128)S(1)}, u32[]{:S(2)}, u32[]{:S(2)}) collective-permute-start(f32[64,1024]{1,0:T(8,128)S(1)} %dynamic-slice_bitcast_fusion), channel_id=1, source_target_pairs={{0,8},{8,0},{16,24},{24,16},{1,9},{9,1},{17,25},{25,17},{2,10},{10... | collective-permute-start | bytes 786440 | tf_op jit(solution)/shard_map/ppermute | solution.py:348
  67.6 6.6 %collective-permute-start.20 = (bf16[64,1024]{1,0:T(8,128)(2,1)S(1)}, bf16[64,1024]{1,0:T(8,128)(2,1)S(1)}, u32[]{:S(2)}, u32[]{:S(2)}) collective-permute-start(bf16[64,1024]{1,0:T(8,128)(2,1)S(1)} %fusion), channel_id=1, source_target_pairs={{0,16},{8,24},{16,0},{24,8},{1,17},{9,25},{17,1},{25,9},{2,18},{10... | collective-permute-start | bytes 393224 | tf_op jit(solution)/shard_map/ppermute | solution.py:352
  74.3 2.3 %collective-permute-start.21 = (f32[64,1024]{1,0:T(8,128)S(1)}, f32[64,1024]{1,0:T(8,128)S(1)}, u32[]{:S(2)}, u32[]{:S(2)}) collective-permute-start(f32[64,1024]{1,0:T(8,128)S(1)} %convert_add_fusion), channel_id=1, source_target_pairs={{0,8},{8,0},{16,24},{24,16},{1,9},{9,1},{17,25},{25,17},{2,10},{10... | collective-permute-start | bytes 786440 | tf_op jit(solution)/shard_map/ppermute | solution.py:355

commit v2 on v1

--- a/solution.py
+++ b/solution.py
@@ -209,15 +209,16 @@
         put(high[pl.ds(start - half, share)])
 
 
-def late_gram(where, lefts, *refs):
+def late_gram(where, lefts, early, *refs):
     back, front = refs[:2], refs[2:4]
     partial, *messages = refs[4:]
     width = partial.shape[1]
     share = messages[0].shape[0] - width
     reach = lefts.shape[0] // 2 + 1
     far_back, far_front = whole(back), whole(front)
-    partial[0] = dot(lefts[0], far_back)
-    partial[1] = dot(lefts[0], far_front)
+    partial[:2 * reach - 1] = early[...]
+    partial[2 * reach - 1] = dot(lefts[0], far_back)
+    partial[2 * reach] = dot(lefts[0], far_front)
     made = []
     for t in range(1, reach):
         made.append((dot(lefts[2 * t], far_back), back, where[2 * t]))
@@ -232,14 +233,19 @@
         rows_of(chunk, device, share, put)
 
 
-def assemble(where, early, late, *refs):
-    *messages, partial = refs
-    width = early.shape[1]
-    held = early.shape[0]
-    blocks = [early[t] for t in range(held)] + [late[0], late[1]]
-    blocks += [message[:width].astype(jnp.float32) for message in messages]
-    for t, block in enumerate(blocks):
-        partial[columns_at(partial, where[t], width)] = block
+def place_blocks(scale, where, odd, *refs):
+    own, own_other, far, far_other, gram = refs
+    half, width = own.shape[1:]
+    first = own.shape[0]
+    for side, (near, distant) in enumerate(((own, far), (own_other, far_other))):
+        rows = pl.ds(pl.multiple_of((odd[0] ^ side) * half, half), half)
+        for t in range(first + far.shape[0]):
+            block = near[t] if t < first else distant[t - first]
+            if len(gram.shape) == 2:
+                start = pl.multiple_of(where[t] * width, width)
+                gram[rows, pl.ds(start, width)] = block * scale
+            else:
+                gram[where[t], rows] = block * scale
 
 
 def filtered_rows(number, where, mine, *refs):
@@ -304,25 +310,28 @@
         compiler_params=params(16),
     )(mine, *chunks[:-4])
     message = jax.ShapeDtypeStruct((width + share, width), mine.dtype)
-    late, *messages = pl.pallas_call(
+    own, *messages = pl.pallas_call(
         late_gram,
-        out_shape=(jax.ShapeDtypeStruct((2, width, width), jnp.float32),)
+        out_shape=(jax.ShapeDtypeStruct((held + 2, width, width), jnp.float32),)
         + (message,) * len(sends),
-        in_specs=[SMEM] + [VMEM] * 5,
+        in_specs=[SMEM] + [VMEM] * 6,
         out_specs=(VMEM,) * (1 + len(sends)),
         compiler_params=params(16),
-    )(where, lefts, *chunks[-4:])
+    )(where, lefts, early, *chunks[-4:])
     messages = [move(value, by) for value, by in zip(messages, sends)]
+    own, messages = lax.optimization_barrier((sum_of_cores(own), messages))
+    far = jnp.stack([message[:width] for message in messages]).astype(jnp.float32)
 
     flat = width % 128 == 0
     shape = (lambda n: (n, size * width)) if flat else (lambda n: (size, n, width))
-    partial = pl.pallas_call(
-        assemble,
+    gram = pl.pallas_call(
+        functools.partial(place_blocks, 1.0 / (rows * lax.axis_size("rows"))),
         out_shape=jax.ShapeDtypeStruct(shape(width), jnp.float32),
-        in_specs=[SMEM] + [VMEM] * (2 + len(messages)),
+        in_specs=[SMEM] * 2 + [VMEM] * 4,
         out_specs=VMEM,
         compiler_params=params(16),
-    )(where, early, late, *messages)
+    )(where, (lax.axis_index("rows") & 1)[None], *sum_of_chips(own),
+      *sum_of_chips(sum_of_cores(far)))
     rowwise = pl.pallas_call(
         functools.partial(filtered_rows, len(chunks)),
         out_shape=jax.ShapeDtypeStruct(shape(share), mine.dtype),
@@ -331,36 +340,32 @@
         compiler_params=params(16),
     )(where, mine, *chunks, *messages)
     if not flat:
-        partial = partial.transpose(1, 0, 2).reshape(width, size * width)
+        gram = gram.transpose(1, 0, 2).reshape(width, size * width)
         rowwise = rowwise.transpose(1, 0, 2).reshape(share, size * width)
-    return partial, rowwise
-
-
-def sum_over_rows(partial):
+    return rowwise, gram
+
+
+def sum_of_cores(blocks):
+    odd = lax.axis_index("rows") & 1
+    half = blocks.shape[1] // 2
+    keep = lax.dynamic_slice_in_dim(blocks, odd * half, half, 1)
+    give = lax.dynamic_slice_in_dim(blocks, (1 - odd) * half, half, 1)
+    return (keep + with_core(give)).astype(jnp.bfloat16)
+
+
+def sum_of_chips(sent):
     size = lax.axis_size("rows")
-    me = lax.axis_index("rows")
-    half = partial.shape[0] // 2
-    odd = me & 1
-    partner = [(i, i ^ 1) for i in range(size)]
-    halves = partial.reshape(2, half, partial.shape[1])
-    keep = lax.dynamic_index_in_dim(halves, odd, 0, keepdims=False)
-    give = lax.dynamic_index_in_dim(halves, 1 - odd, 0, keepdims=False)
-    total = keep + lax.ppermute(give, "rows", partner)
     bit = 2
     while bit < size:
-        sent = total.astype(jnp.bfloat16)
         got = lax.ppermute(sent, "rows", [(i, i ^ bit) for i in range(size)])
         total = sent.astype(jnp.float32) + got.astype(jnp.float32)
+        sent = total.astype(jnp.bfloat16)
         bit *= 2
-    other = lax.ppermute(total, "rows", partner)
-    low = jnp.where(odd == 0, total, other)
-    high = jnp.where(odd == 0, other, total)
-    return jnp.concatenate([low, high], axis=0)
+    return total, with_core(total)
 
 
 def per_device(search_vectors, tile_values, block_columns):
     row_part = lax.axis_index("rows")
-    row_parts = lax.axis_size("rows")
     col_parts = lax.axis_size("cols")
     count, tile, depth = tile_values.shape
     kt = block_columns.shape[1]
@@ -368,7 +373,6 @@
     share = search_vectors.shape[0]
     width = search_vectors.shape[1] // col_parts
     rows = share * col_parts
-    second = with_chip(tile_values)
     pieces = pl.pallas_call(
         split_columns,
         out_shape=jax.ShapeDtypeStruct((col_parts, share, width), search_vectors.dtype),
@@ -376,6 +380,8 @@
         out_specs=VMEM,
         compiler_params=params(4),
     )(search_vectors)
+    pieces, far_tiles = lax.optimization_barrier((pieces, tile_values))
+    second = with_chip(far_tiles)
     columns = lax.all_to_all(pieces, "cols", split_axis=0, concat_axis=0, tiled=True)
     columns = columns.reshape(rows, width)
 
@@ -452,9 +458,7 @@
         compiler_params=params(24),
     )(odd[None], bands, edges, now, last, got_first, got_second)
 
-    partial, rowwise = gram_and_rows(filtered)
-    gram = sum_over_rows(partial)
-    return rowwise, gram * (1.0 / (rows * row_parts))
+    return gram_and_rows(filtered)
 
 
 def solution(mesh):

time: 78 us -> 78.5 us (level)
  starting transfers between devices: 32.3 us -> 36.5 us
  waiting for transfers between devices: 24.1 us -> 20.5 us
  other arithmetic: 1.69 us -> 0.83 us
    ppermute x4 -> x8, starting transfers between devices: 0.65 us -> 5.3 us  [with_core(): lax.ppermute(value, 'rows', [(i, i ^ 1) for i in range(lax.axis_size('row...]
    ppermute x3 -> x2, waiting for transfers between devices: 5.09 us -> 1.71 us  [sum_of_chips(): got = lax.ppermute(sent, 'rows', [(i, i ^ bit) for i in range(size)])]
    mul x1 -> x0, other arithmetic: 0.84 us -> none  [per_device(): return (rowwise, gram * (1.0 / (rows * row_parts)))]
    pallas_call x2, Pallas kernels: 1.66 us -> 2.46 us  [the longest x1 1.38 us: gram_and_rows(): pl.pallas_call(functools.partial(place_blocks, 1.0 / (rows * lax.axis_siz...]
    ppermute x3 -> x2, starting transfers between devices: 4.06 us -> 3.45 us  [sum_of_chips(): got = lax.ppermute(sent, 'rows', [(i, i ^ bit) for i in range(size)])]
  transfers between devices with their start and end apart: 23 -> 26, of which waited for: 14 -> 13; matrix products, arithmetic and copies ran while one was open for 1% -> 1% of each run, Pallas kernels for 9% -> 8%
where the time goes in v2:
time: 78.5 us; the launch traced here: 78 us
  starting transfers between devices  36.5 us (46%)
  waiting for transfers between devices  20.5 us (26%)
  Pallas kernels  16.3 us (21%)
  local copies, waits for them, and re-layouts  2.92 us (4%)
  between operations  0.9 us (1%)
  other arithmetic  0.83 us (1%)
    ppermute x4, starting transfers between devices, with_chip(): lax.ppermute(value, 'rows', [p for k in odds for p in ((k, k + 1), (k + 1...  13.4 us
    ppermute x11, waiting for transfers between devices, move(): lax.ppermute(value, 'cols', [(order[i], order[(i + by) % size]) for i in...  10.9 us
    ppermute x11, starting transfers between devices, move(): lax.ppermute(value, 'cols', [(order[i], order[(i + by) % size]) for i in...  8.81 us
    ppermute x4, waiting for transfers between devices, with_chip(): lax.ppermute(value, 'rows', [p for k in odds for p in ((k, k + 1), (k + 1...  7.91 us
    all_to_all x1, starting transfers between devices, per_device(): lax.all_to_all(pieces, 'cols', split_axis=0, concat_axis=0, tiled=True)  5.57 us
    ppermute x8, starting transfers between devices, with_core(): lax.ppermute(value, 'rows', [(i, i ^ 1) for i in range(lax.axis_size('row...  5.3 us
    ppermute x2, starting transfers between devices, sum_of_chips(): got = lax.ppermute(sent, 'rows', [(i, i ^ bit) for i in range(size)])  3.45 us
    pallas_call x1, Pallas kernels, per_device(): pl.pallas_call(second_stage, out_shape=jax.ShapeDtypeStruct((rows, width)...  3.38 us
  transfers between devices with their start and end apart: 26, of which 13 were waited for; matrix products, arithmetic and copies ran while one was open for 1% of the time, Pallas kernels for 8%

profile of v2, /device:TPU:1, one launch (start us, length us, event | category | flops | bytes accessed | tf_op | source)
XLA Modules:
  0.0 78.0 jit_solution(4786534665547617164)
XLA Ops:
  2.3 4.5 %collective-permute-start.3 = (bf16[16,64,512]{2,1,0:T(8,128)(2,1)}, bf16[16,64,512]{2,1,0:T(8,128)(2,1)S(1)}, u32[]{:S(2)}, u32[]{:S(2)}) collective-permute-start(bf16[16,64,512]{2,1,0:T(8,128)(2,1)} %tiles.1), channel_id=1, source_target_pairs={{8,16},{16,8},{9,17},{17,9},{10,18},{18,10},{11,19},{19,11},{12,20... | collective-permute-start | bytes 3145736 | tf_op jit(solution)/shard_map/ppermute | solution.py:36
  6.8 5.6 %all-to-all-start = ((bf16[8,128,128]{2,1,0:T(8,128)(2,1)}), bf16[8,128,128]{2,1,0:T(8,128)(2,1)S(1)}, u32[]{:S(2)}, u32[]{:S(2)}) async-start(bf16[8,128,128]{2,1,0:T(8,128)(2,1)} %shard_map.59._), calls=%async_computation | async-start | bytes 524288 | tf_op jit(solution)/shard_map/all_to_all | solution.py:385
  13.1 1.2 %copy-done = bf16[16,64,512]{2,1,0:T(8,128)(2,1)S(1)} copy-done((bf16[16,64,512]{2,1,0:T(8,128)(2,1)S(1)}, bf16[16,64,512]{2,1,0:T(8,128)(2,1)}, u32[]{:S(2)}) %copy-start) | copy-done | bytes 1048600
  15.0 2.3 %shard_map.60 = (bf16[4,256,768]{2,1,0:T(8,128)(2,1)S(1)}, bf16[12,64,512]{2,1,0:T(8,128)(2,1)}, s32[8,16]{1,0:T(8,128)S(1)}) custom-call(s32[1]{0:T(128)} %bitcast.odd, s32[8,16]{1,0:T(8,128)S(1)} %subtract_clamp_fusion.2.offsets, s32[8,16]{1,0:T(8,128)S(1)} %bitcast.13, bf16[16,64,512]{2,1,0:T(8,128)(2,1)S(1)} %copy-done, bf16[8,128,128]{2,1,0:T(8,128)(2,1)} %shard_map.59._), custom_call_target="tpu_custom_call" | custom-call | tf_op jit(solution)/shard_map/pallas_call | solution.py:400
  17.9 2.2 %collective-permute-start.1 = (s32[8,16]{1,0:T(8,128)S(1)}, s32[8,16]{1,0:T(8,128)S(1)}, u32[]{:S(2)}, u32[]{:S(2)}) collective-permute-start(s32[8,16]{1,0:T(8,128)S(1)} %get-tuple-element.22), channel_id=1, source_target_pairs={{8,16},{16,8},{9,17},{17,9},{10,18},{18,10},{11,19},{19,11},{12,20... | collective-permute-start | bytes 1544 | tf_op jit(solution)/shard_map/ppermute | solution.py:36
  20.2 3.4 %collective-permute-start.5 = (bf16[1024,128]{1,0:T(8,128)(2,1)S(1)}, bf16[1024,128]{1,0:T(8,128)(2,1)S(1)}, u32[]{:S(2)}, u32[]{:S(2)}) collective-permute-start(bf16[1024,128]{1,0:T(8,128)(2,1)S(1)} %bitcast.11), channel_id=1, source_target_pairs={{8,16},{16,8},{9,17},{17,9},{10,18},{18,10},{11,19},{19,11},{12,20... | collective-permute-start | bytes 786440 | tf_op jit(solution)/shard_map/ppermute | solution.py:36
  23.6 2.4 %shard_map.61.edges = bf16[6,256,768]{2,1,0:T(8,128)(2,1)S(1)} custom-call(s32[1]{0:T(128)} %bitcast.odd, s32[8,16]{1,0:T(8,128)S(1)} %subtract_clamp_fusion.1.at_first, s32[8,16]{1,0:T(8,128)S(1)} %subtract_clamp_fusion.at_second, bf16[12,64,512]{2,1,0:T(8,128)(2,1)} %collective-permute-done.2.first, bf16[16,64,512]{2,1,0:T(8,128)(2,1)S(1)} %collective-permute-done.3.second), custom_call_target="tpu_custom_call" | custom-call | tf_op jit(solution)/shard_map/pallas_call | solution.py:415
  26.0 1.9 %collective-permute-done.5.x_second = bf16[1024,128]{1,0:T(8,128)(2,1)S(1)} collective-permute-done((bf16[1024,128]{1,0:T(8,128)(2,1)S(1)}, bf16[1024,128]{1,0:T(8,128)(2,1)S(1)}, u32[]{:S(2)}, u32[]{:S(2)}) %collective-permute-start.5) | collective-permute-done | bytes 262176 | tf_op jit(solution)/shard_map/ppermute | solution.py:36
  27.9 3.3 %shard_map.62 = (f32[1024,128]{1,0:T(8,128)S(1)}, f32[1536,128]{1,0:T(8,128)S(1)}, bf16[1536,128]{1,0:T(8,128)(2,1)S(1)}) custom-call(s32[1]{0:T(128)} %bitcast.odd, bf16[4,256,768]{2,1,0:T(8,128)(2,1)S(1)} %get-tuple-element.21.own, bf16[6,256,768]{2,1,0:T(8,128)(2,1)S(1)} %shard_map.61.edges, bf16[1024,128]{1,0:T(8,128)(2,1)S(1)} %collective-permute-done.4.x_first, ...), custom_call_target="tpu_custom_call" | custom-call | tf_op jit(solution)/shard_map/pallas_call | solution.py:438
  31.3 3.4 %collective-permute-start.7 = (bf16[1536,128]{1,0:T(8,128)(2,1)S(1)}, bf16[1536,128]{1,0:T(8,128)(2,1)S(1)}, u32[]{:S(2)}, u32[]{:S(2)}) collective-permute-start(bf16[1536,128]{1,0:T(8,128)(2,1)S(1)} %get-tuple-element.27), channel_id=1, source_target_pairs={{8,16},{16,8},{9,17},{17,9},{10,18},{18,10},{11,19},{19,11},{12,20... | collective-permute-start | bytes 1179656 | tf_op jit(solution)/shard_map/ppermute | solution.py:36
  34.6 6.0 %collective-permute-done.7.got_second = bf16[1536,128]{1,0:T(8,128)(2,1)S(1)} collective-permute-done((bf16[1536,128]{1,0:T(8,128)(2,1)S(1)}, bf16[1536,128]{1,0:T(8,128)(2,1)S(1)}, u32[]{:S(2)}, u32[]{:S(2)}) %collective-permute-start.7) | collective-permute-done | bytes 393248 | tf_op jit(solution)/shard_map/ppermute | solution.py:36
  40.6 3.4 %shard_map.63.mine = bf16[1024,128]{1,0:T(8,128)(2,1)S(1)} custom-call(s32[1]{0:T(128)} %bitcast.odd, bf16[4,256,768]{2,1,0:T(8,128)(2,1)S(1)} %get-tuple-element.21.own, bf16[6,256,768]{2,1,0:T(8,128)(2,1)S(1)} %shard_map.61.edges, f32[1024,128]{1,0:T(8,128)S(1)} %get-tuple-element.25.now, f32[1536,128]{1,0:T(8,128)S(1)} %get-tuple-element.26.last, ...), custom_call_target="tpu_custom_call" | custom-call | tf_op jit(solution)/shard_map/pallas_call | solution.py:452
  44.1 1.8 %collective-permute-start.8 = (bf16[512,128]{1,0:T(8,128)(2,1)S(1)}, bf16[512,128]{1,0:T(8,128)(2,1)S(1)}, u32[]{:S(2)}, u32[]{:S(2)}) collective-permute-start(bf16[512,128]{1,0:T(8,128)(2,1)S(1)} %get-tuple-element.39), channel_id=1, source_target_pairs={{0,2},{2,4},{4,6},{6,7},{7,5},{5,3},{3,1},{1,0},{8,10},{10,12},{12... | collective-permute-start | bytes 393224 | tf_op jit(solution)/shard_map/ppermute | solution.py:282
  45.8 1.2 %collective-permute-start.9 = (bf16[512,128]{1,0:T(8,128)(2,1)S(1)}, bf16[512,128]{1,0:T(8,128)(2,1)S(1)}, u32[]{:S(2)}, u32[]{:S(2)}) collective-permute-start(bf16[512,128]{1,0:T(8,128)(2,1)S(1)} %get-tuple-element.38), channel_id=1, source_target_pairs={{0,2},{2,4},{4,6},{6,7},{7,5},{5,3},{3,1},{1,0},{8,10},{10,12},{12... | collective-permute-start | bytes 393224 | tf_op jit(solution)/shard_map/ppermute | solution.py:282
  47.4 2.2 %collective-permute-done.8.refs_0_ = bf16[512,128]{1,0:T(8,128)(2,1)S(1)} collective-permute-done((bf16[512,128]{1,0:T(8,128)(2,1)S(1)}, bf16[512,128]{1,0:T(8,128)(2,1)S(1)}, u32[]{:S(2)}, u32[]{:S(2)}) %collective-permute-start.8) | collective-permute-done | bytes 131104 | tf_op jit(solution)/shard_map/ppermute | solution.py:282
  49.5 1.2 %collective-permute-start.12 = (bf16[512,128]{1,0:T(8,128)(2,1)S(1)}, bf16[512,128]{1,0:T(8,128)(2,1)S(1)}, u32[]{:S(2)}, u32[]{:S(2)}) collective-permute-start(bf16[512,128]{1,0:T(8,128)(2,1)S(1)} %collective-permute-done.8.refs_0_), channel_id=1, source_target_pairs={{0,2},{2,4},{4,6},{6,7},{7,5},{5,3},{3,1},{1,0},{8,10},{10,12},{12... | collective-permute-start | bytes 393224 | tf_op jit(solution)/shard_map/ppermute | solution.py:282
  50.9 1.2 %collective-permute-start.13 = (bf16[512,128]{1,0:T(8,128)(2,1)S(1)}, bf16[512,128]{1,0:T(8,128)(2,1)S(1)}, u32[]{:S(2)}, u32[]{:S(2)}) collective-permute-start(bf16[512,128]{1,0:T(8,128)(2,1)S(1)} %collective-permute-done.9.refs_1_), channel_id=1, source_target_pairs={{0,2},{2,4},{4,6},{6,7},{7,5},{5,3},{3,1},{1,0},{8,10},{10,12},{12... | collective-permute-start | bytes 393224 | tf_op jit(solution)/shard_map/ppermute | solution.py:282
  52.5 1.0 %collective-permute-done.11.refs_3_ = bf16[512,128]{1,0:T(8,128)(2,1)S(1)} collective-permute-done((bf16[512,128]{1,0:T(8,128)(2,1)S(1)}, bf16[512,128]{1,0:T(8,128)(2,1)S(1)}, u32[]{:S(2)}, u32[]{:S(2)}) %collective-permute-start.11) | collective-permute-done | bytes 131104 | tf_op jit(solution)/shard_map/ppermute | solution.py:282
  54.8 1.3 %collective-permute-done.14.refs_2_.refs_6_ = bf16[512,128]{1,0:T(8,128)(2,1)S(1)} collective-permute-done((bf16[512,128]{1,0:T(8,128)(2,1)S(1)}, bf16[512,128]{1,0:T(8,128)(2,1)S(1)}, u32[]{:S(2)}, u32[]{:S(2)}) %collective-permute-start.14) | collective-permute-done | bytes 131104 | tf_op jit(solution)/shard_map/ppermute | solution.py:282
  56.0 1.4 %collective-permute-done.15.refs_3_.refs_7_ = bf16[512,128]{1,0:T(8,128)(2,1)S(1)} collective-permute-done((bf16[512,128]{1,0:T(8,128)(2,1)S(1)}, bf16[512,128]{1,0:T(8,128)(2,1)S(1)}, u32[]{:S(2)}, u32[]{:S(2)}) %collective-permute-start.15) | collective-permute-done | bytes 131104 | tf_op jit(solution)/shard_map/ppermute | solution.py:282
  57.4 1.1 %shard_map.65 = (f32[5,128,128]{2,1,0:T(8,128)S(1)}, bf16[256,128]{1,0:T(8,128)(2,1)S(1)}, bf16[256,128]{1,0:T(8,128)(2,1)S(1)}, bf16[256,128]{1,0:T(8,128)(2,1)S(1)}) custom-call(s32[8]{0:T(128)S(1)} %compare_select_fusion.2.where, bf16[3,128,1024]{2,1,0:T(8,128)(2,1)S(1)} %get-tuple-element.28.lefts, f32[3,128,128]{2,1,0:T(8,128)S(1)} %get-tuple-element.29.early, ...), custom_call_target="tpu_custom_call" | custom-call | tf_op jit(solution)/shard_map/pallas_call | solution.py:313
  58.6 1.2 %collective-permute-start.17 = (bf16[256,128]{1,0:T(8,128)(2,1)S(1)}, bf16[256,128]{1,0:T(8,128)(2,1)S(1)}, u32[]{:S(2)}, u32[]{:S(2)}) collective-permute-start(bf16[256,128]{1,0:T(8,128)(2,1)S(1)} %get-tuple-element.31), channel_id=1, source_target_pairs={{0,2},{2,4},{4,6},{6,7},{7,5},{5,3},{3,1},{1,0},{8,10},{10,12},{12... | collective-permute-start | bytes 196616 | tf_op jit(solution)/shard_map/ppermute | solution.py:282
  60.1 1.0 %collective-permute-start.19 = (bf16[256,128]{1,0:T(8,128)(2,1)S(1)}, bf16[256,128]{1,0:T(8,128)(2,1)S(1)}, u32[]{:S(2)}, u32[]{:S(2)}) collective-permute-start(bf16[256,128]{1,0:T(8,128)(2,1)S(1)} %get-tuple-element.33), channel_id=1, source_target_pairs={{0,3},{2,1},{4,0},{6,2},{7,4},{5,6},{3,7},{1,5},{8,11},{10,9},{12,... | collective-permute-start | bytes 196616 | tf_op jit(solution)/shard_map/ppermute | solution.py:282
  61.8 1.2 %collective-permute-done.18.refs_9_ = bf16[256,128]{1,0:T(8,128)(2,1)S(1)} collective-permute-done((bf16[256,128]{1,0:T(8,128)(2,1)S(1)}, bf16[256,128]{1,0:T(8,128)(2,1)S(1)}, u32[]{:S(2)}, u32[]{:S(2)}) %collective-permute-start.18) | collective-permute-done | bytes 65568 | tf_op jit(solution)/shard_map/ppermute | solution.py:282
  63.0 2.4 %collective-permute-done.19.refs_10_ = bf16[256,128]{1,0:T(8,128)(2,1)S(1)} collective-permute-done((bf16[256,128]{1,0:T(8,128)(2,1)S(1)}, bf16[256,128]{1,0:T(8,128)(2,1)S(1)}, u32[]{:S(2)}, u32[]{:S(2)}) %collective-permute-start.19) | collective-permute-done | bytes 65568 | tf_op jit(solution)/shard_map/ppermute | solution.py:282
  65.5 2.7 %collective-permute-start.22 = (f32[3,64,128]{2,1,0:T(8,128)S(1)}, f32[3,64,128]{2,1,0:T(8,128)S(1)}, u32[]{:S(2)}, u32[]{:S(2)}) collective-permute-start(f32[3,64,128]{2,1,0:T(8,128)S(1)} %constant_dynamic-slice_fusion), channel_id=1, source_target_pairs={{0,8},{8,0},{16,24},{24,16},{1,9},{9,1},{17,25},{25,17},{2,10},{10... | collective-permute-start | bytes 294920 | tf_op jit(solution)/shard_map/ppermute | solution.py:31
  68.2 2.5 %collective-permute-start.20 = (bf16[5,64,128]{2,1,0:T(8,128)(2,1)S(1)}, bf16[5,64,128]{2,1,0:T(8,128)(2,1)S(1)}, u32[]{:S(2)}, u32[]{:S(2)}) collective-permute-start(bf16[5,64,128]{2,1,0:T(8,128)(2,1)S(1)} %add_convert_fusion), channel_id=1, source_target_pairs={{0,16},{8,24},{16,0},{24,8},{1,17},{9,25},{17,1},{25,9},{2,18},{10... | collective-permute-start | bytes 245768 | tf_op jit(solution)/shard_map/ppermute | solution.py:360
  70.7 1.0 %collective-permute-start.23 = (bf16[3,64,128]{2,1,0:T(8,128)(2,1)S(1)}, bf16[3,64,128]{2,1,0:T(8,128)(2,1)S(1)}, u32[]{:S(2)}, u32[]{:S(2)}) collective-permute-start(bf16[3,64,128]{2,1,0:T(8,128)(2,1)S(1)} %add_convert_fusion.1), channel_id=1, source_target_pairs={{0,16},{8,24},{16,0},{24,8},{1,17},{9,25},{17,1},{25,9},{2,18},{10... | collective-permute-start | bytes 147464 | tf_op jit(solution)/shard_map/ppermute | solution.py:360
  71.7 1.7 %collective-permute-done.20 = bf16[5,64,128]{2,1,0:T(8,128)(2,1)S(1)} collective-permute-done((bf16[5,64,128]{2,1,0:T(8,128)(2,1)S(1)}, bf16[5,64,128]{2,1,0:T(8,128)(2,1)S(1)}, u32[]{:S(2)}, u32[]{:S(2)}) %collective-permute-start.20) | collective-permute-done | bytes 81952 | tf_op jit(solution)/shard_map/ppermute | solution.py:360
  74.3 1.0 %collective-permute-start.24 = (f32[3,64,128]{2,1,0:T(8,128)S(1)}, f32[3,64,128]{2,1,0:T(8,128)S(1)}, u32[]{:S(2)}, u32[]{:S(2)}) collective-permute-start(f32[3,64,128]{2,1,0:T(8,128)S(1)} %convert_add_fusion.1.refs_2_), channel_id=1, source_target_pairs={{0,8},{8,0},{16,24},{24,16},{1,9},{9,1},{17,25},{25,17},{2,10},{10... | collective-permute-start | bytes 294920 | tf_op jit(solution)/shard_map/ppermute | solution.py:31
  75.3 1.4 %shard_map.66 = bf16[128,1024]{1,0:T(8,128)(2,1)} custom-call(s32[8]{0:T(128)S(1)} %compare_select_fusion.2.where, bf16[1024,128]{1,0:T(8,128)(2,1)S(1)} %shard_map.63.mine, bf16[512,128]{1,0:T(8,128)(2,1)S(1)} %collective-permute-done.8.refs_0_, bf16[512,128]{1,0:T(8,128)(2,1)S(1)} %collective-permute-done.9.refs_1_, ...), custom_call_target="tpu_custom_call" | custom-call | tf_op jit(solution)/shard_map/pallas_call | solution.py:335
  76.6 1.4 %shard_map.67 = f32[128,1024]{1,0:T(8,128)} custom-call(s32[8]{0:T(128)S(1)} %compare_select_fusion.2.where, s32[1]{0:T(128)} %bitcast.odd, f32[5,64,128]{2,1,0:T(8,128)S(1)} %convert_add_fusion.refs_0_, f32[5,64,128]{2,1,0:T(8,128)S(1)} %collective-permute-done.21.refs_1_, f32[3,64,128]{2,1,0:T(8,128)S(1)} %convert_add_fusion.1.refs_2_, ...), custom_call_target="tpu_custom_call" | custom-call | tf_op jit(solution)/shard_map/pallas_call | solution.py:327
  (54 shorter events, 7.9 us)
Async XLA Ops:
  0.6 1.0 %copy-start.1 = (bf16[128,1024]{1,0:T(8,128)(2,1)S(1)}, bf16[128,1024]{1,0:T(8,128)(2,1)}, u32[]{:S(2)}) copy-start(bf16[128,1024]{1,0:T(8,128)(2,1)} %vectors.1) | copy-start | bytes 786436
  2.3 21.3 %collective-permute-start.3 = (bf16[16,64,512]{2,1,0:T(8,128)(2,1)}, bf16[16,64,512]{2,1,0:T(8,128)(2,1)S(1)}, u32[]{:S(2)}, u32[]{:S(2)}) collective-permute-start(bf16[16,64,512]{2,1,0:T(8,128)(2,1)} %tiles.1), channel_id=1, source_target_pairs={{8,16},{16,8},{9,17},{17,9},{10,18},{18,10},{11,19},{19,11},{12,20... | collective-permute-start | bytes 3145736 | tf_op jit(solution)/shard_map/ppermute | solution.py:36
  6.8 13.3 %all-to-all-start = ((bf16[8,128,128]{2,1,0:T(8,128)(2,1)}), bf16[8,128,128]{2,1,0:T(8,128)(2,1)S(1)}, u32[]{:S(2)}, u32[]{:S(2)}) async-start(bf16[8,128,128]{2,1,0:T(8,128)(2,1)} %shard_map.59._), calls=%async_computation | async-start | bytes 524288 | tf_op jit(solution)/shard_map/all_to_all | solution.py:385
  13.1 1.2 %copy-start = (bf16[16,64,512]{2,1,0:T(8,128)(2,1)S(1)}, bf16[16,64,512]{2,1,0:T(8,128)(2,1)}, u32[]{:S(2)}) copy-start(bf16[16,64,512]{2,1,0:T(8,128)(2,1)} %tiles.1) | copy-start | bytes 3145732
  14.3 0.7 copy-start.2
  17.4 6.3 %collective-permute-start.2 = (bf16[12,64,512]{2,1,0:T(8,128)(2,1)}, bf16[12,64,512]{2,1,0:T(8,128)(2,1)}, u32[]{:S(2)}, u32[]{:S(2)}) collective-permute-start(bf16[12,64,512]{2,1,0:T(8,128)(2,1)} %get-tuple-element.23), channel_id=1, source_target_pairs={{0,8},{8,0},{16,24},{24,16},{1,9},{9,1},{17,25},{25,17},{2,10},{10... | collective-permute-start | bytes 2359304 | tf_op jit(solution)/shard_map/ppermute | solution.py:31
  17.4 2.8 %collective-permute-start = (s32[8,16]{1,0:T(8,128)S(1)}, s32[8,16]{1,0:T(8,128)S(1)}, u32[]{:S(2)}, u32[]{:S(2)}) collective-permute-start(s32[8,16]{1,0:T(8,128)S(1)} %get-tuple-element.22), channel_id=1, source_target_pairs={{0,8},{8,0},{16,24},{24,16},{1,9},{9,1},{17,25},{25,17},{2,10},{10... | collective-permute-start | bytes 1544 | tf_op jit(solution)/shard_map/ppermute | solution.py:31
  17.9 5.7 %collective-permute-start.1 = (s32[8,16]{1,0:T(8,128)S(1)}, s32[8,16]{1,0:T(8,128)S(1)}, u32[]{:S(2)}, u32[]{:S(2)}) collective-permute-start(s32[8,16]{1,0:T(8,128)S(1)} %get-tuple-element.22), channel_id=1, source_target_pairs={{8,16},{16,8},{9,17},{17,9},{10,18},{18,10},{11,19},{19,11},{12,20... | collective-permute-start | bytes 1544 | tf_op jit(solution)/shard_map/ppermute | solution.py:36
  20.1 5.9 %collective-permute-start.4 = (bf16[1024,128]{1,0:T(8,128)(2,1)S(1)}, bf16[1024,128]{1,0:T(8,128)(2,1)S(1)}, u32[]{:S(2)}, u32[]{:S(2)}) collective-permute-start(bf16[1024,128]{1,0:T(8,128)(2,1)S(1)} %bitcast.10), channel_id=1, source_target_pairs={{0,8},{8,0},{16,24},{24,16},{1,9},{9,1},{17,25},{25,17},{2,10},{10... | collective-permute-start | bytes 786440 | tf_op jit(solution)/shard_map/ppermute | solution.py:31
  20.2 7.7 %collective-permute-start.5 = (bf16[1024,128]{1,0:T(8,128)(2,1)S(1)}, bf16[1024,128]{1,0:T(8,128)(2,1)S(1)}, u32[]{:S(2)}, u32[]{:S(2)}) collective-permute-start(bf16[1024,128]{1,0:T(8,128)(2,1)S(1)} %bitcast.11), channel_id=1, source_target_pairs={{8,16},{16,8},{9,17},{17,9},{10,18},{18,10},{11,19},{19,11},{12,20... | collective-permute-start | bytes 786440 | tf_op jit(solution)/shard_map/ppermute | solution.py:36
  31.2 3.5 %collective-permute-start.6 = (bf16[1536,128]{1,0:T(8,128)(2,1)S(1)}, bf16[1536,128]{1,0:T(8,128)(2,1)S(1)}, u32[]{:S(2)}, u32[]{:S(2)}) collective-permute-start(bf16[1536,128]{1,0:T(8,128)(2,1)S(1)} %get-tuple-element.27), channel_id=1, source_target_pairs={{0,8},{8,0},{16,24},{24,16},{1,9},{9,1},{17,25},{25,17},{2,10},{10... | collective-permute-start | bytes 1179656 | tf_op jit(solution)/shard_map/ppermute | solution.py:31
  31.3 9.4 %collective-permute-start.7 = (bf16[1536,128]{1,0:T(8,128)(2,1)S(1)}, bf16[1536,128]{1,0:T(8,128)(2,1)S(1)}, u32[]{:S(2)}, u32[]{:S(2)}) collective-permute-start(bf16[1536,128]{1,0:T(8,128)(2,1)S(1)} %get-tuple-element.27), channel_id=1, source_target_pairs={{8,16},{16,8},{9,17},{17,9},{10,18},{18,10},{11,19},{19,11},{12,20... | collective-permute-start | bytes 1179656 | tf_op jit(solution)/shard_map/ppermute | solution.py:36
  40.6 13.2 %copy-start.3 = (s32[8]{0:T(128)S(1)}, s32[8]{0:T(128)}, u32[]{:S(2)}) copy-start(s32[8]{0:T(128)} %constant.68.clone) | copy-start | bytes 100
  44.1 5.5 %collective-permute-start.8 = (bf16[512,128]{1,0:T(8,128)(2,1)S(1)}, bf16[512,128]{1,0:T(8,128)(2,1)S(1)}, u32[]{:S(2)}, u32[]{:S(2)}) collective-permute-start(bf16[512,128]{1,0:T(8,128)(2,1)S(1)} %get-tuple-element.39), channel_id=1, source_target_pairs={{0,2},{2,4},{4,6},{6,7},{7,5},{5,3},{3,1},{1,0},{8,10},{10,12},{12... | collective-permute-start | bytes 393224 | tf_op jit(solution)/shard_map/ppermute | solution.py:282
  45.8 5.1 %collective-permute-start.9 = (bf16[512,128]{1,0:T(8,128)(2,1)S(1)}, bf16[512,128]{1,0:T(8,128)(2,1)S(1)}, u32[]{:S(2)}, u32[]{:S(2)}) collective-permute-start(bf16[512,128]{1,0:T(8,128)(2,1)S(1)} %get-tuple-element.38), channel_id=1, source_target_pairs={{0,2},{2,4},{4,6},{6,7},{7,5},{5,3},{3,1},{1,0},{8,10},{10,12},{12... | collective-permute-start | bytes 393224 | tf_op jit(solution)/shard_map/ppermute | solution.py:282
  47.0 5.2 %collective-permute-start.10 = (bf16[512,128]{1,0:T(8,128)(2,1)S(1)}, bf16[512,128]{1,0:T(8,128)(2,1)S(1)}, u32[]{:S(2)}, u32[]{:S(2)}) collective-permute-start(bf16[512,128]{1,0:T(8,128)(2,1)S(1)} %get-tuple-element.39), channel_id=1, source_target_pairs={{0,1},{2,0},{4,2},{6,4},{7,6},{5,7},{3,5},{1,3},{8,9},{10,8},{12,1... | collective-permute-start | bytes 393224 | tf_op jit(solution)/shard_map/ppermute | solution.py:282
  47.3 6.2 %collective-permute-start.11 = (bf16[512,128]{1,0:T(8,128)(2,1)S(1)}, bf16[512,128]{1,0:T(8,128)(2,1)S(1)}, u32[]{:S(2)}, u32[]{:S(2)}) collective-permute-start(bf16[512,128]{1,0:T(8,128)(2,1)S(1)} %get-tuple-element.38), channel_id=1, source_target_pairs={{0,1},{2,0},{4,2},{6,4},{7,6},{5,7},{3,5},{1,3},{8,9},{10,8},{12,1... | collective-permute-start | bytes 393224 | tf_op jit(solution)/shard_map/ppermute | solution.py:282
  49.5 4.7 %collective-permute-start.12 = (bf16[512,128]{1,0:T(8,128)(2,1)S(1)}, bf16[512,128]{1,0:T(8,128)(2,1)S(1)}, u32[]{:S(2)}, u32[]{:S(2)}) collective-permute-start(bf16[512,128]{1,0:T(8,128)(2,1)S(1)} %collective-permute-done.8.refs_0_), channel_id=1, source_target_pairs={{0,2},{2,4},{4,6},{6,7},{7,5},{5,3},{3,1},{1,0},{8,10},{10,12},{12... | collective-permute-start | bytes 393224 | tf_op jit(solution)/shard_map/ppermute | solution.py:282
  50.9 3.8 %collective-permute-start.13 = (bf16[512,128]{1,0:T(8,128)(2,1)S(1)}, bf16[512,128]{1,0:T(8,128)(2,1)S(1)}, u32[]{:S(2)}, u32[]{:S(2)}) collective-permute-start(bf16[512,128]{1,0:T(8,128)(2,1)S(1)} %collective-permute-done.9.refs_1_), channel_id=1, source_target_pairs={{0,2},{2,4},{4,6},{6,7},{7,5},{5,3},{3,1},{1,0},{8,10},{10,12},{12... | collective-permute-start | bytes 393224 | tf_op jit(solution)/shard_map/ppermute | solution.py:282
  52.2 3.8 %collective-permute-start.14 = (bf16[512,128]{1,0:T(8,128)(2,1)S(1)}, bf16[512,128]{1,0:T(8,128)(2,1)S(1)}, u32[]{:S(2)}, u32[]{:S(2)}) collective-permute-start(bf16[512,128]{1,0:T(8,128)(2,1)S(1)} %collective-permute-done.10.refs_2_), channel_id=1, source_target_pairs={{0,1},{2,0},{4,2},{6,4},{7,6},{5,7},{3,5},{1,3},{8,9},{10,8},{12,1... | collective-permute-start | bytes 393224 | tf_op jit(solution)/shard_map/ppermute | solution.py:282
  53.5 3.9 %collective-permute-start.15 = (bf16[512,128]{1,0:T(8,128)(2,1)S(1)}, bf16[512,128]{1,0:T(8,128)(2,1)S(1)}, u32[]{:S(2)}, u32[]{:S(2)}) collective-permute-start(bf16[512,128]{1,0:T(8,128)(2,1)S(1)} %collective-permute-done.11.refs_3_), channel_id=1, source_target_pairs={{0,1},{2,0},{4,2},{6,4},{7,6},{5,7},{3,5},{1,3},{8,9},{10,8},{12,1... | collective-permute-start | bytes 393224 | tf_op jit(solution)/shard_map/ppermute | solution.py:282
  58.5 2.6 %collective-permute-start.16 = (f32[5,64,128]{2,1,0:T(8,128)S(1)}, f32[5,64,128]{2,1,0:T(8,128)S(1)}, u32[]{:S(2)}, u32[]{:S(2)}) collective-permute-start(f32[5,64,128]{2,1,0:T(8,128)S(1)} %constant_dynamic-slice_fusion.1), channel_id=1, source_target_pairs={{0,8},{8,0},{16,24},{24,16},{1,9},{9,1},{17,25},{25,17},{2,10},{10... | collective-permute-start | bytes 491528 | tf_op jit(solution)/shard_map/ppermute | solution.py:31
  58.6 3.2 %collective-permute-start.17 = (bf16[256,128]{1,0:T(8,128)(2,1)S(1)}, bf16[256,128]{1,0:T(8,128)(2,1)S(1)}, u32[]{:S(2)}, u32[]{:S(2)}) collective-permute-start(bf16[256,128]{1,0:T(8,128)(2,1)S(1)} %get-tuple-element.31), channel_id=1, source_target_pairs={{0,2},{2,4},{4,6},{6,7},{7,5},{5,3},{3,1},{1,0},{8,10},{10,12},{12... | collective-permute-start | bytes 196616 | tf_op jit(solution)/shard_map/ppermute | solution.py:282
  59.9 3.1 %collective-permute-start.18 = (bf16[256,128]{1,0:T(8,128)(2,1)S(1)}, bf16[256,128]{1,0:T(8,128)(2,1)S(1)}, u32[]{:S(2)}, u32[]{:S(2)}) collective-permute-start(bf16[256,128]{1,0:T(8,128)(2,1)S(1)} %get-tuple-element.32), channel_id=1, source_target_pairs={{0,1},{2,0},{4,2},{6,4},{7,6},{5,7},{3,5},{1,3},{8,9},{10,8},{12,1... | collective-permute-start | bytes 196616 | tf_op jit(solution)/shard_map/ppermute | solution.py:282
  60.1 5.3 %collective-permute-start.19 = (bf16[256,128]{1,0:T(8,128)(2,1)S(1)}, bf16[256,128]{1,0:T(8,128)(2,1)S(1)}, u32[]{:S(2)}, u32[]{:S(2)}) collective-permute-start(bf16[256,128]{1,0:T(8,128)(2,1)S(1)} %get-tuple-element.33), channel_id=1, source_target_pairs={{0,3},{2,1},{4,0},{6,2},{7,4},{5,6},{3,7},{1,5},{8,11},{10,9},{12,... | collective-permute-start | bytes 196616 | tf_op jit(solution)/shard_map/ppermute | solution.py:282
  65.5 5.2 %collective-permute-start.22 = (f32[3,64,128]{2,1,0:T(8,128)S(1)}, f32[3,64,128]{2,1,0:T(8,128)S(1)}, u32[]{:S(2)}, u32[]{:S(2)}) collective-permute-start(f32[3,64,128]{2,1,0:T(8,128)S(1)} %constant_dynamic-slice_fusion), channel_id=1, source_target_pairs={{0,8},{8,0},{16,24},{24,16},{1,9},{9,1},{17,25},{25,17},{2,10},{10... | collective-permute-start | bytes 294920 | tf_op jit(solution)/shard_map/ppermute | solution.py:31
  68.2 5.2 %collective-permute-start.20 = (bf16[5,64,128]{2,1,0:T(8,128)(2,1)S(1)}, bf16[5,64,128]{2,1,0:T(8,128)(2,1)S(1)}, u32[]{:S(2)}, u32[]{:S(2)}) collective-permute-start(bf16[5,64,128]{2,1,0:T(8,128)(2,1)S(1)} %add_convert_fusion), channel_id=1, source_target_pairs={{0,16},{8,24},{16,0},{24,8},{1,17},{9,25},{17,1},{25,9},{2,18},{10... | collective-permute-start | bytes 245768 | tf_op jit(solution)/shard_map/ppermute | solution.py:360
  70.7 3.6 %collective-permute-start.23 = (bf16[3,64,128]{2,1,0:T(8,128)(2,1)S(1)}, bf16[3,64,128]{2,1,0:T(8,128)(2,1)S(1)}, u32[]{:S(2)}, u32[]{:S(2)}) collective-permute-start(bf16[3,64,128]{2,1,0:T(8,128)(2,1)S(1)} %add_convert_fusion.1), channel_id=1, source_target_pairs={{0,16},{8,24},{16,0},{24,8},{1,17},{9,25},{17,1},{25,9},{2,18},{10... | collective-permute-start | bytes 147464 | tf_op jit(solution)/shard_map/ppermute | solution.py:360
  73.4 3.2 %collective-permute-start.21 = (f32[5,64,128]{2,1,0:T(8,128)S(1)}, f32[5,64,128]{2,1,0:T(8,128)S(1)}, u32[]{:S(2)}, u32[]{:S(2)}) collective-permute-start(f32[5,64,128]{2,1,0:T(8,128)S(1)} %convert_add_fusion.refs_0_), channel_id=1, source_target_pairs={{0,8},{8,0},{16,24},{24,16},{1,9},{9,1},{17,25},{25,17},{2,10},{10... | collective-permute-start | bytes 491528 | tf_op jit(solution)/shard_map/ppermute | solution.py:31
  74.3 2.3 %collective-permute-start.24 = (f32[3,64,128]{2,1,0:T(8,128)S(1)}, f32[3,64,128]{2,1,0:T(8,128)S(1)}, u32[]{:S(2)}, u32[]{:S(2)}) collective-permute-start(f32[3,64,128]{2,1,0:T(8,128)S(1)} %convert_add_fusion.1.refs_2_), channel_id=1, source_target_pairs={{0,8},{8,0},{16,24},{24,16},{1,9},{9,1},{17,25},{25,17},{2,10},{10... | collective-permute-start | bytes 294920 | tf_op jit(solution)/shard_map/ppermute | solution.py:31

commit v3 on v2

--- a/solution.py
+++ b/solution.py
@@ -174,63 +174,37 @@
     return (group,)
 
 
-def whole(chunk):
-    low, high = chunk
-    return jnp.concatenate([low[...], high[...]], axis=0)
-
-
-def in_pairs(chunks):
-    return [chunks[t:t + 2] for t in range(0, len(chunks), 2)]
-
-
 def early_gram(mine, *refs):
-    *chunks, partial, lefts = refs
-    half = mine.shape[0] // 2
+    *blocks, partial, lefts = refs
     left = mine[...].T
     lefts[0] = left
-    for t, chunk in enumerate([(mine.at[:half], mine.at[half:])] + in_pairs(chunks)):
-        block = whole(chunk)
+    for t, ref in enumerate((mine, *blocks)):
+        block = ref[...]
         if t:
             lefts[t] = block.T
         partial[t] = dot(left, block)
 
 
-def rows_of(chunk, device, share, put):
-    low, high = chunk
-    half = low.shape[0]
-    start = pl.multiple_of(device * share, share)
-
-    @pl.when(start < half)
-    def _():
-        put(low[pl.ds(start, share)])
-
-    @pl.when(start >= half)
-    def _():
-        put(high[pl.ds(start - half, share)])
-
-
-def late_gram(where, lefts, early, *refs):
-    back, front = refs[:2], refs[2:4]
-    partial, *messages = refs[4:]
-    width = partial.shape[1]
+def far_messages(where, lefts, back, front, *messages):
+    width = lefts.shape[1]
     share = messages[0].shape[0] - width
     reach = lefts.shape[0] // 2 + 1
-    far_back, far_front = whole(back), whole(front)
-    partial[:2 * reach - 1] = early[...]
-    partial[2 * reach - 1] = dot(lefts[0], far_back)
-    partial[2 * reach] = dot(lefts[0], far_front)
+    far_back, far_front = back[...], front[...]
     made = []
     for t in range(1, reach):
         made.append((dot(lefts[2 * t], far_back), back, where[2 * t]))
         made.append((dot(lefts[2 * t - 1], far_front), front, where[2 * t - 1]))
     made.append((dot(far_back.T, far_front), front, where[2 * reach - 1]))
-    for message, (block, chunk, device) in zip(messages, made):
+    for message, (block, source, device) in zip(messages, made):
         message[:width] = block.astype(message.dtype)
-
-        def put(rows, message=message):
-            message[width:] = rows
-
-        rows_of(chunk, device, share, put)
+        message[width:] = source[pl.ds(pl.multiple_of(device * share, share), share)]
+
+
+def own_blocks(lefts, early, back, front, _, partial):
+    held = early.shape[0]
+    partial[:held] = early[...]
+    partial[held] = dot(lefts[0], back[...])
+    partial[held + 1] = dot(lefts[0], front[...])
 
 
 def place_blocks(scale, where, odd, *refs):
@@ -249,19 +223,14 @@
 
 
 def filtered_rows(number, where, mine, *refs):
-    chunks, messages, rowwise = refs[:number], refs[number:-1], refs[-1]
-    rows, width = mine.shape
-    half = rows // 2
+    blocks, messages, rowwise = (mine,) + refs[:number], refs[number:-1], refs[-1]
+    width = mine.shape[1]
     share = rowwise.shape[-2]
-    for t, chunk in enumerate([(mine.at[:half], mine.at[half:])] + in_pairs(chunks)):
-
-        def put(rows, t=t):
-            rowwise[columns_at(rowwise, where[t], width)] = rows
-
-        rows_of(chunk, where[0], share, put)
+    start = pl.multiple_of(where[0] * share, share)
+    for t, block in enumerate(blocks):
+        rowwise[columns_at(rowwise, where[t], width)] = block[pl.ds(start, share)]
     for t, message in enumerate(messages):
-        at = columns_at(rowwise, where[1 + number // 2 + t], width)
-        rowwise[at] = message[width:]
+        rowwise[columns_at(rowwise, where[1 + number + t], width)] = message[width:]
 
 
 def ring_of(size):
@@ -275,7 +244,6 @@
     reach = size // 4
     order = ring_of(size)
     rows, width = mine.shape
-    half = rows // 2
     share = rows // size
 
     def move(value, by):
@@ -283,13 +251,10 @@
             value, "cols", [(order[i], order[(i + by) % size]) for i in range(size)]
         )
 
-    low_ahead = low_behind = mine[:half]
-    high_ahead = high_behind = mine[half:]
-    chunks, steps = [], [0]
+    fetched = {by: move(mine, by) for t in range(reach, 0, -1) for by in (t, -t)}
+    blocks, steps = [], [0]
     for t in range(1, reach + 1):
-        low_ahead, high_behind = move(low_ahead, 1), move(high_behind, -1)
-        high_ahead, low_behind = move(high_ahead, 1), move(low_behind, -1)
-        chunks += [low_ahead, high_ahead, low_behind, high_behind]
+        blocks += [fetched[t], fetched[-t]]
         steps += [-t, t]
     sends = [by for t in range(1, reach) for by in (t, -t)] + [-reach]
     steps += [-(by + reach) if by > 0 else reach - by for by in sends]
@@ -305,19 +270,25 @@
             jax.ShapeDtypeStruct((held, width, width), jnp.float32),
             jax.ShapeDtypeStruct((held, width, rows), mine.dtype),
         ),
-        in_specs=[VMEM] * (1 + 4 * (reach - 1)),
+        in_specs=[VMEM] * held,
         out_specs=(VMEM, VMEM),
         compiler_params=params(16),
-    )(mine, *chunks[:-4])
+    )(mine, *blocks[:-2])
     message = jax.ShapeDtypeStruct((width + share, width), mine.dtype)
-    own, *messages = pl.pallas_call(
-        late_gram,
-        out_shape=(jax.ShapeDtypeStruct((held + 2, width, width), jnp.float32),)
-        + (message,) * len(sends),
-        in_specs=[SMEM] + [VMEM] * 6,
-        out_specs=(VMEM,) * (1 + len(sends)),
-        compiler_params=params(16),
-    )(where, lefts, early, *chunks[-4:])
+    messages = pl.pallas_call(
+        far_messages,
+        out_shape=(message,) * len(sends),
+        in_specs=[SMEM] + [VMEM] * 3,
+        out_specs=(VMEM,) * len(sends),
+        compiler_params=params(16),
+    )(where, lefts, *blocks[-2:])
+    own = pl.pallas_call(
+        own_blocks,
+        out_shape=jax.ShapeDtypeStruct((held + 2, width, width), jnp.float32),
+        in_specs=[VMEM] * 4 + [pl.BlockSpec(memory_space=pl.ANY)],
+        out_specs=VMEM,
+        compiler_params=params(16),
+    )(lefts, early, *blocks[-2:], messages[-1])
     messages = [move(value, by) for value, by in zip(messages, sends)]
     own, messages = lax.optimization_barrier((sum_of_cores(own), messages))
     far = jnp.stack([message[:width] for message in messages]).astype(jnp.float32)
@@ -333,12 +304,12 @@
     )(where, (lax.axis_index("rows") & 1)[None], *sum_of_chips(own),
       *sum_of_chips(sum_of_cores(far)))
     rowwise = pl.pallas_call(
-        functools.partial(filtered_rows, len(chunks)),
+        functools.partial(filtered_rows, len(blocks)),
         out_shape=jax.ShapeDtypeStruct(shape(share), mine.dtype),
-        in_specs=[SMEM] + [VMEM] * (1 + len(chunks) + len(messages)),
-        out_specs=VMEM,
-        compiler_params=params(16),
-    )(where, mine, *chunks, *messages)
+        in_specs=[SMEM] + [VMEM] * (1 + len(blocks) + len(messages)),
+        out_specs=VMEM,
+        compiler_params=params(16),
+    )(where, mine, *blocks, *messages)
     if not flat:
         gram = gram.transpose(1, 0, 2).reshape(width, size * width)
         rowwise = rowwise.transpose(1, 0, 2).reshape(share, size * width)
@@ -373,6 +344,7 @@
     share = search_vectors.shape[0]
     width = search_vectors.shape[1] // col_parts
     rows = share * col_parts
+    second = with_chip(tile_values)
     pieces = pl.pallas_call(
         split_columns,
         out_shape=jax.ShapeDtypeStruct((col_parts, share, width), search_vectors.dtype),
@@ -380,8 +352,6 @@
         out_specs=VMEM,
         compiler_params=params(4),
     )(search_vectors)
-    pieces, far_tiles = lax.optimization_barrier((pieces, tile_values))
-    second = with_chip(far_tiles)
     columns = lax.all_to_all(pieces, "cols", split_axis=0, concat_axis=0, tiled=True)
     columns = columns.reshape(rows, width)
 

time: 78.5 us -> 76.7 us (0.977)
  starting transfers between devices: 36.5 us -> 32.5 us
  waiting for transfers between devices: 20.5 us -> 22.8 us
    ppermute x2, starting transfers between devices: 3.45 us -> 1.48 us  [sum_of_chips(): got = lax.ppermute(sent, 'rows', [(i, i ^ bit) for i in range(size)])]
    ppermute x11 -> x7, waiting for transfers between devices: 10.9 us -> 12.3 us  [move(): lax.ppermute(value, 'cols', [(order[i], order[(i + by) % size]) for i in...]
    ppermute x11 -> x7, starting transfers between devices: 8.81 us -> 7.69 us  [move(): lax.ppermute(value, 'cols', [(order[i], order[(i + by) % size]) for i in...]
    ppermute x8, starting transfers between devices: 5.3 us -> 4.32 us  [with_core(): lax.ppermute(value, 'rows', [(i, i ^ 1) for i in range(lax.axis_size('row...]
    pallas_call x2 -> x3, Pallas kernels: 2.45 us -> 2.5 us  [the longest x1 1.31 us: gram_and_rows(): pl.pallas_call(functools.partial(filtered_rows, len(blocks)), out_shape=j...]
  transfers between devices with their start and end apart: 26 -> 22, of which waited for: 13 -> 10; matrix products, arithmetic and copies ran while one was open for 1% -> 1% of each run, Pallas kernels for 8% -> 9%
where the time goes in v3:
time: 76.7 us; the launch traced here: 76.2 us
  starting transfers between devices  32.5 us (42%)
  waiting for transfers between devices  22.8 us (30%)
  Pallas kernels  16.4 us (21%)
  local copies, waits for them, and re-layouts  2.9 us (4%)
  between operations  0.89 us (1%)
  other arithmetic  0.83 us (1%)
    ppermute x4, starting transfers between devices, with_chip(): lax.ppermute(value, 'rows', [p for k in odds for p in ((k, k + 1), (k + 1...  13.4 us
    ppermute x7, waiting for transfers between devices, move(): lax.ppermute(value, 'cols', [(order[i], order[(i + by) % size]) for i in...  12.3 us
    ppermute x4, waiting for transfers between devices, with_chip(): lax.ppermute(value, 'rows', [p for k in odds for p in ((k, k + 1), (k + 1...  7.9 us
    ppermute x7, starting transfers between devices, move(): lax.ppermute(value, 'cols', [(order[i], order[(i + by) % size]) for i in...  7.69 us
    all_to_all x1, starting transfers between devices, per_device(): lax.all_to_all(pieces, 'cols', split_axis=0, concat_axis=0, tiled=True)  5.55 us
    ppermute x8, starting transfers between devices, with_core(): lax.ppermute(value, 'rows', [(i, i ^ 1) for i in range(lax.axis_size('row...  4.32 us
    pallas_call x1, Pallas kernels, per_device(): pl.pallas_call(second_stage, out_shape=jax.ShapeDtypeStruct((rows, width)...  3.38 us
    pallas_call x1, Pallas kernels, per_device(): pl.pallas_call(first_stage, out_shape=(jax.ShapeDtypeStruct((rows, width)...  3.28 us
  transfers between devices with their start and end apart: 22, of which 10 were waited for; matrix products, arithmetic and copies ran while one was open for 1% of the time, Pallas kernels for 9%

profile of v3, /device:TPU:1, one launch (start us, length us, event | category | flops | bytes accessed | tf_op | source)
XLA Modules:
  0.0 76.2 jit_solution(9352329848913842162)
XLA Ops:
  0.6 4.5 %collective-permute-start.3 = (bf16[16,64,512]{2,1,0:T(8,128)(2,1)}, bf16[16,64,512]{2,1,0:T(8,128)(2,1)S(1)}, u32[]{:S(2)}, u32[]{:S(2)}) collective-permute-start(bf16[16,64,512]{2,1,0:T(8,128)(2,1)} %tiles.1), channel_id=1, source_target_pairs={{8,16},{16,8},{9,17},{17,9},{10,18},{18,10},{11,19},{19,11},{12,20... | collective-permute-start | bytes 3145736 | tf_op jit(solution)/shard_map/ppermute | solution.py:36
  5.2 0.9 %copy-done.1 = bf16[128,1024]{1,0:T(8,128)(2,1)S(1)} copy-done((bf16[128,1024]{1,0:T(8,128)(2,1)S(1)}, bf16[128,1024]{1,0:T(8,128)(2,1)}, u32[]{:S(2)}) %copy-start.1) | copy-done | bytes 262168
  6.1 0.7 shard_map.59._
  6.8 5.6 %all-to-all-start = ((bf16[8,128,128]{2,1,0:T(8,128)(2,1)}), bf16[8,128,128]{2,1,0:T(8,128)(2,1)S(1)}, u32[]{:S(2)}, u32[]{:S(2)}) async-start(bf16[8,128,128]{2,1,0:T(8,128)(2,1)} %shard_map.59._), calls=%async_computation | async-start | bytes 524288 | tf_op jit(solution)/shard_map/all_to_all | solution.py:355
  13.1 1.2 %copy-done = bf16[16,64,512]{2,1,0:T(8,128)(2,1)S(1)} copy-done((bf16[16,64,512]{2,1,0:T(8,128)(2,1)S(1)}, bf16[16,64,512]{2,1,0:T(8,128)(2,1)}, u32[]{:S(2)}) %copy-start) | copy-done | bytes 1048600
  15.0 2.3 %shard_map.60 = (bf16[4,256,768]{2,1,0:T(8,128)(2,1)S(1)}, bf16[12,64,512]{2,1,0:T(8,128)(2,1)}, s32[8,16]{1,0:T(8,128)S(1)}) custom-call(s32[1]{0:T(128)} %bitcast.odd, s32[8,16]{1,0:T(8,128)S(1)} %subtract_clamp_fusion.2.offsets, s32[8,16]{1,0:T(8,128)S(1)} %bitcast.13, bf16[16,64,512]{2,1,0:T(8,128)(2,1)S(1)} %copy-done, bf16[8,128,128]{2,1,0:T(8,128)(2,1)} %shard_map.59._), custom_call_target="tpu_custom_call" | custom-call | tf_op jit(solution)/shard_map/pallas_call | solution.py:370
  17.9 2.2 %collective-permute-start.1 = (s32[8,16]{1,0:T(8,128)S(1)}, s32[8,16]{1,0:T(8,128)S(1)}, u32[]{:S(2)}, u32[]{:S(2)}) collective-permute-start(s32[8,16]{1,0:T(8,128)S(1)} %get-tuple-element.18), channel_id=1, source_target_pairs={{8,16},{16,8},{9,17},{17,9},{10,18},{18,10},{11,19},{19,11},{12,20... | collective-permute-start | bytes 1544 | tf_op jit(solution)/shard_map/ppermute | solution.py:36
  20.2 3.4 %collective-permute-start.5 = (bf16[1024,128]{1,0:T(8,128)(2,1)S(1)}, bf16[1024,128]{1,0:T(8,128)(2,1)S(1)}, u32[]{:S(2)}, u32[]{:S(2)}) collective-permute-start(bf16[1024,128]{1,0:T(8,128)(2,1)S(1)} %bitcast.11), channel_id=1, source_target_pairs={{8,16},{16,8},{9,17},{17,9},{10,18},{18,10},{11,19},{19,11},{12,20... | collective-permute-start | bytes 786440 | tf_op jit(solution)/shard_map/ppermute | solution.py:36
  23.6 2.4 %shard_map.61.edges = bf16[6,256,768]{2,1,0:T(8,128)(2,1)S(1)} custom-call(s32[1]{0:T(128)} %bitcast.odd, s32[8,16]{1,0:T(8,128)S(1)} %subtract_clamp_fusion.1.at_first, s32[8,16]{1,0:T(8,128)S(1)} %subtract_clamp_fusion.at_second, bf16[12,64,512]{2,1,0:T(8,128)(2,1)} %collective-permute-done.2.first, bf16[16,64,512]{2,1,0:T(8,128)(2,1)S(1)} %collective-permute-done.3.second), custom_call_target="tpu_custom_call" | custom-call | tf_op jit(solution)/shard_map/pallas_call | solution.py:385
  26.0 1.9 %collective-permute-done.5.x_second = bf16[1024,128]{1,0:T(8,128)(2,1)S(1)} collective-permute-done((bf16[1024,128]{1,0:T(8,128)(2,1)S(1)}, bf16[1024,128]{1,0:T(8,128)(2,1)S(1)}, u32[]{:S(2)}, u32[]{:S(2)}) %collective-permute-start.5) | collective-permute-done | bytes 262176 | tf_op jit(solution)/shard_map/ppermute | solution.py:36
  27.9 3.3 %shard_map.62 = (f32[1024,128]{1,0:T(8,128)S(1)}, f32[1536,128]{1,0:T(8,128)S(1)}, bf16[1536,128]{1,0:T(8,128)(2,1)S(1)}) custom-call(s32[1]{0:T(128)} %bitcast.odd, bf16[4,256,768]{2,1,0:T(8,128)(2,1)S(1)} %get-tuple-element.17.own, bf16[6,256,768]{2,1,0:T(8,128)(2,1)S(1)} %shard_map.61.edges, bf16[1024,128]{1,0:T(8,128)(2,1)S(1)} %collective-permute-done.4.x_first, ...), custom_call_target="tpu_custom_call" | custom-call | tf_op jit(solution)/shard_map/pallas_call | solution.py:408
  31.3 3.4 %collective-permute-start.7 = (bf16[1536,128]{1,0:T(8,128)(2,1)S(1)}, bf16[1536,128]{1,0:T(8,128)(2,1)S(1)}, u32[]{:S(2)}, u32[]{:S(2)}) collective-permute-start(bf16[1536,128]{1,0:T(8,128)(2,1)S(1)} %get-tuple-element.22), channel_id=1, source_target_pairs={{8,16},{16,8},{9,17},{17,9},{10,18},{18,10},{11,19},{19,11},{12,20... | collective-permute-start | bytes 1179656 | tf_op jit(solution)/shard_map/ppermute | solution.py:36
  34.6 6.0 %collective-permute-done.7.got_second = bf16[1536,128]{1,0:T(8,128)(2,1)S(1)} collective-permute-done((bf16[1536,128]{1,0:T(8,128)(2,1)S(1)}, bf16[1536,128]{1,0:T(8,128)(2,1)S(1)}, u32[]{:S(2)}, u32[]{:S(2)}) %collective-permute-start.7) | collective-permute-done | bytes 393248 | tf_op jit(solution)/shard_map/ppermute | solution.py:36
  40.7 3.4 %shard_map.63.mine = bf16[1024,128]{1,0:T(8,128)(2,1)S(1)} custom-call(s32[1]{0:T(128)} %bitcast.odd, bf16[4,256,768]{2,1,0:T(8,128)(2,1)S(1)} %get-tuple-element.17.own, bf16[6,256,768]{2,1,0:T(8,128)(2,1)S(1)} %shard_map.61.edges, f32[1024,128]{1,0:T(8,128)S(1)} %get-tuple-element.20.now, f32[1536,128]{1,0:T(8,128)S(1)} %get-tuple-element.21.last, ...), custom_call_target="tpu_custom_call" | custom-call | tf_op jit(solution)/shard_map/pallas_call | solution.py:422
  44.0 1.8 %collective-permute-start.8 = (bf16[1024,128]{1,0:T(8,128)(2,1)S(1)}, bf16[1024,128]{1,0:T(8,128)(2,1)S(1)}, u32[]{:S(2)}, u32[]{:S(2)}) collective-permute-start(bf16[1024,128]{1,0:T(8,128)(2,1)S(1)} %shard_map.63.mine), channel_id=1, source_target_pairs={{0,2},{2,4},{4,6},{6,7},{7,5},{5,3},{3,1},{1,0},{8,10},{10,12},{12... | collective-permute-start | bytes 786440 | tf_op jit(solution)/shard_map/ppermute | solution.py:250
  45.9 2.3 %collective-permute-start.10 = (bf16[1024,128]{1,0:T(8,128)(2,1)S(1)}, bf16[1024,128]{1,0:T(8,128)(2,1)S(1)}, u32[]{:S(2)}, u32[]{:S(2)}) collective-permute-start(bf16[1024,128]{1,0:T(8,128)(2,1)S(1)} %shard_map.63.mine), channel_id=1, source_target_pairs={{0,4},{2,6},{4,7},{6,5},{7,3},{5,1},{3,0},{1,2},{8,12},{10,14},{12... | collective-permute-start | bytes 786440 | tf_op jit(solution)/shard_map/ppermute | solution.py:250
  48.3 2.4 %collective-permute-done.8.refs_0_ = bf16[1024,128]{1,0:T(8,128)(2,1)S(1)} collective-permute-done((bf16[1024,128]{1,0:T(8,128)(2,1)S(1)}, bf16[1024,128]{1,0:T(8,128)(2,1)S(1)}, u32[]{:S(2)}, u32[]{:S(2)}) %collective-permute-start.8) | collective-permute-done | bytes 262176 | tf_op jit(solution)/shard_map/ppermute | solution.py:250
  50.6 2.1 %collective-permute-done.9.refs_1_ = bf16[1024,128]{1,0:T(8,128)(2,1)S(1)} collective-permute-done((bf16[1024,128]{1,0:T(8,128)(2,1)S(1)}, bf16[1024,128]{1,0:T(8,128)(2,1)S(1)}, u32[]{:S(2)}, u32[]{:S(2)}) %collective-permute-start.9) | collective-permute-done | bytes 262176 | tf_op jit(solution)/shard_map/ppermute | solution.py:250
  53.2 3.2 %collective-permute-done.10.back.refs_2_ = bf16[1024,128]{1,0:T(8,128)(2,1)S(1)} collective-permute-done((bf16[1024,128]{1,0:T(8,128)(2,1)S(1)}, bf16[1024,128]{1,0:T(8,128)(2,1)S(1)}, u32[]{:S(2)}, u32[]{:S(2)}) %collective-permute-start.10) | collective-permute-done | bytes 262176 | tf_op jit(solution)/shard_map/ppermute | solution.py:250
  56.4 1.0 %collective-permute-done.11.front.refs_3_ = bf16[1024,128]{1,0:T(8,128)(2,1)S(1)} collective-permute-done((bf16[1024,128]{1,0:T(8,128)(2,1)S(1)}, bf16[1024,128]{1,0:T(8,128)(2,1)S(1)}, u32[]{:S(2)}, u32[]{:S(2)}) %collective-permute-start.11) | collective-permute-done | bytes 262176 | tf_op jit(solution)/shard_map/ppermute | solution.py:250
  57.4 0.9 %shard_map.65 = (bf16[256,128]{1,0:T(8,128)(2,1)S(1)}, bf16[256,128]{1,0:T(8,128)(2,1)S(1)}, bf16[256,128]{1,0:T(8,128)(2,1)S(1)}) custom-call(s32[8]{0:T(128)S(1)} %compare_select_fusion.2.where, bf16[3,128,1024]{2,1,0:T(8,128)(2,1)S(1)} %get-tuple-element.23.lefts, bf16[1024,128]{1,0:T(8,128)(2,1)S(1)} %collective-permute-done.10.back.refs_2_, ...), custom_call_target="tpu_custom_call" | custom-call | tf_op jit(solution)/shard_map/pallas_call | solution.py:278
  58.7 1.8 %collective-permute-start.15 = (bf16[256,128]{1,0:T(8,128)(2,1)S(1)}, bf16[256,128]{1,0:T(8,128)(2,1)S(1)}, u32[]{:S(2)}, u32[]{:S(2)}) collective-permute-start(bf16[256,128]{1,0:T(8,128)(2,1)S(1)} %get-tuple-element.25._), channel_id=1, source_target_pairs={{0,3},{2,1},{4,0},{6,2},{7,4},{5,6},{3,7},{1,5},{8,11},{10,9},{12,... | collective-permute-start | bytes 196616 | tf_op jit(solution)/shard_map/ppermute | solution.py:250
  60.5 1.7 %collective-permute-start.13 = (bf16[256,128]{1,0:T(8,128)(2,1)S(1)}, bf16[256,128]{1,0:T(8,128)(2,1)S(1)}, u32[]{:S(2)}, u32[]{:S(2)}) collective-permute-start(bf16[256,128]{1,0:T(8,128)(2,1)S(1)} %get-tuple-element.26), channel_id=1, source_target_pairs={{0,2},{2,4},{4,6},{6,7},{7,5},{5,3},{3,1},{1,0},{8,10},{10,12},{12... | collective-permute-start | bytes 196616 | tf_op jit(solution)/shard_map/ppermute | solution.py:250
  62.2 1.8 %collective-permute-done.13.refs_4_ = bf16[256,128]{1,0:T(8,128)(2,1)S(1)} collective-permute-done((bf16[256,128]{1,0:T(8,128)(2,1)S(1)}, bf16[256,128]{1,0:T(8,128)(2,1)S(1)}, u32[]{:S(2)}, u32[]{:S(2)}) %collective-permute-start.13) | collective-permute-done | bytes 65568 | tf_op jit(solution)/shard_map/ppermute | solution.py:250
  64.0 1.9 %collective-permute-done.14.refs_5_ = bf16[256,128]{1,0:T(8,128)(2,1)S(1)} collective-permute-done((bf16[256,128]{1,0:T(8,128)(2,1)S(1)}, bf16[256,128]{1,0:T(8,128)(2,1)S(1)}, u32[]{:S(2)}, u32[]{:S(2)}) %collective-permute-start.14) | collective-permute-done | bytes 65568 | tf_op jit(solution)/shard_map/ppermute | solution.py:250
  65.9 1.7 %collective-permute-start.18 = (f32[3,64,128]{2,1,0:T(8,128)S(1)}, f32[3,64,128]{2,1,0:T(8,128)S(1)}, u32[]{:S(2)}, u32[]{:S(2)}) collective-permute-start(f32[3,64,128]{2,1,0:T(8,128)S(1)} %constant_dynamic-slice_fusion), channel_id=1, source_target_pairs={{0,8},{8,0},{16,24},{24,16},{1,9},{9,1},{17,25},{25,17},{2,10},{10... | collective-permute-start | bytes 294920 | tf_op jit(solution)/shard_map/ppermute | solution.py:31
  67.5 0.7 collective-permute-start.16
  68.5 0.8 %collective-permute-start.19 = (bf16[3,64,128]{2,1,0:T(8,128)(2,1)S(1)}, bf16[3,64,128]{2,1,0:T(8,128)(2,1)S(1)}, u32[]{:S(2)}, u32[]{:S(2)}) collective-permute-start(bf16[3,64,128]{2,1,0:T(8,128)(2,1)S(1)} %add_convert_fusion.1), channel_id=1, source_target_pairs={{0,16},{8,24},{16,0},{24,8},{1,17},{9,25},{17,1},{25,9},{2,18},{10... | collective-permute-start | bytes 147464 | tf_op jit(solution)/shard_map/ppermute | solution.py:331
  69.3 2.3 %collective-permute-done.16 = bf16[5,64,128]{2,1,0:T(8,128)(2,1)S(1)} collective-permute-done((bf16[5,64,128]{2,1,0:T(8,128)(2,1)S(1)}, bf16[5,64,128]{2,1,0:T(8,128)(2,1)S(1)}, u32[]{:S(2)}, u32[]{:S(2)}) %collective-permute-start.16) | collective-permute-done | bytes 81952 | tf_op jit(solution)/shard_map/ppermute | solution.py:331
  71.6 1.4 %collective-permute-start.17 = (f32[5,64,128]{2,1,0:T(8,128)S(1)}, f32[5,64,128]{2,1,0:T(8,128)S(1)}, u32[]{:S(2)}, u32[]{:S(2)}) collective-permute-start(f32[5,64,128]{2,1,0:T(8,128)S(1)} %convert_add_fusion.refs_0_), channel_id=1, source_target_pairs={{0,8},{8,0},{16,24},{24,16},{1,9},{9,1},{17,25},{25,17},{2,10},{10... | collective-permute-start | bytes 491528 | tf_op jit(solution)/shard_map/ppermute | solution.py:31
  73.5 1.3 %shard_map.67 = bf16[128,1024]{1,0:T(8,128)(2,1)} custom-call(s32[8]{0:T(128)S(1)} %compare_select_fusion.2.where, bf16[1024,128]{1,0:T(8,128)(2,1)S(1)} %shard_map.63.mine, bf16[1024,128]{1,0:T(8,128)(2,1)S(1)} %collective-permute-done.8.refs_0_, bf16[1024,128]{1,0:T(8,128)(2,1)S(1)} %collective-permute-done.9.refs_1_, ...), custom_call_target="tpu_custom_call" | custom-call | tf_op jit(solution)/shard_map/pallas_call | solution.py:306
  74.9 1.4 %shard_map.68 = f32[128,1024]{1,0:T(8,128)} custom-call(s32[8]{0:T(128)S(1)} %compare_select_fusion.2.where, s32[1]{0:T(128)} %bitcast.odd, f32[5,64,128]{2,1,0:T(8,128)S(1)} %convert_add_fusion.refs_0_, f32[5,64,128]{2,1,0:T(8,128)S(1)} %collective-permute-done.17.refs_1_, f32[3,64,128]{2,1,0:T(8,128)S(1)} %convert_add_fusion.1.refs_2_, ...), custom_call_target="tpu_custom_call" | custom-call | tf_op jit(solution)/shard_map/pallas_call | solution.py:298
  (46 shorter events, 4.0 us)
Async XLA Ops:
  0.6 23.0 %collective-permute-start.3 = (bf16[16,64,512]{2,1,0:T(8,128)(2,1)}, bf16[16,64,512]{2,1,0:T(8,128)(2,1)S(1)}, u32[]{:S(2)}, u32[]{:S(2)}) collective-permute-start(bf16[16,64,512]{2,1,0:T(8,128)(2,1)} %tiles.1), channel_id=1, source_target_pairs={{8,16},{16,8},{9,17},{17,9},{10,18},{18,10},{11,19},{19,11},{12,20... | collective-permute-start | bytes 3145736 | tf_op jit(solution)/shard_map/ppermute | solution.py:36
  5.1 1.0 %copy-start.1 = (bf16[128,1024]{1,0:T(8,128)(2,1)S(1)}, bf16[128,1024]{1,0:T(8,128)(2,1)}, u32[]{:S(2)}) copy-start(bf16[128,1024]{1,0:T(8,128)(2,1)} %vectors.1) | copy-start | bytes 786436
  6.8 13.3 %all-to-all-start = ((bf16[8,128,128]{2,1,0:T(8,128)(2,1)}), bf16[8,128,128]{2,1,0:T(8,128)(2,1)S(1)}, u32[]{:S(2)}, u32[]{:S(2)}) async-start(bf16[8,128,128]{2,1,0:T(8,128)(2,1)} %shard_map.59._), calls=%async_computation | async-start | bytes 524288 | tf_op jit(solution)/shard_map/all_to_all | solution.py:355
  13.1 1.2 %copy-start = (bf16[16,64,512]{2,1,0:T(8,128)(2,1)S(1)}, bf16[16,64,512]{2,1,0:T(8,128)(2,1)}, u32[]{:S(2)}) copy-start(bf16[16,64,512]{2,1,0:T(8,128)(2,1)} %tiles.1) | copy-start | bytes 3145732
  14.3 0.7 copy-start.2
  17.4 6.3 %collective-permute-start.2 = (bf16[12,64,512]{2,1,0:T(8,128)(2,1)}, bf16[12,64,512]{2,1,0:T(8,128)(2,1)}, u32[]{:S(2)}, u32[]{:S(2)}) collective-permute-start(bf16[12,64,512]{2,1,0:T(8,128)(2,1)} %get-tuple-element.19), channel_id=1, source_target_pairs={{0,8},{8,0},{16,24},{24,16},{1,9},{9,1},{17,25},{25,17},{2,10},{10... | collective-permute-start | bytes 2359304 | tf_op jit(solution)/shard_map/ppermute | solution.py:31
  17.4 2.8 %collective-permute-start = (s32[8,16]{1,0:T(8,128)S(1)}, s32[8,16]{1,0:T(8,128)S(1)}, u32[]{:S(2)}, u32[]{:S(2)}) collective-permute-start(s32[8,16]{1,0:T(8,128)S(1)} %get-tuple-element.18), channel_id=1, source_target_pairs={{0,8},{8,0},{16,24},{24,16},{1,9},{9,1},{17,25},{25,17},{2,10},{10... | collective-permute-start | bytes 1544 | tf_op jit(solution)/shard_map/ppermute | solution.py:31
  17.9 5.7 %collective-permute-start.1 = (s32[8,16]{1,0:T(8,128)S(1)}, s32[8,16]{1,0:T(8,128)S(1)}, u32[]{:S(2)}, u32[]{:S(2)}) collective-permute-start(s32[8,16]{1,0:T(8,128)S(1)} %get-tuple-element.18), channel_id=1, source_target_pairs={{8,16},{16,8},{9,17},{17,9},{10,18},{18,10},{11,19},{19,11},{12,20... | collective-permute-start | bytes 1544 | tf_op jit(solution)/shard_map/ppermute | solution.py:36
  20.1 5.9 %collective-permute-start.4 = (bf16[1024,128]{1,0:T(8,128)(2,1)S(1)}, bf16[1024,128]{1,0:T(8,128)(2,1)S(1)}, u32[]{:S(2)}, u32[]{:S(2)}) collective-permute-start(bf16[1024,128]{1,0:T(8,128)(2,1)S(1)} %bitcast.10), channel_id=1, source_target_pairs={{0,8},{8,0},{16,24},{24,16},{1,9},{9,1},{17,25},{25,17},{2,10},{10... | collective-permute-start | bytes 786440 | tf_op jit(solution)/shard_map/ppermute | solution.py:31
  20.2 7.7 %collective-permute-start.5 = (bf16[1024,128]{1,0:T(8,128)(2,1)S(1)}, bf16[1024,128]{1,0:T(8,128)(2,1)S(1)}, u32[]{:S(2)}, u32[]{:S(2)}) collective-permute-start(bf16[1024,128]{1,0:T(8,128)(2,1)S(1)} %bitcast.11), channel_id=1, source_target_pairs={{8,16},{16,8},{9,17},{17,9},{10,18},{18,10},{11,19},{19,11},{12,20... | collective-permute-start | bytes 786440 | tf_op jit(solution)/shard_map/ppermute | solution.py:36
  31.2 3.5 %collective-permute-start.6 = (bf16[1536,128]{1,0:T(8,128)(2,1)S(1)}, bf16[1536,128]{1,0:T(8,128)(2,1)S(1)}, u32[]{:S(2)}, u32[]{:S(2)}) collective-permute-start(bf16[1536,128]{1,0:T(8,128)(2,1)S(1)} %get-tuple-element.22), channel_id=1, source_target_pairs={{0,8},{8,0},{16,24},{24,16},{1,9},{9,1},{17,25},{25,17},{2,10},{10... | collective-permute-start | bytes 1179656 | tf_op jit(solution)/shard_map/ppermute | solution.py:31
  31.3 9.4 %collective-permute-start.7 = (bf16[1536,128]{1,0:T(8,128)(2,1)S(1)}, bf16[1536,128]{1,0:T(8,128)(2,1)S(1)}, u32[]{:S(2)}, u32[]{:S(2)}) collective-permute-start(bf16[1536,128]{1,0:T(8,128)(2,1)S(1)} %get-tuple-element.22), channel_id=1, source_target_pairs={{8,16},{16,8},{9,17},{17,9},{10,18},{18,10},{11,19},{19,11},{12,20... | collective-permute-start | bytes 1179656 | tf_op jit(solution)/shard_map/ppermute | solution.py:36
  40.7 7.6 %copy-start.3 = (s32[8]{0:T(128)S(1)}, s32[8]{0:T(128)}, u32[]{:S(2)}) copy-start(s32[8]{0:T(128)} %constant.68.clone) | copy-start | bytes 100
  44.0 6.6 %collective-permute-start.8 = (bf16[1024,128]{1,0:T(8,128)(2,1)S(1)}, bf16[1024,128]{1,0:T(8,128)(2,1)S(1)}, u32[]{:S(2)}, u32[]{:S(2)}) collective-permute-start(bf16[1024,128]{1,0:T(8,128)(2,1)S(1)} %shard_map.63.mine), channel_id=1, source_target_pairs={{0,2},{2,4},{4,6},{6,7},{7,5},{5,3},{3,1},{1,0},{8,10},{10,12},{12... | collective-permute-start | bytes 786440 | tf_op jit(solution)/shard_map/ppermute | solution.py:250
  45.8 7.0 %collective-permute-start.9 = (bf16[1024,128]{1,0:T(8,128)(2,1)S(1)}, bf16[1024,128]{1,0:T(8,128)(2,1)S(1)}, u32[]{:S(2)}, u32[]{:S(2)}) collective-permute-start(bf16[1024,128]{1,0:T(8,128)(2,1)S(1)} %shard_map.63.mine), channel_id=1, source_target_pairs={{0,1},{2,0},{4,2},{6,4},{7,6},{5,7},{3,5},{1,3},{8,9},{10,8},{12,1... | collective-permute-start | bytes 786440 | tf_op jit(solution)/shard_map/ppermute | solution.py:250
  45.9 10.5 %collective-permute-start.10 = (bf16[1024,128]{1,0:T(8,128)(2,1)S(1)}, bf16[1024,128]{1,0:T(8,128)(2,1)S(1)}, u32[]{:S(2)}, u32[]{:S(2)}) collective-permute-start(bf16[1024,128]{1,0:T(8,128)(2,1)S(1)} %shard_map.63.mine), channel_id=1, source_target_pairs={{0,4},{2,6},{4,7},{6,5},{7,3},{5,1},{3,0},{1,2},{8,12},{10,14},{12... | collective-permute-start | bytes 786440 | tf_op jit(solution)/shard_map/ppermute | solution.py:250
  48.2 9.2 %collective-permute-start.11 = (bf16[1024,128]{1,0:T(8,128)(2,1)S(1)}, bf16[1024,128]{1,0:T(8,128)(2,1)S(1)}, u32[]{:S(2)}, u32[]{:S(2)}) collective-permute-start(bf16[1024,128]{1,0:T(8,128)(2,1)S(1)} %shard_map.63.mine), channel_id=1, source_target_pairs={{0,3},{2,1},{4,0},{6,2},{7,4},{5,6},{3,7},{1,5},{8,11},{10,9},{12,... | collective-permute-start | bytes 786440 | tf_op jit(solution)/shard_map/ppermute | solution.py:250
  58.6 3.6 %collective-permute-start.12 = (f32[5,64,128]{2,1,0:T(8,128)S(1)}, f32[5,64,128]{2,1,0:T(8,128)S(1)}, u32[]{:S(2)}, u32[]{:S(2)}) collective-permute-start(f32[5,64,128]{2,1,0:T(8,128)S(1)} %constant_dynamic-slice_fusion.1), channel_id=1, source_target_pairs={{0,8},{8,0},{16,24},{24,16},{1,9},{9,1},{17,25},{25,17},{2,10},{10... | collective-permute-start | bytes 491528 | tf_op jit(solution)/shard_map/ppermute | solution.py:31
  58.7 7.1 %collective-permute-start.15 = (bf16[256,128]{1,0:T(8,128)(2,1)S(1)}, bf16[256,128]{1,0:T(8,128)(2,1)S(1)}, u32[]{:S(2)}, u32[]{:S(2)}) collective-permute-start(bf16[256,128]{1,0:T(8,128)(2,1)S(1)} %get-tuple-element.25._), channel_id=1, source_target_pairs={{0,3},{2,1},{4,0},{6,2},{7,4},{5,6},{3,7},{1,5},{8,11},{10,9},{12,... | collective-permute-start | bytes 196616 | tf_op jit(solution)/shard_map/ppermute | solution.py:250
  60.5 3.5 %collective-permute-start.13 = (bf16[256,128]{1,0:T(8,128)(2,1)S(1)}, bf16[256,128]{1,0:T(8,128)(2,1)S(1)}, u32[]{:S(2)}, u32[]{:S(2)}) collective-permute-start(bf16[256,128]{1,0:T(8,128)(2,1)S(1)} %get-tuple-element.26), channel_id=1, source_target_pairs={{0,2},{2,4},{4,6},{6,7},{7,5},{5,3},{3,1},{1,0},{8,10},{10,12},{12... | collective-permute-start | bytes 196616 | tf_op jit(solution)/shard_map/ppermute | solution.py:250
  62.1 3.7 %collective-permute-start.14 = (bf16[256,128]{1,0:T(8,128)(2,1)S(1)}, bf16[256,128]{1,0:T(8,128)(2,1)S(1)}, u32[]{:S(2)}, u32[]{:S(2)}) collective-permute-start(bf16[256,128]{1,0:T(8,128)(2,1)S(1)} %get-tuple-element.27), channel_id=1, source_target_pairs={{0,1},{2,0},{4,2},{6,4},{7,6},{5,7},{3,5},{1,3},{8,9},{10,8},{12,1... | collective-permute-start | bytes 196616 | tf_op jit(solution)/shard_map/ppermute | solution.py:250
  65.9 2.6 %collective-permute-start.18 = (f32[3,64,128]{2,1,0:T(8,128)S(1)}, f32[3,64,128]{2,1,0:T(8,128)S(1)}, u32[]{:S(2)}, u32[]{:S(2)}) collective-permute-start(f32[3,64,128]{2,1,0:T(8,128)S(1)} %constant_dynamic-slice_fusion), channel_id=1, source_target_pairs={{0,8},{8,0},{16,24},{24,16},{1,9},{9,1},{17,25},{25,17},{2,10},{10... | collective-permute-start | bytes 294920 | tf_op jit(solution)/shard_map/ppermute | solution.py:31
  67.5 4.0 %collective-permute-start.16 = (bf16[5,64,128]{2,1,0:T(8,128)(2,1)S(1)}, bf16[5,64,128]{2,1,0:T(8,128)(2,1)S(1)}, u32[]{:S(2)}, u32[]{:S(2)}) collective-permute-start(bf16[5,64,128]{2,1,0:T(8,128)(2,1)S(1)} %add_convert_fusion), channel_id=1, source_target_pairs={{0,16},{8,24},{16,0},{24,8},{1,17},{9,25},{17,1},{25,9},{2,18},{10... | collective-permute-start | bytes 245768 | tf_op jit(solution)/shard_map/ppermute | solution.py:331
  68.5 4.5 %collective-permute-start.19 = (bf16[3,64,128]{2,1,0:T(8,128)(2,1)S(1)}, bf16[3,64,128]{2,1,0:T(8,128)(2,1)S(1)}, u32[]{:S(2)}, u32[]{:S(2)}) collective-permute-start(bf16[3,64,128]{2,1,0:T(8,128)(2,1)S(1)} %add_convert_fusion.1), channel_id=1, source_target_pairs={{0,16},{8,24},{16,0},{24,8},{1,17},{9,25},{17,1},{25,9},{2,18},{10... | collective-permute-start | bytes 147464 | tf_op jit(solution)/shard_map/ppermute | solution.py:331
  71.6 3.3 %collective-permute-start.17 = (f32[5,64,128]{2,1,0:T(8,128)S(1)}, f32[5,64,128]{2,1,0:T(8,128)S(1)}, u32[]{:S(2)}, u32[]{:S(2)}) collective-permute-start(f32[5,64,128]{2,1,0:T(8,128)S(1)} %convert_add_fusion.refs_0_), channel_id=1, source_target_pairs={{0,8},{8,0},{16,24},{24,16},{1,9},{9,1},{17,25},{25,17},{2,10},{10... | collective-permute-start | bytes 491528 | tf_op jit(solution)/shard_map/ppermute | solution.py:31
  73.0 1.9 %collective-permute-start.20 = (f32[3,64,128]{2,1,0:T(8,128)S(1)}, f32[3,64,128]{2,1,0:T(8,128)S(1)}, u32[]{:S(2)}, u32[]{:S(2)}) collective-permute-start(f32[3,64,128]{2,1,0:T(8,128)S(1)} %convert_add_fusion.1.refs_2_), channel_id=1, source_target_pairs={{0,8},{8,0},{16,24},{24,16},{1,9},{9,1},{17,25},{25,17},{2,10},{10... | collective-permute-start | bytes 294920 | tf_op jit(solution)/shard_map/ppermute | solution.py:31

commit v4 on v3

--- a/solution.py
+++ b/solution.py
@@ -21,6 +21,7 @@
 
 SMEM = pl.BlockSpec(memory_space=pltpu.SMEM)
 VMEM = pl.BlockSpec(memory_space=pltpu.VMEM)
+ANY = pl.BlockSpec(memory_space=pl.ANY)
 
 
 def params(mebibytes):
@@ -77,6 +78,20 @@
         pieces[i] = vectors[:, i * width:(i + 1) * width]
 
 
+def copy_columns(vectors, pieces, done):
+    width = pieces.shape[2]
+    copies = [
+        pltpu.make_async_copy(
+            vectors.at[:, i * width:(i + 1) * width], pieces.at[i], done.at[i]
+        )
+        for i in range(pieces.shape[0])
+    ]
+    for copy in copies:
+        copy.start()
+    for copy in copies:
+        copy.wait()
+
+
 def own_bands(odd, offsets, columns, tiles, _, bands, to_first, columns_out, doubled, slot):
     count = tiles.shape[0]
     sent = to_first.shape[0]
@@ -285,7 +300,7 @@
     own = pl.pallas_call(
         own_blocks,
         out_shape=jax.ShapeDtypeStruct((held + 2, width, width), jnp.float32),
-        in_specs=[VMEM] * 4 + [pl.BlockSpec(memory_space=pl.ANY)],
+        in_specs=[VMEM] * 4 + [ANY],
         out_specs=VMEM,
         compiler_params=params(16),
     )(lefts, early, *blocks[-2:], messages[-1])
@@ -295,21 +310,23 @@
 
     flat = width % 128 == 0
     shape = (lambda n: (n, size * width)) if flat else (lambda n: (size, n, width))
+    far = sum_of_cores(far)
+    rowwise = pl.pallas_call(
+        functools.partial(filtered_rows, len(blocks)),
+        out_shape=jax.ShapeDtypeStruct(shape(share), mine.dtype),
+        in_specs=[SMEM] + [VMEM] * (1 + len(blocks) + len(messages)),
+        out_specs=VMEM,
+        compiler_params=params(16),
+    )(where, mine, *blocks, *messages)
+    own = sum_of_chips(own)
+    far = sum_of_chips(far)
     gram = pl.pallas_call(
         functools.partial(place_blocks, 1.0 / (rows * lax.axis_size("rows"))),
         out_shape=jax.ShapeDtypeStruct(shape(width), jnp.float32),
         in_specs=[SMEM] * 2 + [VMEM] * 4,
         out_specs=VMEM,
         compiler_params=params(16),
-    )(where, (lax.axis_index("rows") & 1)[None], *sum_of_chips(own),
-      *sum_of_chips(sum_of_cores(far)))
-    rowwise = pl.pallas_call(
-        functools.partial(filtered_rows, len(blocks)),
-        out_shape=jax.ShapeDtypeStruct(shape(share), mine.dtype),
-        in_specs=[SMEM] + [VMEM] * (1 + len(blocks) + len(messages)),
-        out_specs=VMEM,
-        compiler_params=params(16),
-    )(where, mine, *blocks, *messages)
+    )(where, (lax.axis_index("rows") & 1)[None], own, with_core(own), far, with_core(far))
     if not flat:
         gram = gram.transpose(1, 0, 2).reshape(width, size * width)
         rowwise = rowwise.transpose(1, 0, 2).reshape(share, size * width)
@@ -326,13 +343,14 @@
 
 def sum_of_chips(sent):
     size = lax.axis_size("rows")
+    total = sent.astype(jnp.float32)
     bit = 2
     while bit < size:
         got = lax.ppermute(sent, "rows", [(i, i ^ bit) for i in range(size)])
         total = sent.astype(jnp.float32) + got.astype(jnp.float32)
         sent = total.astype(jnp.bfloat16)
         bit *= 2
-    return total, with_core(total)
+    return total
 
 
 def per_device(search_vectors, tile_values, block_columns):
@@ -345,11 +363,13 @@
     width = search_vectors.shape[1] // col_parts
     rows = share * col_parts
     second = with_chip(tile_values)
+    lanes = width % 128 == 0
     pieces = pl.pallas_call(
-        split_columns,
+        copy_columns if lanes else split_columns,
         out_shape=jax.ShapeDtypeStruct((col_parts, share, width), search_vectors.dtype),
-        in_specs=[VMEM],
-        out_specs=VMEM,
+        in_specs=[pl.BlockSpec(memory_space=pltpu.HBM) if lanes else VMEM],
+        out_specs=pl.BlockSpec(memory_space=pltpu.HBM) if lanes else VMEM,
+        scratch_shapes=[pltpu.SemaphoreType.DMA((col_parts,))] if lanes else [],
         compiler_params=params(4),
     )(search_vectors)
     columns = lax.all_to_all(pieces, "cols", split_axis=0, concat_axis=0, tiled=True)
@@ -374,7 +394,7 @@
             jax.ShapeDtypeStruct((TILES_REACH, tile, depth), jnp.bfloat16),
             jax.ShapeDtypeStruct((kt, count), jnp.int32),
         ),
-        in_specs=[SMEM, SMEM, VMEM, VMEM, pl.BlockSpec(memory_space=pl.ANY)],
+        in_specs=[SMEM, SMEM, VMEM, VMEM, ANY],
         out_specs=(VMEM,) * 3,
         scratch_shapes=scratch,
         compiler_params=params(16),

time: 76.7 us -> 76.7 us (level)
  no operation moved by 1% of the time
where the time goes in v4:
time: 76.7 us; the launch traced here: 76.3 us
  starting transfers between devices  32.5 us (42%)
  waiting for transfers between devices  22.8 us (30%)
  Pallas kernels  16.4 us (21%)
  local copies, waits for them, and re-layouts  2.9 us (4%)
  between operations  0.89 us (1%)
  other arithmetic  0.83 us (1%)
    ppermute x4, starting transfers between devices, with_chip(): lax.ppermute(value, 'rows', [p for k in odds for p in ((k, k + 1), (k + 1...  13.4 us
    ppermute x7, waiting for transfers between devices, move(): lax.ppermute(value, 'cols', [(order[i], order[(i + by) % size]) for i in...  12.3 us
    ppermute x4, waiting for transfers between devices, with_chip(): lax.ppermute(value, 'rows', [p for k in odds for p in ((k, k + 1), (k + 1...  7.9 us
    ppermute x7, starting transfers between devices, move(): lax.ppermute(value, 'cols', [(order[i], order[(i + by) % size]) for i in...  7.68 us
    all_to_all x1, starting transfers between devices, per_device(): lax.all_to_all(pieces, 'cols', split_axis=0, concat_axis=0, tiled=True)  5.57 us
    ppermute x8, starting transfers between devices, with_core(): lax.ppermute(value, 'rows', [(i, i ^ 1) for i in range(lax.axis_size('row...  4.32 us
    pallas_call x1, Pallas kernels, per_device(): pl.pallas_call(second_stage, out_shape=jax.ShapeDtypeStruct((rows, width)...  3.38 us
    pallas_call x1, Pallas kernels, per_device(): pl.pallas_call(first_stage, out_shape=(jax.ShapeDtypeStruct((rows, width)...  3.28 us
  transfers between devices with their start and end apart: 22, of which 10 were waited for; matrix products, arithmetic and copies ran while one was open for 1% of the time, Pallas kernels for 9%

profile of v4, /device:TPU:1, one launch (start us, length us, event | category | flops | bytes accessed | tf_op | source)
XLA Modules:
  0.0 76.3 jit_solution(2744227701939201902)
XLA Ops:
  0.6 4.5 %collective-permute-start.3 = (bf16[16,64,512]{2,1,0:T(8,128)(2,1)}, bf16[16,64,512]{2,1,0:T(8,128)(2,1)S(1)}, u32[]{:S(2)}, u32[]{:S(2)}) collective-permute-start(bf16[16,64,512]{2,1,0:T(8,128)(2,1)} %tiles.1), channel_id=1, source_target_pairs={{8,16},{16,8},{9,17},{17,9},{10,18},{18,10},{11,19},{19,11},{12,20... | collective-permute-start | bytes 3145736 | tf_op jit(solution)/shard_map/ppermute | solution.py:37
  5.2 0.9 %copy-done.1 = bf16[128,1024]{1,0:T(8,128)(2,1)S(1)} copy-done((bf16[128,1024]{1,0:T(8,128)(2,1)S(1)}, bf16[128,1024]{1,0:T(8,128)(2,1)}, u32[]{:S(2)}) %copy-start.1) | copy-done | bytes 262168
  6.1 0.8 shard_map.59._
  6.9 5.6 %all-to-all-start = ((bf16[8,128,128]{2,1,0:T(8,128)(2,1)}), bf16[8,128,128]{2,1,0:T(8,128)(2,1)S(1)}, u32[]{:S(2)}, u32[]{:S(2)}) async-start(bf16[8,128,128]{2,1,0:T(8,128)(2,1)} %shard_map.59._), calls=%async_computation | async-start | bytes 524288 | tf_op jit(solution)/shard_map/all_to_all | solution.py:375
  13.1 1.2 %copy-done = bf16[16,64,512]{2,1,0:T(8,128)(2,1)S(1)} copy-done((bf16[16,64,512]{2,1,0:T(8,128)(2,1)S(1)}, bf16[16,64,512]{2,1,0:T(8,128)(2,1)}, u32[]{:S(2)}) %copy-start) | copy-done | bytes 1048600
  15.0 2.3 %shard_map.60 = (bf16[4,256,768]{2,1,0:T(8,128)(2,1)S(1)}, bf16[12,64,512]{2,1,0:T(8,128)(2,1)}, s32[8,16]{1,0:T(8,128)S(1)}) custom-call(s32[1]{0:T(128)} %bitcast.odd, s32[8,16]{1,0:T(8,128)S(1)} %subtract_clamp_fusion.2.offsets, s32[8,16]{1,0:T(8,128)S(1)} %bitcast.13, bf16[16,64,512]{2,1,0:T(8,128)(2,1)S(1)} %copy-done, bf16[8,128,128]{2,1,0:T(8,128)(2,1)} %shard_map.59._), custom_call_target="tpu_custom_call" | custom-call | tf_op jit(solution)/shard_map/pallas_call | solution.py:390
  17.9 2.2 %collective-permute-start.1 = (s32[8,16]{1,0:T(8,128)S(1)}, s32[8,16]{1,0:T(8,128)S(1)}, u32[]{:S(2)}, u32[]{:S(2)}) collective-permute-start(s32[8,16]{1,0:T(8,128)S(1)} %get-tuple-element.18), channel_id=1, source_target_pairs={{8,16},{16,8},{9,17},{17,9},{10,18},{18,10},{11,19},{19,11},{12,20... | collective-permute-start | bytes 1544 | tf_op jit(solution)/shard_map/ppermute | solution.py:37
  20.2 3.4 %collective-permute-start.5 = (bf16[1024,128]{1,0:T(8,128)(2,1)S(1)}, bf16[1024,128]{1,0:T(8,128)(2,1)S(1)}, u32[]{:S(2)}, u32[]{:S(2)}) collective-permute-start(bf16[1024,128]{1,0:T(8,128)(2,1)S(1)} %bitcast.11), channel_id=1, source_target_pairs={{8,16},{16,8},{9,17},{17,9},{10,18},{18,10},{11,19},{19,11},{12,20... | collective-permute-start | bytes 786440 | tf_op jit(solution)/shard_map/ppermute | solution.py:37
  23.7 2.4 %shard_map.61.edges = bf16[6,256,768]{2,1,0:T(8,128)(2,1)S(1)} custom-call(s32[1]{0:T(128)} %bitcast.odd, s32[8,16]{1,0:T(8,128)S(1)} %subtract_clamp_fusion.1.at_first, s32[8,16]{1,0:T(8,128)S(1)} %subtract_clamp_fusion.at_second, bf16[12,64,512]{2,1,0:T(8,128)(2,1)} %collective-permute-done.2.first, bf16[16,64,512]{2,1,0:T(8,128)(2,1)S(1)} %collective-permute-done.3.second), custom_call_target="tpu_custom_call" | custom-call | tf_op jit(solution)/shard_map/pallas_call | solution.py:405
  26.0 1.9 %collective-permute-done.5.x_second = bf16[1024,128]{1,0:T(8,128)(2,1)S(1)} collective-permute-done((bf16[1024,128]{1,0:T(8,128)(2,1)S(1)}, bf16[1024,128]{1,0:T(8,128)(2,1)S(1)}, u32[]{:S(2)}, u32[]{:S(2)}) %collective-permute-start.5) | collective-permute-done | bytes 262176 | tf_op jit(solution)/shard_map/ppermute | solution.py:37
  27.9 3.3 %shard_map.62 = (f32[1024,128]{1,0:T(8,128)S(1)}, f32[1536,128]{1,0:T(8,128)S(1)}, bf16[1536,128]{1,0:T(8,128)(2,1)S(1)}) custom-call(s32[1]{0:T(128)} %bitcast.odd, bf16[4,256,768]{2,1,0:T(8,128)(2,1)S(1)} %get-tuple-element.17.own, bf16[6,256,768]{2,1,0:T(8,128)(2,1)S(1)} %shard_map.61.edges, bf16[1024,128]{1,0:T(8,128)(2,1)S(1)} %collective-permute-done.4.x_first, ...), custom_call_target="tpu_custom_call" | custom-call | tf_op jit(solution)/shard_map/pallas_call | solution.py:428
  31.3 3.4 %collective-permute-start.7 = (bf16[1536,128]{1,0:T(8,128)(2,1)S(1)}, bf16[1536,128]{1,0:T(8,128)(2,1)S(1)}, u32[]{:S(2)}, u32[]{:S(2)}) collective-permute-start(bf16[1536,128]{1,0:T(8,128)(2,1)S(1)} %get-tuple-element.22), channel_id=1, source_target_pairs={{8,16},{16,8},{9,17},{17,9},{10,18},{18,10},{11,19},{19,11},{12,20... | collective-permute-start | bytes 1179656 | tf_op jit(solution)/shard_map/ppermute | solution.py:37
  34.7 6.0 %collective-permute-done.7.got_second = bf16[1536,128]{1,0:T(8,128)(2,1)S(1)} collective-permute-done((bf16[1536,128]{1,0:T(8,128)(2,1)S(1)}, bf16[1536,128]{1,0:T(8,128)(2,1)S(1)}, u32[]{:S(2)}, u32[]{:S(2)}) %collective-permute-start.7) | collective-permute-done | bytes 393248 | tf_op jit(solution)/shard_map/ppermute | solution.py:37
  40.7 3.4 %shard_map.63.mine = bf16[1024,128]{1,0:T(8,128)(2,1)S(1)} custom-call(s32[1]{0:T(128)} %bitcast.odd, bf16[4,256,768]{2,1,0:T(8,128)(2,1)S(1)} %get-tuple-element.17.own, bf16[6,256,768]{2,1,0:T(8,128)(2,1)S(1)} %shard_map.61.edges, f32[1024,128]{1,0:T(8,128)S(1)} %get-tuple-element.20.now, f32[1536,128]{1,0:T(8,128)S(1)} %get-tuple-element.21.last, ...), custom_call_target="tpu_custom_call" | custom-call | tf_op jit(solution)/shard_map/pallas_call | solution.py:442
  44.1 1.8 %collective-permute-start.8 = (bf16[1024,128]{1,0:T(8,128)(2,1)S(1)}, bf16[1024,128]{1,0:T(8,128)(2,1)S(1)}, u32[]{:S(2)}, u32[]{:S(2)}) collective-permute-start(bf16[1024,128]{1,0:T(8,128)(2,1)S(1)} %shard_map.63.mine), channel_id=1, source_target_pairs={{0,2},{2,4},{4,6},{6,7},{7,5},{5,3},{3,1},{1,0},{8,10},{10,12},{12... | collective-permute-start | bytes 786440 | tf_op jit(solution)/shard_map/ppermute | solution.py:265
  45.9 2.3 %collective-permute-start.10 = (bf16[1024,128]{1,0:T(8,128)(2,1)S(1)}, bf16[1024,128]{1,0:T(8,128)(2,1)S(1)}, u32[]{:S(2)}, u32[]{:S(2)}) collective-permute-start(bf16[1024,128]{1,0:T(8,128)(2,1)S(1)} %shard_map.63.mine), channel_id=1, source_target_pairs={{0,4},{2,6},{4,7},{6,5},{7,3},{5,1},{3,0},{1,2},{8,12},{10,14},{12... | collective-permute-start | bytes 786440 | tf_op jit(solution)/shard_map/ppermute | solution.py:265
  48.3 2.4 %collective-permute-done.8.refs_0_ = bf16[1024,128]{1,0:T(8,128)(2,1)S(1)} collective-permute-done((bf16[1024,128]{1,0:T(8,128)(2,1)S(1)}, bf16[1024,128]{1,0:T(8,128)(2,1)S(1)}, u32[]{:S(2)}, u32[]{:S(2)}) %collective-permute-start.8) | collective-permute-done | bytes 262176 | tf_op jit(solution)/shard_map/ppermute | solution.py:265
  50.7 2.1 %collective-permute-done.9.refs_1_ = bf16[1024,128]{1,0:T(8,128)(2,1)S(1)} collective-permute-done((bf16[1024,128]{1,0:T(8,128)(2,1)S(1)}, bf16[1024,128]{1,0:T(8,128)(2,1)S(1)}, u32[]{:S(2)}, u32[]{:S(2)}) %collective-permute-start.9) | collective-permute-done | bytes 262176 | tf_op jit(solution)/shard_map/ppermute | solution.py:265
  53.2 3.2 %collective-permute-done.10.back.refs_2_ = bf16[1024,128]{1,0:T(8,128)(2,1)S(1)} collective-permute-done((bf16[1024,128]{1,0:T(8,128)(2,1)S(1)}, bf16[1024,128]{1,0:T(8,128)(2,1)S(1)}, u32[]{:S(2)}, u32[]{:S(2)}) %collective-permute-start.10) | collective-permute-done | bytes 262176 | tf_op jit(solution)/shard_map/ppermute | solution.py:265
  56.5 1.0 %collective-permute-done.11.front.refs_3_ = bf16[1024,128]{1,0:T(8,128)(2,1)S(1)} collective-permute-done((bf16[1024,128]{1,0:T(8,128)(2,1)S(1)}, bf16[1024,128]{1,0:T(8,128)(2,1)S(1)}, u32[]{:S(2)}, u32[]{:S(2)}) %collective-permute-start.11) | collective-permute-done | bytes 262176 | tf_op jit(solution)/shard_map/ppermute | solution.py:265
  57.4 0.9 %shard_map.65 = (bf16[256,128]{1,0:T(8,128)(2,1)S(1)}, bf16[256,128]{1,0:T(8,128)(2,1)S(1)}, bf16[256,128]{1,0:T(8,128)(2,1)S(1)}) custom-call(s32[8]{0:T(128)S(1)} %compare_select_fusion.2.where, bf16[3,128,1024]{2,1,0:T(8,128)(2,1)S(1)} %get-tuple-element.23.lefts, bf16[1024,128]{1,0:T(8,128)(2,1)S(1)} %collective-permute-done.10.back.refs_2_, ...), custom_call_target="tpu_custom_call" | custom-call | tf_op jit(solution)/shard_map/pallas_call | solution.py:293
  58.7 1.8 %collective-permute-start.15 = (bf16[256,128]{1,0:T(8,128)(2,1)S(1)}, bf16[256,128]{1,0:T(8,128)(2,1)S(1)}, u32[]{:S(2)}, u32[]{:S(2)}) collective-permute-start(bf16[256,128]{1,0:T(8,128)(2,1)S(1)} %get-tuple-element.25._), channel_id=1, source_target_pairs={{0,3},{2,1},{4,0},{6,2},{7,4},{5,6},{3,7},{1,5},{8,11},{10,9},{12,... | collective-permute-start | bytes 196616 | tf_op jit(solution)/shard_map/ppermute | solution.py:265
  60.5 1.7 %collective-permute-start.13 = (bf16[256,128]{1,0:T(8,128)(2,1)S(1)}, bf16[256,128]{1,0:T(8,128)(2,1)S(1)}, u32[]{:S(2)}, u32[]{:S(2)}) collective-permute-start(bf16[256,128]{1,0:T(8,128)(2,1)S(1)} %get-tuple-element.26), channel_id=1, source_target_pairs={{0,2},{2,4},{4,6},{6,7},{7,5},{5,3},{3,1},{1,0},{8,10},{10,12},{12... | collective-permute-start | bytes 196616 | tf_op jit(solution)/shard_map/ppermute | solution.py:265
  62.2 1.8 %collective-permute-done.13.refs_4_ = bf16[256,128]{1,0:T(8,128)(2,1)S(1)} collective-permute-done((bf16[256,128]{1,0:T(8,128)(2,1)S(1)}, bf16[256,128]{1,0:T(8,128)(2,1)S(1)}, u32[]{:S(2)}, u32[]{:S(2)}) %collective-permute-start.13) | collective-permute-done | bytes 65568 | tf_op jit(solution)/shard_map/ppermute | solution.py:265
  64.0 1.9 %collective-permute-done.14.refs_5_ = bf16[256,128]{1,0:T(8,128)(2,1)S(1)} collective-permute-done((bf16[256,128]{1,0:T(8,128)(2,1)S(1)}, bf16[256,128]{1,0:T(8,128)(2,1)S(1)}, u32[]{:S(2)}, u32[]{:S(2)}) %collective-permute-start.14) | collective-permute-done | bytes 65568 | tf_op jit(solution)/shard_map/ppermute | solution.py:265
  65.9 1.7 %collective-permute-start.18 = (f32[3,64,128]{2,1,0:T(8,128)S(1)}, f32[3,64,128]{2,1,0:T(8,128)S(1)}, u32[]{:S(2)}, u32[]{:S(2)}) collective-permute-start(f32[3,64,128]{2,1,0:T(8,128)S(1)} %constant_dynamic-slice_fusion), channel_id=1, source_target_pairs={{0,8},{8,0},{16,24},{24,16},{1,9},{9,1},{17,25},{25,17},{2,10},{10... | collective-permute-start | bytes 294920 | tf_op jit(solution)/shard_map/ppermute | solution.py:32
  67.6 0.7 collective-permute-start.16
  68.5 0.8 %collective-permute-start.19 = (bf16[3,64,128]{2,1,0:T(8,128)(2,1)S(1)}, bf16[3,64,128]{2,1,0:T(8,128)(2,1)S(1)}, u32[]{:S(2)}, u32[]{:S(2)}) collective-permute-start(bf16[3,64,128]{2,1,0:T(8,128)(2,1)S(1)} %add_convert_fusion.1), channel_id=1, source_target_pairs={{0,16},{8,24},{16,0},{24,8},{1,17},{9,25},{17,1},{25,9},{2,18},{10... | collective-permute-start | bytes 147464 | tf_op jit(solution)/shard_map/ppermute | solution.py:349
  69.3 2.3 %collective-permute-done.16 = bf16[5,64,128]{2,1,0:T(8,128)(2,1)S(1)} collective-permute-done((bf16[5,64,128]{2,1,0:T(8,128)(2,1)S(1)}, bf16[5,64,128]{2,1,0:T(8,128)(2,1)S(1)}, u32[]{:S(2)}, u32[]{:S(2)}) %collective-permute-start.16) | collective-permute-done | bytes 81952 | tf_op jit(solution)/shard_map/ppermute | solution.py:349
  71.6 1.4 %collective-permute-start.17 = (f32[5,64,128]{2,1,0:T(8,128)S(1)}, f32[5,64,128]{2,1,0:T(8,128)S(1)}, u32[]{:S(2)}, u32[]{:S(2)}) collective-permute-start(f32[5,64,128]{2,1,0:T(8,128)S(1)} %convert_add_fusion.refs_0_), channel_id=1, source_target_pairs={{0,8},{8,0},{16,24},{24,16},{1,9},{9,1},{17,25},{25,17},{2,10},{10... | collective-permute-start | bytes 491528 | tf_op jit(solution)/shard_map/ppermute | solution.py:32
  73.6 1.3 %shard_map.67 = bf16[128,1024]{1,0:T(8,128)(2,1)} custom-call(s32[8]{0:T(128)S(1)} %compare_select_fusion.2.where, bf16[1024,128]{1,0:T(8,128)(2,1)S(1)} %shard_map.63.mine, bf16[1024,128]{1,0:T(8,128)(2,1)S(1)} %collective-permute-done.8.refs_0_, bf16[1024,128]{1,0:T(8,128)(2,1)S(1)} %collective-permute-done.9.refs_1_, ...), custom_call_target="tpu_custom_call" | custom-call | tf_op jit(solution)/shard_map/pallas_call | solution.py:314
  74.9 1.4 %shard_map.68 = f32[128,1024]{1,0:T(8,128)} custom-call(s32[8]{0:T(128)S(1)} %compare_select_fusion.2.where, s32[1]{0:T(128)} %bitcast.odd, f32[5,64,128]{2,1,0:T(8,128)S(1)} %convert_add_fusion.refs_0_, f32[5,64,128]{2,1,0:T(8,128)S(1)} %collective-permute-done.17.refs_1_, f32[3,64,128]{2,1,0:T(8,128)S(1)} %convert_add_fusion.1.refs_2_, ...), custom_call_target="tpu_custom_call" | custom-call | tf_op jit(solution)/shard_map/pallas_call | solution.py:323
  (46 shorter events, 4.0 us)
Async XLA Ops:
  0.6 23.0 %collective-permute-start.3 = (bf16[16,64,512]{2,1,0:T(8,128)(2,1)}, bf16[16,64,512]{2,1,0:T(8,128)(2,1)S(1)}, u32[]{:S(2)}, u32[]{:S(2)}) collective-permute-start(bf16[16,64,512]{2,1,0:T(8,128)(2,1)} %tiles.1), channel_id=1, source_target_pairs={{8,16},{16,8},{9,17},{17,9},{10,18},{18,10},{11,19},{19,11},{12,20... | collective-permute-start | bytes 3145736 | tf_op jit(solution)/shard_map/ppermute | solution.py:37
  5.1 1.0 %copy-start.1 = (bf16[128,1024]{1,0:T(8,128)(2,1)S(1)}, bf16[128,1024]{1,0:T(8,128)(2,1)}, u32[]{:S(2)}) copy-start(bf16[128,1024]{1,0:T(8,128)(2,1)} %vectors.1) | copy-start | bytes 786436
  6.9 13.3 %all-to-all-start = ((bf16[8,128,128]{2,1,0:T(8,128)(2,1)}), bf16[8,128,128]{2,1,0:T(8,128)(2,1)S(1)}, u32[]{:S(2)}, u32[]{:S(2)}) async-start(bf16[8,128,128]{2,1,0:T(8,128)(2,1)} %shard_map.59._), calls=%async_computation | async-start | bytes 524288 | tf_op jit(solution)/shard_map/all_to_all | solution.py:375
  13.1 1.2 %copy-start = (bf16[16,64,512]{2,1,0:T(8,128)(2,1)S(1)}, bf16[16,64,512]{2,1,0:T(8,128)(2,1)}, u32[]{:S(2)}) copy-start(bf16[16,64,512]{2,1,0:T(8,128)(2,1)} %tiles.1) | copy-start | bytes 3145732
  14.4 0.7 copy-start.2
  17.4 6.3 %collective-permute-start.2 = (bf16[12,64,512]{2,1,0:T(8,128)(2,1)}, bf16[12,64,512]{2,1,0:T(8,128)(2,1)}, u32[]{:S(2)}, u32[]{:S(2)}) collective-permute-start(bf16[12,64,512]{2,1,0:T(8,128)(2,1)} %get-tuple-element.19), channel_id=1, source_target_pairs={{0,8},{8,0},{16,24},{24,16},{1,9},{9,1},{17,25},{25,17},{2,10},{10... | collective-permute-start | bytes 2359304 | tf_op jit(solution)/shard_map/ppermute | solution.py:32
  17.4 2.8 %collective-permute-start = (s32[8,16]{1,0:T(8,128)S(1)}, s32[8,16]{1,0:T(8,128)S(1)}, u32[]{:S(2)}, u32[]{:S(2)}) collective-permute-start(s32[8,16]{1,0:T(8,128)S(1)} %get-tuple-element.18), channel_id=1, source_target_pairs={{0,8},{8,0},{16,24},{24,16},{1,9},{9,1},{17,25},{25,17},{2,10},{10... | collective-permute-start | bytes 1544 | tf_op jit(solution)/shard_map/ppermute | solution.py:32
  17.9 5.7 %collective-permute-start.1 = (s32[8,16]{1,0:T(8,128)S(1)}, s32[8,16]{1,0:T(8,128)S(1)}, u32[]{:S(2)}, u32[]{:S(2)}) collective-permute-start(s32[8,16]{1,0:T(8,128)S(1)} %get-tuple-element.18), channel_id=1, source_target_pairs={{8,16},{16,8},{9,17},{17,9},{10,18},{18,10},{11,19},{19,11},{12,20... | collective-permute-start | bytes 1544 | tf_op jit(solution)/shard_map/ppermute | solution.py:37
  20.1 5.9 %collective-permute-start.4 = (bf16[1024,128]{1,0:T(8,128)(2,1)S(1)}, bf16[1024,128]{1,0:T(8,128)(2,1)S(1)}, u32[]{:S(2)}, u32[]{:S(2)}) collective-permute-start(bf16[1024,128]{1,0:T(8,128)(2,1)S(1)} %bitcast.10), channel_id=1, source_target_pairs={{0,8},{8,0},{16,24},{24,16},{1,9},{9,1},{17,25},{25,17},{2,10},{10... | collective-permute-start | bytes 786440 | tf_op jit(solution)/shard_map/ppermute | solution.py:32
  20.2 7.7 %collective-permute-start.5 = (bf16[1024,128]{1,0:T(8,128)(2,1)S(1)}, bf16[1024,128]{1,0:T(8,128)(2,1)S(1)}, u32[]{:S(2)}, u32[]{:S(2)}) collective-permute-start(bf16[1024,128]{1,0:T(8,128)(2,1)S(1)} %bitcast.11), channel_id=1, source_target_pairs={{8,16},{16,8},{9,17},{17,9},{10,18},{18,10},{11,19},{19,11},{12,20... | collective-permute-start | bytes 786440 | tf_op jit(solution)/shard_map/ppermute | solution.py:37
  31.2 3.5 %collective-permute-start.6 = (bf16[1536,128]{1,0:T(8,128)(2,1)S(1)}, bf16[1536,128]{1,0:T(8,128)(2,1)S(1)}, u32[]{:S(2)}, u32[]{:S(2)}) collective-permute-start(bf16[1536,128]{1,0:T(8,128)(2,1)S(1)} %get-tuple-element.22), channel_id=1, source_target_pairs={{0,8},{8,0},{16,24},{24,16},{1,9},{9,1},{17,25},{25,17},{2,10},{10... | collective-permute-start | bytes 1179656 | tf_op jit(solution)/shard_map/ppermute | solution.py:32
  31.3 9.4 %collective-permute-start.7 = (bf16[1536,128]{1,0:T(8,128)(2,1)S(1)}, bf16[1536,128]{1,0:T(8,128)(2,1)S(1)}, u32[]{:S(2)}, u32[]{:S(2)}) collective-permute-start(bf16[1536,128]{1,0:T(8,128)(2,1)S(1)} %get-tuple-element.22), channel_id=1, source_target_pairs={{8,16},{16,8},{9,17},{17,9},{10,18},{18,10},{11,19},{19,11},{12,20... | collective-permute-start | bytes 1179656 | tf_op jit(solution)/shard_map/ppermute | solution.py:37
  40.7 7.6 %copy-start.3 = (s32[8]{0:T(128)S(1)}, s32[8]{0:T(128)}, u32[]{:S(2)}) copy-start(s32[8]{0:T(128)} %constant.68.clone) | copy-start | bytes 100
  44.1 6.6 %collective-permute-start.8 = (bf16[1024,128]{1,0:T(8,128)(2,1)S(1)}, bf16[1024,128]{1,0:T(8,128)(2,1)S(1)}, u32[]{:S(2)}, u32[]{:S(2)}) collective-permute-start(bf16[1024,128]{1,0:T(8,128)(2,1)S(1)} %shard_map.63.mine), channel_id=1, source_target_pairs={{0,2},{2,4},{4,6},{6,7},{7,5},{5,3},{3,1},{1,0},{8,10},{10,12},{12... | collective-permute-start | bytes 786440 | tf_op jit(solution)/shard_map/ppermute | solution.py:265
  45.9 7.0 %collective-permute-start.9 = (bf16[1024,128]{1,0:T(8,128)(2,1)S(1)}, bf16[1024,128]{1,0:T(8,128)(2,1)S(1)}, u32[]{:S(2)}, u32[]{:S(2)}) collective-permute-start(bf16[1024,128]{1,0:T(8,128)(2,1)S(1)} %shard_map.63.mine), channel_id=1, source_target_pairs={{0,1},{2,0},{4,2},{6,4},{7,6},{5,7},{3,5},{1,3},{8,9},{10,8},{12,1... | collective-permute-start | bytes 786440 | tf_op jit(solution)/shard_map/ppermute | solution.py:265
  45.9 10.5 %collective-permute-start.10 = (bf16[1024,128]{1,0:T(8,128)(2,1)S(1)}, bf16[1024,128]{1,0:T(8,128)(2,1)S(1)}, u32[]{:S(2)}, u32[]{:S(2)}) collective-permute-start(bf16[1024,128]{1,0:T(8,128)(2,1)S(1)} %shard_map.63.mine), channel_id=1, source_target_pairs={{0,4},{2,6},{4,7},{6,5},{7,3},{5,1},{3,0},{1,2},{8,12},{10,14},{12... | collective-permute-start | bytes 786440 | tf_op jit(solution)/shard_map/ppermute | solution.py:265
  48.2 9.2 %collective-permute-start.11 = (bf16[1024,128]{1,0:T(8,128)(2,1)S(1)}, bf16[1024,128]{1,0:T(8,128)(2,1)S(1)}, u32[]{:S(2)}, u32[]{:S(2)}) collective-permute-start(bf16[1024,128]{1,0:T(8,128)(2,1)S(1)} %shard_map.63.mine), channel_id=1, source_target_pairs={{0,3},{2,1},{4,0},{6,2},{7,4},{5,6},{3,7},{1,5},{8,11},{10,9},{12,... | collective-permute-start | bytes 786440 | tf_op jit(solution)/shard_map/ppermute | solution.py:265
  58.6 3.6 %collective-permute-start.12 = (f32[5,64,128]{2,1,0:T(8,128)S(1)}, f32[5,64,128]{2,1,0:T(8,128)S(1)}, u32[]{:S(2)}, u32[]{:S(2)}) collective-permute-start(f32[5,64,128]{2,1,0:T(8,128)S(1)} %constant_dynamic-slice_fusion.1), channel_id=1, source_target_pairs={{0,8},{8,0},{16,24},{24,16},{1,9},{9,1},{17,25},{25,17},{2,10},{10... | collective-permute-start | bytes 491528 | tf_op jit(solution)/shard_map/ppermute | solution.py:32
  58.7 7.1 %collective-permute-start.15 = (bf16[256,128]{1,0:T(8,128)(2,1)S(1)}, bf16[256,128]{1,0:T(8,128)(2,1)S(1)}, u32[]{:S(2)}, u32[]{:S(2)}) collective-permute-start(bf16[256,128]{1,0:T(8,128)(2,1)S(1)} %get-tuple-element.25._), channel_id=1, source_target_pairs={{0,3},{2,1},{4,0},{6,2},{7,4},{5,6},{3,7},{1,5},{8,11},{10,9},{12,... | collective-permute-start | bytes 196616 | tf_op jit(solution)/shard_map/ppermute | solution.py:265
  60.5 3.5 %collective-permute-start.13 = (bf16[256,128]{1,0:T(8,128)(2,1)S(1)}, bf16[256,128]{1,0:T(8,128)(2,1)S(1)}, u32[]{:S(2)}, u32[]{:S(2)}) collective-permute-start(bf16[256,128]{1,0:T(8,128)(2,1)S(1)} %get-tuple-element.26), channel_id=1, source_target_pairs={{0,2},{2,4},{4,6},{6,7},{7,5},{5,3},{3,1},{1,0},{8,10},{10,12},{12... | collective-permute-start | bytes 196616 | tf_op jit(solution)/shard_map/ppermute | solution.py:265
  62.2 3.7 %collective-permute-start.14 = (bf16[256,128]{1,0:T(8,128)(2,1)S(1)}, bf16[256,128]{1,0:T(8,128)(2,1)S(1)}, u32[]{:S(2)}, u32[]{:S(2)}) collective-permute-start(bf16[256,128]{1,0:T(8,128)(2,1)S(1)} %get-tuple-element.27), channel_id=1, source_target_pairs={{0,1},{2,0},{4,2},{6,4},{7,6},{5,7},{3,5},{1,3},{8,9},{10,8},{12,1... | collective-permute-start | bytes 196616 | tf_op jit(solution)/shard_map/ppermute | solution.py:265
  65.9 2.6 %collective-permute-start.18 = (f32[3,64,128]{2,1,0:T(8,128)S(1)}, f32[3,64,128]{2,1,0:T(8,128)S(1)}, u32[]{:S(2)}, u32[]{:S(2)}) collective-permute-start(f32[3,64,128]{2,1,0:T(8,128)S(1)} %constant_dynamic-slice_fusion), channel_id=1, source_target_pairs={{0,8},{8,0},{16,24},{24,16},{1,9},{9,1},{17,25},{25,17},{2,10},{10... | collective-permute-start | bytes 294920 | tf_op jit(solution)/shard_map/ppermute | solution.py:32
  67.6 4.0 %collective-permute-start.16 = (bf16[5,64,128]{2,1,0:T(8,128)(2,1)S(1)}, bf16[5,64,128]{2,1,0:T(8,128)(2,1)S(1)}, u32[]{:S(2)}, u32[]{:S(2)}) collective-permute-start(bf16[5,64,128]{2,1,0:T(8,128)(2,1)S(1)} %add_convert_fusion), channel_id=1, source_target_pairs={{0,16},{8,24},{16,0},{24,8},{1,17},{9,25},{17,1},{25,9},{2,18},{10... | collective-permute-start | bytes 245768 | tf_op jit(solution)/shard_map/ppermute | solution.py:349
  68.5 4.5 %collective-permute-start.19 = (bf16[3,64,128]{2,1,0:T(8,128)(2,1)S(1)}, bf16[3,64,128]{2,1,0:T(8,128)(2,1)S(1)}, u32[]{:S(2)}, u32[]{:S(2)}) collective-permute-start(bf16[3,64,128]{2,1,0:T(8,128)(2,1)S(1)} %add_convert_fusion.1), channel_id=1, source_target_pairs={{0,16},{8,24},{16,0},{24,8},{1,17},{9,25},{17,1},{25,9},{2,18},{10... | collective-permute-start | bytes 147464 | tf_op jit(solution)/shard_map/ppermute | solution.py:349
  71.6 3.3 %collective-permute-start.17 = (f32[5,64,128]{2,1,0:T(8,128)S(1)}, f32[5,64,128]{2,1,0:T(8,128)S(1)}, u32[]{:S(2)}, u32[]{:S(2)}) collective-permute-start(f32[5,64,128]{2,1,0:T(8,128)S(1)} %convert_add_fusion.refs_0_), channel_id=1, source_target_pairs={{0,8},{8,0},{16,24},{24,16},{1,9},{9,1},{17,25},{25,17},{2,10},{10... | collective-permute-start | bytes 491528 | tf_op jit(solution)/shard_map/ppermute | solution.py:32
  73.0 1.9 %collective-permute-start.20 = (f32[3,64,128]{2,1,0:T(8,128)S(1)}, f32[3,64,128]{2,1,0:T(8,128)S(1)}, u32[]{:S(2)}, u32[]{:S(2)}) collective-permute-start(f32[3,64,128]{2,1,0:T(8,128)S(1)} %convert_add_fusion.1.refs_2_), channel_id=1, source_target_pairs={{0,8},{8,0},{16,24},{24,16},{1,9},{9,1},{17,25},{25,17},{2,10},{10... | collective-permute-start | bytes 294920 | tf_op jit(solution)/shard_map/ppermute | solution.py:32

commit v5 on v4

--- a/solution.py
+++ b/solution.py
@@ -189,37 +189,41 @@
     return (group,)
 
 
-def early_gram(mine, *refs):
-    *blocks, partial, lefts = refs
+def early_gram(where, mine, back, front, partial, lefts, message):
+    width = lefts.shape[1]
+    share = message.shape[0] - width
+    far_front = front[...]
     left = mine[...].T
+    left_back = back[...].T
     lefts[0] = left
-    for t, ref in enumerate((mine, *blocks)):
-        block = ref[...]
-        if t:
-            lefts[t] = block.T
-        partial[t] = dot(left, block)
-
-
-def far_messages(where, lefts, back, front, *messages):
+    lefts[1] = left_back
+    lefts[2] = far_front.T
+    message[:width] = dot(left_back, far_front).astype(message.dtype)
+    message[width:] = front[pl.ds(pl.multiple_of(where[1] * share, share), share)]
+    partial[0] = dot(left, mine[...])
+    partial[1] = dot(left, back[...])
+    partial[2] = dot(left, far_front)
+
+
+def near_messages(where, lefts, back, front, *refs):
+    number = len(refs) // 2
+    near, messages = refs[:number], refs[number:]
     width = lefts.shape[1]
     share = messages[0].shape[0] - width
-    reach = lefts.shape[0] // 2 + 1
-    far_back, far_front = back[...], front[...]
-    made = []
-    for t in range(1, reach):
-        made.append((dot(lefts[2 * t], far_back), back, where[2 * t]))
-        made.append((dot(lefts[2 * t - 1], far_front), front, where[2 * t - 1]))
-    made.append((dot(far_back.T, far_front), front, where[2 * reach - 1]))
-    for message, (block, source, device) in zip(messages, made):
-        message[:width] = block.astype(message.dtype)
-        message[width:] = source[pl.ds(pl.multiple_of(device * share, share), share)]
-
-
-def own_blocks(lefts, early, back, front, _, partial):
-    held = early.shape[0]
-    partial[:held] = early[...]
-    partial[held] = dot(lefts[0], back[...])
-    partial[held + 1] = dot(lefts[0], front[...])
+    for t in range(number):
+        ahead = t % 2 == 0
+        block = dot(lefts[1 if ahead else 2], near[t ^ 1][...])
+        device = where[3 + (t ^ 1)]
+        source = back if ahead else front
+        messages[t][:width] = block.T.astype(messages[t].dtype)
+        messages[t][width:] = source[pl.ds(pl.multiple_of(device * share, share), share)]
+
+
+def own_blocks(lefts, early, *refs):
+    *near, _, partial = refs
+    partial[:3] = early[...]
+    for t, block in enumerate(near):
+        partial[3 + t] = dot(lefts[0], block[...])
 
 
 def place_blocks(scale, where, odd, *refs):
@@ -266,45 +270,45 @@
             value, "cols", [(order[i], order[(i + by) % size]) for i in range(size)]
         )
 
-    fetched = {by: move(mine, by) for t in range(reach, 0, -1) for by in (t, -t)}
-    blocks, steps = [], [0]
-    for t in range(1, reach + 1):
-        blocks += [fetched[t], fetched[-t]]
-        steps += [-t, t]
-    sends = [by for t in range(1, reach) for by in (t, -t)] + [-reach]
+    distances = [reach] + list(range(1, reach))
+    fetched = {by: move(mine, by) for t in distances for by in (t, -t)}
+    blocks = [fetched[by] for t in distances for by in (t, -t)]
+    sends = [-reach] + [by for t in range(1, reach) for by in (t, -t)]
+    steps = [0] + [by for t in distances for by in (-t, t)]
     steps += [-(by + reach) if by > 0 else reach - by for by in sends]
 
     place = jnp.where(device % 2 == 0, device // 2, size - 1 - device // 2)
     where = (place + jnp.array(steps, jnp.int32)) % size
     where = jnp.where(where < size // 2, 2 * where, 2 * (size - 1 - where) + 1)
 
-    held = 2 * reach - 1
-    early, lefts = pl.pallas_call(
+    message = jax.ShapeDtypeStruct((width + share, width), mine.dtype)
+    early, lefts, far_message = pl.pallas_call(
         early_gram,
         out_shape=(
-            jax.ShapeDtypeStruct((held, width, width), jnp.float32),
-            jax.ShapeDtypeStruct((held, width, rows), mine.dtype),
+            jax.ShapeDtypeStruct((3, width, width), jnp.float32),
+            jax.ShapeDtypeStruct((3, width, rows), mine.dtype),
+            message,
         ),
-        in_specs=[VMEM] * held,
-        out_specs=(VMEM, VMEM),
-        compiler_params=params(16),
-    )(mine, *blocks[:-2])
-    message = jax.ShapeDtypeStruct((width + share, width), mine.dtype)
+        in_specs=[SMEM] + [VMEM] * 3,
+        out_specs=(VMEM,) * 3,
+        compiler_params=params(16),
+    )(where, mine, *blocks[:2])
+    near = blocks[2:]
     messages = pl.pallas_call(
-        far_messages,
-        out_shape=(message,) * len(sends),
-        in_specs=[SMEM] + [VMEM] * 3,
-        out_specs=(VMEM,) * len(sends),
-        compiler_params=params(16),
-    )(where, lefts, *blocks[-2:])
+        near_messages,
+        out_shape=(message,) * len(near),
+        in_specs=[SMEM] + [VMEM] * (3 + len(near)),
+        out_specs=(VMEM,) * len(near),
+        compiler_params=params(16),
+    )(where, lefts, *blocks)
     own = pl.pallas_call(
         own_blocks,
-        out_shape=jax.ShapeDtypeStruct((held + 2, width, width), jnp.float32),
-        in_specs=[VMEM] * 4 + [ANY],
+        out_shape=jax.ShapeDtypeStruct((1 + len(blocks), width, width), jnp.float32),
+        in_specs=[VMEM] * (2 + len(near)) + [ANY],
         out_specs=VMEM,
         compiler_params=params(16),
-    )(lefts, early, *blocks[-2:], messages[-1])
-    messages = [move(value, by) for value, by in zip(messages, sends)]
+    )(lefts, early, *near, messages[-1])
+    messages = [move(value, by) for value, by in zip((far_message, *messages), sends)]
     own, messages = lax.optimization_barrier((sum_of_cores(own), messages))
     far = jnp.stack([message[:width] for message in messages]).astype(jnp.float32)
 

time: 76.7 us -> 78.2 us (1.020)
  waiting for transfers between devices: 22.8 us -> 24.5 us
  starting transfers between devices: 32.5 us -> 31.5 us
    ppermute x7, waiting for transfers between devices: 12.3 us -> 14.1 us  [move(): lax.ppermute(value, 'cols', [(order[i], order[(i + by) % size]) for i in...]
    ppermute x7, starting transfers between devices: 7.68 us -> 6.67 us  [move(): lax.ppermute(value, 'cols', [(order[i], order[(i + by) % size]) for i in...]
  transfers between devices with their start and end apart: 22 -> 22, of which waited for: 10 -> 8; matrix products, arithmetic and copies ran while one was open for 1% -> 1% of each run, Pallas kernels for 9% -> 10%
where the time goes in v5:
time: 78.2 us; the launch traced here: 77.7 us
  starting transfers between devices  31.5 us (40%)
  waiting for transfers between devices  24.5 us (31%)
  Pallas kernels  17 us (22%)
  local copies, waits for them, and re-layouts  2.9 us (4%)
  between operations  0.91 us (1%)
  other arithmetic  0.83 us (1%)
    ppermute x7, waiting for transfers between devices, move(): lax.ppermute(value, 'cols', [(order[i], order[(i + by) % size]) for i in...  14.1 us
    ppermute x4, starting transfers between devices, with_chip(): lax.ppermute(value, 'rows', [p for k in odds for p in ((k, k + 1), (k + 1...  13.4 us
    ppermute x4, waiting for transfers between devices, with_chip(): lax.ppermute(value, 'rows', [p for k in odds for p in ((k, k + 1), (k + 1...  7.9 us
    ppermute x7, starting transfers between devices, move(): lax.ppermute(value, 'cols', [(order[i], order[(i + by) % size]) for i in...  6.67 us
    all_to_all x1, starting transfers between devices, per_device(): lax.all_to_all(pieces, 'cols', split_axis=0, concat_axis=0, tiled=True)  5.57 us
    ppermute x8, starting transfers between devices, with_core(): lax.ppermute(value, 'rows', [(i, i ^ 1) for i in range(lax.axis_size('row...  4.31 us
    pallas_call x1, Pallas kernels, per_device(): pl.pallas_call(second_stage, out_shape=jax.ShapeDtypeStruct((rows, width)...  3.38 us
    pallas_call x1, Pallas kernels, per_device(): pl.pallas_call(first_stage, out_shape=(jax.ShapeDtypeStruct((rows, width)...  3.28 us
  transfers between devices with their start and end apart: 22, of which 8 were waited for; matrix products, arithmetic and copies ran while one was open for 1% of the time, Pallas kernels for 10%

profile of v5, /device:TPU:1, one launch (start us, length us, event | category | flops | bytes accessed | tf_op | source)
XLA Modules:
  0.0 77.7 jit_solution(4092664468368982613)
XLA Ops:
  0.6 4.5 %collective-permute-start.3 = (bf16[16,64,512]{2,1,0:T(8,128)(2,1)}, bf16[16,64,512]{2,1,0:T(8,128)(2,1)S(1)}, u32[]{:S(2)}, u32[]{:S(2)}) collective-permute-start(bf16[16,64,512]{2,1,0:T(8,128)(2,1)} %tiles.1), channel_id=1, source_target_pairs={{8,16},{16,8},{9,17},{17,9},{10,18},{18,10},{11,19},{19,11},{12,20... | collective-permute-start | bytes 3145736 | tf_op jit(solution)/shard_map/ppermute | solution.py:37
  5.2 0.9 %copy-done.1 = bf16[128,1024]{1,0:T(8,128)(2,1)S(1)} copy-done((bf16[128,1024]{1,0:T(8,128)(2,1)S(1)}, bf16[128,1024]{1,0:T(8,128)(2,1)}, u32[]{:S(2)}) %copy-start.1) | copy-done | bytes 262168
  6.1 0.8 shard_map.59._
  6.9 5.6 %all-to-all-start = ((bf16[8,128,128]{2,1,0:T(8,128)(2,1)}), bf16[8,128,128]{2,1,0:T(8,128)(2,1)S(1)}, u32[]{:S(2)}, u32[]{:S(2)}) async-start(bf16[8,128,128]{2,1,0:T(8,128)(2,1)} %shard_map.59._), calls=%async_computation | async-start | bytes 524288 | tf_op jit(solution)/shard_map/all_to_all | solution.py:379
  12.4 0.7 subtract_clamp_fusion.2.offsets
  13.1 1.2 %copy-done = bf16[16,64,512]{2,1,0:T(8,128)(2,1)S(1)} copy-done((bf16[16,64,512]{2,1,0:T(8,128)(2,1)S(1)}, bf16[16,64,512]{2,1,0:T(8,128)(2,1)}, u32[]{:S(2)}) %copy-start) | copy-done | bytes 1048600
  14.4 0.7 copy-done.2
  15.0 2.3 %shard_map.60 = (bf16[4,256,768]{2,1,0:T(8,128)(2,1)S(1)}, bf16[12,64,512]{2,1,0:T(8,128)(2,1)}, s32[8,16]{1,0:T(8,128)S(1)}) custom-call(s32[1]{0:T(128)} %bitcast.odd, s32[8,16]{1,0:T(8,128)S(1)} %subtract_clamp_fusion.2.offsets, s32[8,16]{1,0:T(8,128)S(1)} %bitcast.13, bf16[16,64,512]{2,1,0:T(8,128)(2,1)S(1)} %copy-done, bf16[8,128,128]{2,1,0:T(8,128)(2,1)} %shard_map.59._), custom_call_target="tpu_custom_call" | custom-call | tf_op jit(solution)/shard_map/pallas_call | solution.py:394
  17.9 2.2 %collective-permute-start.1 = (s32[8,16]{1,0:T(8,128)S(1)}, s32[8,16]{1,0:T(8,128)S(1)}, u32[]{:S(2)}, u32[]{:S(2)}) collective-permute-start(s32[8,16]{1,0:T(8,128)S(1)} %get-tuple-element.18), channel_id=1, source_target_pairs={{8,16},{16,8},{9,17},{17,9},{10,18},{18,10},{11,19},{19,11},{12,20... | collective-permute-start | bytes 1544 | tf_op jit(solution)/shard_map/ppermute | solution.py:37
  20.2 3.4 %collective-permute-start.5 = (bf16[1024,128]{1,0:T(8,128)(2,1)S(1)}, bf16[1024,128]{1,0:T(8,128)(2,1)S(1)}, u32[]{:S(2)}, u32[]{:S(2)}) collective-permute-start(bf16[1024,128]{1,0:T(8,128)(2,1)S(1)} %bitcast.11), channel_id=1, source_target_pairs={{8,16},{16,8},{9,17},{17,9},{10,18},{18,10},{11,19},{19,11},{12,20... | collective-permute-start | bytes 786440 | tf_op jit(solution)/shard_map/ppermute | solution.py:37
  23.7 2.4 %shard_map.61.edges = bf16[6,256,768]{2,1,0:T(8,128)(2,1)S(1)} custom-call(s32[1]{0:T(128)} %bitcast.odd, s32[8,16]{1,0:T(8,128)S(1)} %subtract_clamp_fusion.1.at_first, s32[8,16]{1,0:T(8,128)S(1)} %subtract_clamp_fusion.at_second, bf16[12,64,512]{2,1,0:T(8,128)(2,1)} %collective-permute-done.2.first, bf16[16,64,512]{2,1,0:T(8,128)(2,1)S(1)} %collective-permute-done.3.second), custom_call_target="tpu_custom_call" | custom-call | tf_op jit(solution)/shard_map/pallas_call | solution.py:409
  26.0 1.9 %collective-permute-done.5.x_second = bf16[1024,128]{1,0:T(8,128)(2,1)S(1)} collective-permute-done((bf16[1024,128]{1,0:T(8,128)(2,1)S(1)}, bf16[1024,128]{1,0:T(8,128)(2,1)S(1)}, u32[]{:S(2)}, u32[]{:S(2)}) %collective-permute-start.5) | collective-permute-done | bytes 262176 | tf_op jit(solution)/shard_map/ppermute | solution.py:37
  27.9 3.3 %shard_map.62 = (f32[1024,128]{1,0:T(8,128)S(1)}, f32[1536,128]{1,0:T(8,128)S(1)}, bf16[1536,128]{1,0:T(8,128)(2,1)S(1)}) custom-call(s32[1]{0:T(128)} %bitcast.odd, bf16[4,256,768]{2,1,0:T(8,128)(2,1)S(1)} %get-tuple-element.17.own, bf16[6,256,768]{2,1,0:T(8,128)(2,1)S(1)} %shard_map.61.edges, bf16[1024,128]{1,0:T(8,128)(2,1)S(1)} %collective-permute-done.4.x_first, ...), custom_call_target="tpu_custom_call" | custom-call | tf_op jit(solution)/shard_map/pallas_call | solution.py:432
  31.3 3.4 %collective-permute-start.7 = (bf16[1536,128]{1,0:T(8,128)(2,1)S(1)}, bf16[1536,128]{1,0:T(8,128)(2,1)S(1)}, u32[]{:S(2)}, u32[]{:S(2)}) collective-permute-start(bf16[1536,128]{1,0:T(8,128)(2,1)S(1)} %get-tuple-element.22), channel_id=1, source_target_pairs={{8,16},{16,8},{9,17},{17,9},{10,18},{18,10},{11,19},{19,11},{12,20... | collective-permute-start | bytes 1179656 | tf_op jit(solution)/shard_map/ppermute | solution.py:37
  34.7 6.0 %collective-permute-done.7.got_second = bf16[1536,128]{1,0:T(8,128)(2,1)S(1)} collective-permute-done((bf16[1536,128]{1,0:T(8,128)(2,1)S(1)}, bf16[1536,128]{1,0:T(8,128)(2,1)S(1)}, u32[]{:S(2)}, u32[]{:S(2)}) %collective-permute-start.7) | collective-permute-done | bytes 393248 | tf_op jit(solution)/shard_map/ppermute | solution.py:37
  40.7 3.4 %shard_map.63.mine = bf16[1024,128]{1,0:T(8,128)(2,1)S(1)} custom-call(s32[1]{0:T(128)} %bitcast.odd, bf16[4,256,768]{2,1,0:T(8,128)(2,1)S(1)} %get-tuple-element.17.own, bf16[6,256,768]{2,1,0:T(8,128)(2,1)S(1)} %shard_map.61.edges, f32[1024,128]{1,0:T(8,128)S(1)} %get-tuple-element.20.now, f32[1536,128]{1,0:T(8,128)S(1)} %get-tuple-element.21.last, ...), custom_call_target="tpu_custom_call" | custom-call | tf_op jit(solution)/shard_map/pallas_call | solution.py:446
  44.1 2.7 %collective-permute-start.8 = (bf16[1024,128]{1,0:T(8,128)(2,1)S(1)}, bf16[1024,128]{1,0:T(8,128)(2,1)S(1)}, u32[]{:S(2)}, u32[]{:S(2)}) collective-permute-start(bf16[1024,128]{1,0:T(8,128)(2,1)S(1)} %shard_map.63.mine), channel_id=1, source_target_pairs={{0,4},{2,6},{4,7},{6,5},{7,3},{5,1},{3,0},{1,2},{8,12},{10,14},{12... | collective-permute-start | bytes 786440 | tf_op jit(solution)/shard_map/ppermute | solution.py:269
  46.8 1.4 %collective-permute-start.10 = (bf16[1024,128]{1,0:T(8,128)(2,1)S(1)}, bf16[1024,128]{1,0:T(8,128)(2,1)S(1)}, u32[]{:S(2)}, u32[]{:S(2)}) collective-permute-start(bf16[1024,128]{1,0:T(8,128)(2,1)S(1)} %shard_map.63.mine), channel_id=1, source_target_pairs={{0,2},{2,4},{4,6},{6,7},{7,5},{5,3},{3,1},{1,0},{8,10},{10,12},{12... | collective-permute-start | bytes 786440 | tf_op jit(solution)/shard_map/ppermute | solution.py:269
  48.3 4.5 %collective-permute-done.8.back.refs_0_ = bf16[1024,128]{1,0:T(8,128)(2,1)S(1)} collective-permute-done((bf16[1024,128]{1,0:T(8,128)(2,1)S(1)}, bf16[1024,128]{1,0:T(8,128)(2,1)S(1)}, u32[]{:S(2)}, u32[]{:S(2)}) %collective-permute-start.8) | collective-permute-done | bytes 262176 | tf_op jit(solution)/shard_map/ppermute | solution.py:269
  52.8 4.6 %collective-permute-done.9.front.refs_1_ = bf16[1024,128]{1,0:T(8,128)(2,1)S(1)} collective-permute-done((bf16[1024,128]{1,0:T(8,128)(2,1)S(1)}, bf16[1024,128]{1,0:T(8,128)(2,1)S(1)}, u32[]{:S(2)}, u32[]{:S(2)}) %collective-permute-start.9) | collective-permute-done | bytes 262176 | tf_op jit(solution)/shard_map/ppermute | solution.py:269
  57.5 1.0 %shard_map.64 = (f32[3,128,128]{2,1,0:T(8,128)S(1)}, bf16[3,128,1024]{2,1,0:T(8,128)(2,1)S(1)}, bf16[256,128]{1,0:T(8,128)(2,1)S(1)}) custom-call(s32[8]{0:T(128)S(1)} %compare_select_fusion.2.where, bf16[1024,128]{1,0:T(8,128)(2,1)S(1)} %shard_map.63.mine, bf16[1024,128]{1,0:T(8,128)(2,1)S(1)} %collective-permute-done.8.back.refs_0_, ...), custom_call_target="tpu_custom_call" | custom-call | tf_op jit(solution)/shard_map/pallas_call | solution.py:285
  58.5 0.8 collective-permute-done.11.refs_1_.refs_3_
  59.3 0.9 %shard_map.65 = (bf16[256,128]{1,0:T(8,128)(2,1)S(1)}, bf16[256,128]{1,0:T(8,128)(2,1)S(1)}) custom-call(s32[8]{0:T(128)S(1)} %compare_select_fusion.2.where, bf16[3,128,1024]{2,1,0:T(8,128)(2,1)S(1)} %get-tuple-element.23.lefts, bf16[1024,128]{1,0:T(8,128)(2,1)S(1)} %collective-permute-done.8.back.refs_0_, ...), custom_call_target="tpu_custom_call" | custom-call | tf_op jit(solution)/shard_map/pallas_call | solution.py:297
  60.6 2.4 %collective-permute-start.13 = (bf16[256,128]{1,0:T(8,128)(2,1)S(1)}, bf16[256,128]{1,0:T(8,128)(2,1)S(1)}, u32[]{:S(2)}, u32[]{:S(2)}) collective-permute-start(bf16[256,128]{1,0:T(8,128)(2,1)S(1)} %get-tuple-element.26), channel_id=1, source_target_pairs={{0,3},{2,1},{4,0},{6,2},{7,4},{5,6},{3,7},{1,5},{8,11},{10,9},{12,... | collective-permute-start | bytes 196616 | tf_op jit(solution)/shard_map/ppermute | solution.py:269
  63.1 4.2 %collective-permute-done.13.refs_4_ = bf16[256,128]{1,0:T(8,128)(2,1)S(1)} collective-permute-done((bf16[256,128]{1,0:T(8,128)(2,1)S(1)}, bf16[256,128]{1,0:T(8,128)(2,1)S(1)}, u32[]{:S(2)}, u32[]{:S(2)}) %collective-permute-start.13) | collective-permute-done | bytes 65568 | tf_op jit(solution)/shard_map/ppermute | solution.py:269
  67.4 1.6 %collective-permute-start.18 = (f32[3,64,128]{2,1,0:T(8,128)S(1)}, f32[3,64,128]{2,1,0:T(8,128)S(1)}, u32[]{:S(2)}, u32[]{:S(2)}) collective-permute-start(f32[3,64,128]{2,1,0:T(8,128)S(1)} %constant_dynamic-slice_fusion), channel_id=1, source_target_pairs={{0,8},{8,0},{16,24},{24,16},{1,9},{9,1},{17,25},{25,17},{2,10},{10... | collective-permute-start | bytes 294920 | tf_op jit(solution)/shard_map/ppermute | solution.py:32
  69.0 0.7 collective-permute-start.16
  70.0 0.8 %collective-permute-start.19 = (bf16[3,64,128]{2,1,0:T(8,128)(2,1)S(1)}, bf16[3,64,128]{2,1,0:T(8,128)(2,1)S(1)}, u32[]{:S(2)}, u32[]{:S(2)}) collective-permute-start(bf16[3,64,128]{2,1,0:T(8,128)(2,1)S(1)} %add_convert_fusion.1), channel_id=1, source_target_pairs={{0,16},{8,24},{16,0},{24,8},{1,17},{9,25},{17,1},{25,9},{2,18},{10... | collective-permute-start | bytes 147464 | tf_op jit(solution)/shard_map/ppermute | solution.py:353
  70.8 2.3 %collective-permute-done.16 = bf16[5,64,128]{2,1,0:T(8,128)(2,1)S(1)} collective-permute-done((bf16[5,64,128]{2,1,0:T(8,128)(2,1)S(1)}, bf16[5,64,128]{2,1,0:T(8,128)(2,1)S(1)}, u32[]{:S(2)}, u32[]{:S(2)}) %collective-permute-start.16) | collective-permute-done | bytes 81952 | tf_op jit(solution)/shard_map/ppermute | solution.py:353
  73.0 1.4 %collective-permute-start.17 = (f32[5,64,128]{2,1,0:T(8,128)S(1)}, f32[5,64,128]{2,1,0:T(8,128)S(1)}, u32[]{:S(2)}, u32[]{:S(2)}) collective-permute-start(f32[5,64,128]{2,1,0:T(8,128)S(1)} %convert_add_fusion.refs_0_), channel_id=1, source_target_pairs={{0,8},{8,0},{16,24},{24,16},{1,9},{9,1},{17,25},{25,17},{2,10},{10... | collective-permute-start | bytes 491528 | tf_op jit(solution)/shard_map/ppermute | solution.py:32
  75.0 1.3 %shard_map.67 = bf16[128,1024]{1,0:T(8,128)(2,1)} custom-call(s32[8]{0:T(128)S(1)} %compare_select_fusion.2.where, bf16[1024,128]{1,0:T(8,128)(2,1)S(1)} %shard_map.63.mine, bf16[1024,128]{1,0:T(8,128)(2,1)S(1)} %collective-permute-done.8.back.refs_0_, bf16[1024,128]{1,0:T(8,128)(2,1)S(1)} %collective-permute-done.9.front.refs_1_, ...), custom_call_target="tpu_custom_call" | custom-call | tf_op jit(solution)/shard_map/pallas_call | solution.py:318
  76.3 1.4 %shard_map.68 = f32[128,1024]{1,0:T(8,128)} custom-call(s32[8]{0:T(128)S(1)} %compare_select_fusion.2.where, s32[1]{0:T(128)} %bitcast.odd, f32[5,64,128]{2,1,0:T(8,128)S(1)} %convert_add_fusion.refs_0_, f32[5,64,128]{2,1,0:T(8,128)S(1)} %collective-permute-done.17.refs_1_, f32[3,64,128]{2,1,0:T(8,128)S(1)} %convert_add_fusion.1.refs_2_, ...), custom_call_target="tpu_custom_call" | custom-call | tf_op jit(solution)/shard_map/pallas_call | solution.py:327
  (46 shorter events, 2.2 us)
Async XLA Ops:
  0.6 23.0 %collective-permute-start.3 = (bf16[16,64,512]{2,1,0:T(8,128)(2,1)}, bf16[16,64,512]{2,1,0:T(8,128)(2,1)S(1)}, u32[]{:S(2)}, u32[]{:S(2)}) collective-permute-start(bf16[16,64,512]{2,1,0:T(8,128)(2,1)} %tiles.1), channel_id=1, source_target_pairs={{8,16},{16,8},{9,17},{17,9},{10,18},{18,10},{11,19},{19,11},{12,20... | collective-permute-start | bytes 3145736 | tf_op jit(solution)/shard_map/ppermute | solution.py:37
  5.1 1.0 %copy-start.1 = (bf16[128,1024]{1,0:T(8,128)(2,1)S(1)}, bf16[128,1024]{1,0:T(8,128)(2,1)}, u32[]{:S(2)}) copy-start(bf16[128,1024]{1,0:T(8,128)(2,1)} %vectors.1) | copy-start | bytes 786436
  6.9 13.3 %all-to-all-start = ((bf16[8,128,128]{2,1,0:T(8,128)(2,1)}), bf16[8,128,128]{2,1,0:T(8,128)(2,1)S(1)}, u32[]{:S(2)}, u32[]{:S(2)}) async-start(bf16[8,128,128]{2,1,0:T(8,128)(2,1)} %shard_map.59._), calls=%async_computation | async-start | bytes 524288 | tf_op jit(solution)/shard_map/all_to_all | solution.py:379
  13.1 1.2 %copy-start = (bf16[16,64,512]{2,1,0:T(8,128)(2,1)S(1)}, bf16[16,64,512]{2,1,0:T(8,128)(2,1)}, u32[]{:S(2)}) copy-start(bf16[16,64,512]{2,1,0:T(8,128)(2,1)} %tiles.1) | copy-start | bytes 3145732
  14.4 0.7 copy-start.2
  17.4 6.3 %collective-permute-start.2 = (bf16[12,64,512]{2,1,0:T(8,128)(2,1)}, bf16[12,64,512]{2,1,0:T(8,128)(2,1)}, u32[]{:S(2)}, u32[]{:S(2)}) collective-permute-start(bf16[12,64,512]{2,1,0:T(8,128)(2,1)} %get-tuple-element.19), channel_id=1, source_target_pairs={{0,8},{8,0},{16,24},{24,16},{1,9},{9,1},{17,25},{25,17},{2,10},{10... | collective-permute-start | bytes 2359304 | tf_op jit(solution)/shard_map/ppermute | solution.py:32
  17.4 2.8 %collective-permute-start = (s32[8,16]{1,0:T(8,128)S(1)}, s32[8,16]{1,0:T(8,128)S(1)}, u32[]{:S(2)}, u32[]{:S(2)}) collective-permute-start(s32[8,16]{1,0:T(8,128)S(1)} %get-tuple-element.18), channel_id=1, source_target_pairs={{0,8},{8,0},{16,24},{24,16},{1,9},{9,1},{17,25},{25,17},{2,10},{10... | collective-permute-start | bytes 1544 | tf_op jit(solution)/shard_map/ppermute | solution.py:32
  17.9 5.7 %collective-permute-start.1 = (s32[8,16]{1,0:T(8,128)S(1)}, s32[8,16]{1,0:T(8,128)S(1)}, u32[]{:S(2)}, u32[]{:S(2)}) collective-permute-start(s32[8,16]{1,0:T(8,128)S(1)} %get-tuple-element.18), channel_id=1, source_target_pairs={{8,16},{16,8},{9,17},{17,9},{10,18},{18,10},{11,19},{19,11},{12,20... | collective-permute-start | bytes 1544 | tf_op jit(solution)/shard_map/ppermute | solution.py:37
  20.1 5.9 %collective-permute-start.4 = (bf16[1024,128]{1,0:T(8,128)(2,1)S(1)}, bf16[1024,128]{1,0:T(8,128)(2,1)S(1)}, u32[]{:S(2)}, u32[]{:S(2)}) collective-permute-start(bf16[1024,128]{1,0:T(8,128)(2,1)S(1)} %bitcast.10), channel_id=1, source_target_pairs={{0,8},{8,0},{16,24},{24,16},{1,9},{9,1},{17,25},{25,17},{2,10},{10... | collective-permute-start | bytes 786440 | tf_op jit(solution)/shard_map/ppermute | solution.py:32
  20.2 7.7 %collective-permute-start.5 = (bf16[1024,128]{1,0:T(8,128)(2,1)S(1)}, bf16[1024,128]{1,0:T(8,128)(2,1)S(1)}, u32[]{:S(2)}, u32[]{:S(2)}) collective-permute-start(bf16[1024,128]{1,0:T(8,128)(2,1)S(1)} %bitcast.11), channel_id=1, source_target_pairs={{8,16},{16,8},{9,17},{17,9},{10,18},{18,10},{11,19},{19,11},{12,20... | collective-permute-start | bytes 786440 | tf_op jit(solution)/shard_map/ppermute | solution.py:37
  31.2 3.5 %collective-permute-start.6 = (bf16[1536,128]{1,0:T(8,128)(2,1)S(1)}, bf16[1536,128]{1,0:T(8,128)(2,1)S(1)}, u32[]{:S(2)}, u32[]{:S(2)}) collective-permute-start(bf16[1536,128]{1,0:T(8,128)(2,1)S(1)} %get-tuple-element.22), channel_id=1, source_target_pairs={{0,8},{8,0},{16,24},{24,16},{1,9},{9,1},{17,25},{25,17},{2,10},{10... | collective-permute-start | bytes 1179656 | tf_op jit(solution)/shard_map/ppermute | solution.py:32
  31.3 9.4 %collective-permute-start.7 = (bf16[1536,128]{1,0:T(8,128)(2,1)S(1)}, bf16[1536,128]{1,0:T(8,128)(2,1)S(1)}, u32[]{:S(2)}, u32[]{:S(2)}) collective-permute-start(bf16[1536,128]{1,0:T(8,128)(2,1)S(1)} %get-tuple-element.22), channel_id=1, source_target_pairs={{8,16},{16,8},{9,17},{17,9},{10,18},{18,10},{11,19},{19,11},{12,20... | collective-permute-start | bytes 1179656 | tf_op jit(solution)/shard_map/ppermute | solution.py:37
  40.7 7.6 %copy-start.3 = (s32[8]{0:T(128)S(1)}, s32[8]{0:T(128)}, u32[]{:S(2)}) copy-start(s32[8]{0:T(128)} %constant.68.clone) | copy-start | bytes 100
  44.1 8.7 %collective-permute-start.8 = (bf16[1024,128]{1,0:T(8,128)(2,1)S(1)}, bf16[1024,128]{1,0:T(8,128)(2,1)S(1)}, u32[]{:S(2)}, u32[]{:S(2)}) collective-permute-start(bf16[1024,128]{1,0:T(8,128)(2,1)S(1)} %shard_map.63.mine), channel_id=1, source_target_pairs={{0,4},{2,6},{4,7},{6,5},{7,3},{5,1},{3,0},{1,2},{8,12},{10,14},{12... | collective-permute-start | bytes 786440 | tf_op jit(solution)/shard_map/ppermute | solution.py:269
  46.8 10.7 %collective-permute-start.9 = (bf16[1024,128]{1,0:T(8,128)(2,1)S(1)}, bf16[1024,128]{1,0:T(8,128)(2,1)S(1)}, u32[]{:S(2)}, u32[]{:S(2)}) collective-permute-start(bf16[1024,128]{1,0:T(8,128)(2,1)S(1)} %shard_map.63.mine), channel_id=1, source_target_pairs={{0,3},{2,1},{4,0},{6,2},{7,4},{5,6},{3,7},{1,5},{8,11},{10,9},{12,... | collective-permute-start | bytes 786440 | tf_op jit(solution)/shard_map/ppermute | solution.py:269
  46.8 11.7 %collective-permute-start.10 = (bf16[1024,128]{1,0:T(8,128)(2,1)S(1)}, bf16[1024,128]{1,0:T(8,128)(2,1)S(1)}, u32[]{:S(2)}, u32[]{:S(2)}) collective-permute-start(bf16[1024,128]{1,0:T(8,128)(2,1)S(1)} %shard_map.63.mine), channel_id=1, source_target_pairs={{0,2},{2,4},{4,6},{6,7},{7,5},{5,3},{3,1},{1,0},{8,10},{10,12},{12... | collective-permute-start | bytes 786440 | tf_op jit(solution)/shard_map/ppermute | solution.py:269
  48.2 11.0 %collective-permute-start.11 = (bf16[1024,128]{1,0:T(8,128)(2,1)S(1)}, bf16[1024,128]{1,0:T(8,128)(2,1)S(1)}, u32[]{:S(2)}, u32[]{:S(2)}) collective-permute-start(bf16[1024,128]{1,0:T(8,128)(2,1)S(1)} %shard_map.63.mine), channel_id=1, source_target_pairs={{0,1},{2,0},{4,2},{6,4},{7,6},{5,7},{3,5},{1,3},{8,9},{10,8},{12,1... | collective-permute-start | bytes 786440 | tf_op jit(solution)/shard_map/ppermute | solution.py:269
  60.5 2.6 %collective-permute-start.12 = (f32[5,64,128]{2,1,0:T(8,128)S(1)}, f32[5,64,128]{2,1,0:T(8,128)S(1)}, u32[]{:S(2)}, u32[]{:S(2)}) collective-permute-start(f32[5,64,128]{2,1,0:T(8,128)S(1)} %constant_dynamic-slice_fusion.1), channel_id=1, source_target_pairs={{0,8},{8,0},{16,24},{24,16},{1,9},{9,1},{17,25},{25,17},{2,10},{10... | collective-permute-start | bytes 491528 | tf_op jit(solution)/shard_map/ppermute | solution.py:32
  60.6 6.7 %collective-permute-start.15 = (bf16[256,128]{1,0:T(8,128)(2,1)S(1)}, bf16[256,128]{1,0:T(8,128)(2,1)S(1)}, u32[]{:S(2)}, u32[]{:S(2)}) collective-permute-start(bf16[256,128]{1,0:T(8,128)(2,1)S(1)} %get-tuple-element.25.refs_2_), channel_id=1, source_target_pairs={{0,1},{2,0},{4,2},{6,4},{7,6},{5,7},{3,5},{1,3},{8,9},{10,8},{12,1... | collective-permute-start | bytes 196616 | tf_op jit(solution)/shard_map/ppermute | solution.py:269
  60.6 6.6 %collective-permute-start.13 = (bf16[256,128]{1,0:T(8,128)(2,1)S(1)}, bf16[256,128]{1,0:T(8,128)(2,1)S(1)}, u32[]{:S(2)}, u32[]{:S(2)}) collective-permute-start(bf16[256,128]{1,0:T(8,128)(2,1)S(1)} %get-tuple-element.26), channel_id=1, source_target_pairs={{0,3},{2,1},{4,0},{6,2},{7,4},{5,6},{3,7},{1,5},{8,11},{10,9},{12,... | collective-permute-start | bytes 196616 | tf_op jit(solution)/shard_map/ppermute | solution.py:269
  63.0 4.2 %collective-permute-start.14 = (bf16[256,128]{1,0:T(8,128)(2,1)S(1)}, bf16[256,128]{1,0:T(8,128)(2,1)S(1)}, u32[]{:S(2)}, u32[]{:S(2)}) collective-permute-start(bf16[256,128]{1,0:T(8,128)(2,1)S(1)} %get-tuple-element.27), channel_id=1, source_target_pairs={{0,2},{2,4},{4,6},{6,7},{7,5},{5,3},{3,1},{1,0},{8,10},{10,12},{12... | collective-permute-start | bytes 196616 | tf_op jit(solution)/shard_map/ppermute | solution.py:269
  67.4 2.6 %collective-permute-start.18 = (f32[3,64,128]{2,1,0:T(8,128)S(1)}, f32[3,64,128]{2,1,0:T(8,128)S(1)}, u32[]{:S(2)}, u32[]{:S(2)}) collective-permute-start(f32[3,64,128]{2,1,0:T(8,128)S(1)} %constant_dynamic-slice_fusion), channel_id=1, source_target_pairs={{0,8},{8,0},{16,24},{24,16},{1,9},{9,1},{17,25},{25,17},{2,10},{10... | collective-permute-start | bytes 294920 | tf_op jit(solution)/shard_map/ppermute | solution.py:32
  69.0 4.0 %collective-permute-start.16 = (bf16[5,64,128]{2,1,0:T(8,128)(2,1)S(1)}, bf16[5,64,128]{2,1,0:T(8,128)(2,1)S(1)}, u32[]{:S(2)}, u32[]{:S(2)}) collective-permute-start(bf16[5,64,128]{2,1,0:T(8,128)(2,1)S(1)} %add_convert_fusion), channel_id=1, source_target_pairs={{0,16},{8,24},{16,0},{24,8},{1,17},{9,25},{17,1},{25,9},{2,18},{10... | collective-permute-start | bytes 245768 | tf_op jit(solution)/shard_map/ppermute | solution.py:353
  70.0 4.5 %collective-permute-start.19 = (bf16[3,64,128]{2,1,0:T(8,128)(2,1)S(1)}, bf16[3,64,128]{2,1,0:T(8,128)(2,1)S(1)}, u32[]{:S(2)}, u32[]{:S(2)}) collective-permute-start(bf16[3,64,128]{2,1,0:T(8,128)(2,1)S(1)} %add_convert_fusion.1), channel_id=1, source_target_pairs={{0,16},{8,24},{16,0},{24,8},{1,17},{9,25},{17,1},{25,9},{2,18},{10... | collective-permute-start | bytes 147464 | tf_op jit(solution)/shard_map/ppermute | solution.py:353
  73.0 3.3 %collective-permute-start.17 = (f32[5,64,128]{2,1,0:T(8,128)S(1)}, f32[5,64,128]{2,1,0:T(8,128)S(1)}, u32[]{:S(2)}, u32[]{:S(2)}) collective-permute-start(f32[5,64,128]{2,1,0:T(8,128)S(1)} %convert_add_fusion.refs_0_), channel_id=1, source_target_pairs={{0,8},{8,0},{16,24},{24,16},{1,9},{9,1},{17,25},{25,17},{2,10},{10... | collective-permute-start | bytes 491528 | tf_op jit(solution)/shard_map/ppermute | solution.py:32
  74.4 1.9 %collective-permute-start.20 = (f32[3,64,128]{2,1,0:T(8,128)S(1)}, f32[3,64,128]{2,1,0:T(8,128)S(1)}, u32[]{:S(2)}, u32[]{:S(2)}) collective-permute-start(f32[3,64,128]{2,1,0:T(8,128)S(1)} %convert_add_fusion.1.refs_2_), channel_id=1, source_target_pairs={{0,8},{8,0},{16,24},{24,16},{1,9},{9,1},{17,25},{25,17},{2,10},{10... | collective-permute-start | bytes 294920 | tf_op jit(solution)/shard_map/ppermute | solution.py:32

commit v6 on v4

--- a/solution.py
+++ b/solution.py
@@ -72,6 +72,41 @@
     )
 
 
+def place_group(offsets, ahead, tiles, start, bands, band, doubled, slot):
+    kt = offsets.shape[0]
+    tile = tiles.shape[1]
+    blank = kt
+    nothing = jnp.zeros((tile, tile), doubled.dtype)
+    for i in range(HALO):
+        values = tiles[start + i]
+        for k in range(kt):
+            one = values[:, k * tile:(k + 1) * tile]
+            doubled[i, k] = jnp.concatenate([one, one], axis=1)
+        for place in range(2 * HALO + 1):
+            slot[i, place] = blank
+        for k in range(kt):
+            slot[i, offsets[k, ahead + start + i] + HALO] = k
+    for i in range(HALO):
+        rows = slice(i * tile, (i + 1) * tile)
+        for pair in range(SPAN * HALO // 2):
+            halves = []
+            for side in range(2):
+                place = 2 * pair + side - i
+                if 0 <= place <= 2 * HALO:
+                    both = doubled[i, slot[i, place]]
+                    halves.append(both[:, side * tile:(side + 1) * tile])
+                else:
+                    halves.append(nothing)
+            columns = slice(2 * pair * tile, 2 * (pair + 1) * tile)
+            bands[band, rows, columns] = jnp.concatenate(halves, axis=1)
+
+
+def clear(doubled):
+    doubled[:, doubled.shape[1] - 1] = jnp.zeros(
+        doubled.shape[:1] + doubled.shape[2:], doubled.dtype
+    )
+
+
 def split_columns(vectors, pieces):
     width = pieces.shape[2]
     for i in range(pieces.shape[0]):
@@ -92,7 +127,7 @@
         copy.wait()
 
 
-def own_bands(odd, offsets, columns, tiles, _, bands, to_first, columns_out, doubled, slot):
+def own_bands(odd, offsets, columns, tiles, bands, to_first, columns_out, doubled, slot):
     count = tiles.shape[0]
     sent = to_first.shape[0]
     to_first[...] = tiles[pl.ds((1 - odd[0]) * (count - sent), sent)]
@@ -133,8 +168,12 @@
             start = j * size
             here = slice(start + size, start + 2 * size)
             product = dot(bands[j][...], src[start:start + span])
-            value = product - shift_value * cur[here]
-            value = value / half_width if degree + step == 0 else value - new[here]
+            if degree + step == 0:
+                value = (product - shift_value * src[here].astype(jnp.float32)) / half_width
+            elif degree + step == 1:
+                value = product - shift_value * cur[here] - dst[here].astype(jnp.float32)
+            else:
+                value = product - shift_value * cur[here] - new[here]
             new[here] = value
             dst[here] = value.astype(jnp.bfloat16)
         cur, new = new, cur
@@ -153,7 +192,6 @@
     starts = (placed(odd[0], rows), rows, placed(1 - odd[0], rows))
     for start, ref in zip(starts, (x_first, x_own, x_second)):
         w0[pl.ds(start, rows)] = ref[...]
-        y0[pl.ds(start, rows)] = ref[...].astype(jnp.float32)
     cur, prev, rounded = run_steps(own, edges, (w0, w1), (y0, y1), 0)
     now_out[...] = cur[rows:2 * rows]
     last_out[...] = prev[rows - size:2 * rows + size]
@@ -363,17 +401,7 @@
     width = search_vectors.shape[1] // col_parts
     rows = share * col_parts
     second = with_chip(tile_values)
-    lanes = width % 128 == 0
-    pieces = pl.pallas_call(
-        copy_columns if lanes else split_columns,
-        out_shape=jax.ShapeDtypeStruct((col_parts, share, width), search_vectors.dtype),
-        in_specs=[pl.BlockSpec(memory_space=pltpu.HBM) if lanes else VMEM],
-        out_specs=pl.BlockSpec(memory_space=pltpu.HBM) if lanes else VMEM,
-        scratch_shapes=[pltpu.SemaphoreType.DMA((col_parts,))] if lanes else [],
-        compiler_params=params(4),
-    )(search_vectors)
-    columns = lax.all_to_all(pieces, "cols", split_axis=0, concat_axis=0, tiled=True)
-    columns = columns.reshape(rows, width)
+    columns = lax.all_to_all(search_vectors, "cols", split_axis=1, concat_axis=0, tiled=True)
 
     size = HALO * tile
     odd = row_part & 1
@@ -394,11 +422,11 @@
             jax.ShapeDtypeStruct((TILES_REACH, tile, depth), jnp.bfloat16),
             jax.ShapeDtypeStruct((kt, count), jnp.int32),
         ),
-        in_specs=[SMEM, SMEM, VMEM, VMEM, ANY],
+        in_specs=[SMEM, SMEM, VMEM, VMEM],
         out_specs=(VMEM,) * 3,
         scratch_shapes=scratch,
         compiler_params=params(16),
-    )(odd[None], offsets_of(block_columns, row_part), block_columns, tile_values, pieces)
+    )(odd[None], offsets_of(block_columns, row_part), block_columns, tile_values)
     first = with_core(to_first)
     at_first = with_core(sent_columns)
     at_second = with_chip(sent_columns)

time: 76.7 us -> 75.8 us (0.988)
  Pallas kernels: 16.4 us -> 15.6 us
    unnamed x8, local copies, waits for them, and re-layouts: 2.86 us -> 1.92 us
  transfers between devices with their start and end apart: 22 -> 22, of which waited for: 10 -> 10; matrix products, arithmetic and copies ran while one was open for 1% -> 2% of each run, Pallas kernels for 9% -> 9%
where the time goes in v6:
time: 75.8 us; the launch traced here: 75.4 us
  starting transfers between devices  32.6 us (43%)
  waiting for transfers between devices  22.8 us (30%)
  Pallas kernels  15.6 us (21%)
  local copies, waits for them, and re-layouts  2.72 us (4%)
  between operations  0.89 us (1%)
  other arithmetic  0.83 us (1%)
    ppermute x4, starting transfers between devices, with_chip(): lax.ppermute(value, 'rows', [p for k in odds for p in ((k, k + 1), (k + 1...  13.6 us
    ppermute x7, waiting for transfers between devices, move(): lax.ppermute(value, 'cols', [(order[i], order[(i + by) % size]) for i in...  12.3 us
    ppermute x4, waiting for transfers between devices, with_chip(): lax.ppermute(value, 'rows', [p for k in odds for p in ((k, k + 1), (k + 1...  7.9 us
    ppermute x7, starting transfers between devices, move(): lax.ppermute(value, 'cols', [(order[i], order[(i + by) % size]) for i in...  7.68 us
    all_to_all x1, starting transfers between devices, per_device(): lax.all_to_all(search_vectors, 'cols', split_axis=1, concat_axis=0, tiled...  5.55 us
    ppermute x8, starting transfers between devices, with_core(): lax.ppermute(value, 'rows', [(i, i ^ 1) for i in range(lax.axis_size('row...  4.32 us
    pallas_call x1, Pallas kernels, per_device(): pl.pallas_call(second_stage, out_shape=jax.ShapeDtypeStruct((rows, width)...  3.38 us
    pallas_call x1, Pallas kernels, per_device(): pl.pallas_call(first_stage, out_shape=(jax.ShapeDtypeStruct((rows, width)...  3.24 us
  transfers between devices with their start and end apart: 22, of which 10 were waited for; matrix products, arithmetic and copies ran while one was open for 2% of the time, Pallas kernels for 9%

profile of v6, /device:TPU:1, one launch (start us, length us, event | category | flops | bytes accessed | tf_op | source)
XLA Modules:
  0.0 75.4 jit_solution(9021480964334824025)
XLA Ops:
  0.6 4.6 %collective-permute-start.3 = (bf16[16,64,512]{2,1,0:T(8,128)(2,1)}, bf16[16,64,512]{2,1,0:T(8,128)(2,1)S(1)}, u32[]{:S(2)}, u32[]{:S(2)}) collective-permute-start(bf16[16,64,512]{2,1,0:T(8,128)(2,1)} %tiles.1), channel_id=1, source_target_pairs={{8,16},{16,8},{9,17},{17,9},{10,18},{18,10},{11,19},{19,11},{12,20... | collective-permute-start | bytes 3145736 | tf_op jit(solution)/shard_map/ppermute | solution.py:37
  5.3 0.8 copy_bitcast_fusion
  6.1 5.6 %all-to-all-start = ((bf16[128,8,128]{2,0,1:T(8,128)(2,1)}), bf16[128,8,128]{2,0,1:T(8,128)(2,1)S(1)}, u32[]{:S(2)}, u32[]{:S(2)}) async-start(bf16[128,8,128]{2,0,1:T(8,128)(2,1)} %copy_bitcast_fusion), calls=%async_computation | async-start | bytes 524288 | tf_op jit(solution)/shard_map/all_to_all | solution.py:404
  11.6 0.7 subtract_clamp_fusion.2.offsets
  12.3 1.2 %copy-done.1 = bf16[16,64,512]{2,1,0:T(8,128)(2,1)S(1)} copy-done((bf16[16,64,512]{2,1,0:T(8,128)(2,1)S(1)}, bf16[16,64,512]{2,1,0:T(8,128)(2,1)}, u32[]{:S(2)}) %copy-start.1) | copy-done | bytes 1048600
  14.2 2.3 %shard_map.59 = (bf16[4,256,768]{2,1,0:T(8,128)(2,1)S(1)}, bf16[12,64,512]{2,1,0:T(8,128)(2,1)}, s32[8,16]{1,0:T(8,128)S(1)}) custom-call(s32[1]{0:T(128)} %bitcast.odd, s32[8,16]{1,0:T(8,128)S(1)} %subtract_clamp_fusion.2.offsets, s32[8,16]{1,0:T(8,128)S(1)} %bitcast.20, bf16[16,64,512]{2,1,0:T(8,128)(2,1)S(1)} %copy-done.1), custom_call_target="tpu_custom_call" | custom-call | tf_op jit(solution)/shard_map/pallas_call | solution.py:418
  17.1 2.2 %collective-permute-start.1 = (s32[8,16]{1,0:T(8,128)S(1)}, s32[8,16]{1,0:T(8,128)S(1)}, u32[]{:S(2)}, u32[]{:S(2)}) collective-permute-start(s32[8,16]{1,0:T(8,128)S(1)} %get-tuple-element.18), channel_id=1, source_target_pairs={{8,16},{16,8},{9,17},{17,9},{10,18},{18,10},{11,19},{19,11},{12,20... | collective-permute-start | bytes 1544 | tf_op jit(solution)/shard_map/ppermute | solution.py:37
  19.4 3.4 %collective-permute-start.5 = (bf16[1024,128]{1,0:T(8,128)(2,1)S(1)}, bf16[1024,128]{1,0:T(8,128)(2,1)S(1)}, u32[]{:S(2)}, u32[]{:S(2)}) collective-permute-start(bf16[1024,128]{1,0:T(8,128)(2,1)S(1)} %bitcast.18), channel_id=1, source_target_pairs={{8,16},{16,8},{9,17},{17,9},{10,18},{18,10},{11,19},{19,11},{12,20... | collective-permute-start | bytes 786440 | tf_op jit(solution)/shard_map/ppermute | solution.py:37
  22.8 2.4 %shard_map.60.edges = bf16[6,256,768]{2,1,0:T(8,128)(2,1)S(1)} custom-call(s32[1]{0:T(128)} %bitcast.odd, s32[8,16]{1,0:T(8,128)S(1)} %subtract_clamp_fusion.1.at_first, s32[8,16]{1,0:T(8,128)S(1)} %subtract_clamp_fusion.at_second, bf16[12,64,512]{2,1,0:T(8,128)(2,1)} %collective-permute-done.2.first, bf16[16,64,512]{2,1,0:T(8,128)(2,1)S(1)} %collective-permute-done.3.second), custom_call_target="tpu_custom_call" | custom-call | tf_op jit(solution)/shard_map/pallas_call | solution.py:433
  25.2 1.9 %collective-permute-done.5.x_second = bf16[1024,128]{1,0:T(8,128)(2,1)S(1)} collective-permute-done((bf16[1024,128]{1,0:T(8,128)(2,1)S(1)}, bf16[1024,128]{1,0:T(8,128)(2,1)S(1)}, u32[]{:S(2)}, u32[]{:S(2)}) %collective-permute-start.5) | collective-permute-done | bytes 262176 | tf_op jit(solution)/shard_map/ppermute | solution.py:37
  27.1 3.2 %shard_map.61 = (f32[1024,128]{1,0:T(8,128)S(1)}, f32[1536,128]{1,0:T(8,128)S(1)}, bf16[1536,128]{1,0:T(8,128)(2,1)S(1)}) custom-call(s32[1]{0:T(128)} %bitcast.odd, bf16[4,256,768]{2,1,0:T(8,128)(2,1)S(1)} %get-tuple-element.17.own, bf16[6,256,768]{2,1,0:T(8,128)(2,1)S(1)} %shard_map.60.edges, bf16[1024,128]{1,0:T(8,128)(2,1)S(1)} %collective-permute-done.4.x_first, ...), custom_call_target="tpu_custom_call" | custom-call | tf_op jit(solution)/shard_map/pallas_call | solution.py:456
  30.4 3.4 %collective-permute-start.7 = (bf16[1536,128]{1,0:T(8,128)(2,1)S(1)}, bf16[1536,128]{1,0:T(8,128)(2,1)S(1)}, u32[]{:S(2)}, u32[]{:S(2)}) collective-permute-start(bf16[1536,128]{1,0:T(8,128)(2,1)S(1)} %get-tuple-element.22), channel_id=1, source_target_pairs={{8,16},{16,8},{9,17},{17,9},{10,18},{18,10},{11,19},{19,11},{12,20... | collective-permute-start | bytes 1179656 | tf_op jit(solution)/shard_map/ppermute | solution.py:37
  33.8 6.0 %collective-permute-done.7.got_second = bf16[1536,128]{1,0:T(8,128)(2,1)S(1)} collective-permute-done((bf16[1536,128]{1,0:T(8,128)(2,1)S(1)}, bf16[1536,128]{1,0:T(8,128)(2,1)S(1)}, u32[]{:S(2)}, u32[]{:S(2)}) %collective-permute-start.7) | collective-permute-done | bytes 393248 | tf_op jit(solution)/shard_map/ppermute | solution.py:37
  39.8 3.4 %shard_map.62.mine = bf16[1024,128]{1,0:T(8,128)(2,1)S(1)} custom-call(s32[1]{0:T(128)} %bitcast.odd, bf16[4,256,768]{2,1,0:T(8,128)(2,1)S(1)} %get-tuple-element.17.own, bf16[6,256,768]{2,1,0:T(8,128)(2,1)S(1)} %shard_map.60.edges, f32[1024,128]{1,0:T(8,128)S(1)} %get-tuple-element.20.now, f32[1536,128]{1,0:T(8,128)S(1)} %get-tuple-element.21.last, ...), custom_call_target="tpu_custom_call" | custom-call | tf_op jit(solution)/shard_map/pallas_call | solution.py:470
  43.2 1.8 %collective-permute-start.8 = (bf16[1024,128]{1,0:T(8,128)(2,1)S(1)}, bf16[1024,128]{1,0:T(8,128)(2,1)S(1)}, u32[]{:S(2)}, u32[]{:S(2)}) collective-permute-start(bf16[1024,128]{1,0:T(8,128)(2,1)S(1)} %shard_map.62.mine), channel_id=1, source_target_pairs={{0,2},{2,4},{4,6},{6,7},{7,5},{5,3},{3,1},{1,0},{8,10},{10,12},{12... | collective-permute-start | bytes 786440 | tf_op jit(solution)/shard_map/ppermute | solution.py:303
  45.0 2.3 %collective-permute-start.10 = (bf16[1024,128]{1,0:T(8,128)(2,1)S(1)}, bf16[1024,128]{1,0:T(8,128)(2,1)S(1)}, u32[]{:S(2)}, u32[]{:S(2)}) collective-permute-start(bf16[1024,128]{1,0:T(8,128)(2,1)S(1)} %shard_map.62.mine), channel_id=1, source_target_pairs={{0,4},{2,6},{4,7},{6,5},{7,3},{5,1},{3,0},{1,2},{8,12},{10,14},{12... | collective-permute-start | bytes 786440 | tf_op jit(solution)/shard_map/ppermute | solution.py:303
  47.4 2.4 %collective-permute-done.8.refs_0_ = bf16[1024,128]{1,0:T(8,128)(2,1)S(1)} collective-permute-done((bf16[1024,128]{1,0:T(8,128)(2,1)S(1)}, bf16[1024,128]{1,0:T(8,128)(2,1)S(1)}, u32[]{:S(2)}, u32[]{:S(2)}) %collective-permute-start.8) | collective-permute-done | bytes 262176 | tf_op jit(solution)/shard_map/ppermute | solution.py:303
  49.8 2.1 %collective-permute-done.9.refs_1_ = bf16[1024,128]{1,0:T(8,128)(2,1)S(1)} collective-permute-done((bf16[1024,128]{1,0:T(8,128)(2,1)S(1)}, bf16[1024,128]{1,0:T(8,128)(2,1)S(1)}, u32[]{:S(2)}, u32[]{:S(2)}) %collective-permute-start.9) | collective-permute-done | bytes 262176 | tf_op jit(solution)/shard_map/ppermute | solution.py:303
  52.4 3.2 %collective-permute-done.10.back.refs_2_ = bf16[1024,128]{1,0:T(8,128)(2,1)S(1)} collective-permute-done((bf16[1024,128]{1,0:T(8,128)(2,1)S(1)}, bf16[1024,128]{1,0:T(8,128)(2,1)S(1)}, u32[]{:S(2)}, u32[]{:S(2)}) %collective-permute-start.10) | collective-permute-done | bytes 262176 | tf_op jit(solution)/shard_map/ppermute | solution.py:303
  55.6 1.0 %collective-permute-done.11.front.refs_3_ = bf16[1024,128]{1,0:T(8,128)(2,1)S(1)} collective-permute-done((bf16[1024,128]{1,0:T(8,128)(2,1)S(1)}, bf16[1024,128]{1,0:T(8,128)(2,1)S(1)}, u32[]{:S(2)}, u32[]{:S(2)}) %collective-permute-start.11) | collective-permute-done | bytes 262176 | tf_op jit(solution)/shard_map/ppermute | solution.py:303
  56.5 0.9 %shard_map.64 = (bf16[256,128]{1,0:T(8,128)(2,1)S(1)}, bf16[256,128]{1,0:T(8,128)(2,1)S(1)}, bf16[256,128]{1,0:T(8,128)(2,1)S(1)}) custom-call(s32[8]{0:T(128)S(1)} %compare_select_fusion.2.where, bf16[3,128,1024]{2,1,0:T(8,128)(2,1)S(1)} %get-tuple-element.23.lefts, bf16[1024,128]{1,0:T(8,128)(2,1)S(1)} %collective-permute-done.10.back.refs_2_, ...), custom_call_target="tpu_custom_call" | custom-call | tf_op jit(solution)/shard_map/pallas_call | solution.py:331
  57.8 1.8 %collective-permute-start.15 = (bf16[256,128]{1,0:T(8,128)(2,1)S(1)}, bf16[256,128]{1,0:T(8,128)(2,1)S(1)}, u32[]{:S(2)}, u32[]{:S(2)}) collective-permute-start(bf16[256,128]{1,0:T(8,128)(2,1)S(1)} %get-tuple-element.25._), channel_id=1, source_target_pairs={{0,3},{2,1},{4,0},{6,2},{7,4},{5,6},{3,7},{1,5},{8,11},{10,9},{12,... | collective-permute-start | bytes 196616 | tf_op jit(solution)/shard_map/ppermute | solution.py:303
  59.6 1.7 %collective-permute-start.13 = (bf16[256,128]{1,0:T(8,128)(2,1)S(1)}, bf16[256,128]{1,0:T(8,128)(2,1)S(1)}, u32[]{:S(2)}, u32[]{:S(2)}) collective-permute-start(bf16[256,128]{1,0:T(8,128)(2,1)S(1)} %get-tuple-element.26), channel_id=1, source_target_pairs={{0,2},{2,4},{4,6},{6,7},{7,5},{5,3},{3,1},{1,0},{8,10},{10,12},{12... | collective-permute-start | bytes 196616 | tf_op jit(solution)/shard_map/ppermute | solution.py:303
  61.3 1.8 %collective-permute-done.13.refs_4_ = bf16[256,128]{1,0:T(8,128)(2,1)S(1)} collective-permute-done((bf16[256,128]{1,0:T(8,128)(2,1)S(1)}, bf16[256,128]{1,0:T(8,128)(2,1)S(1)}, u32[]{:S(2)}, u32[]{:S(2)}) %collective-permute-start.13) | collective-permute-done | bytes 65568 | tf_op jit(solution)/shard_map/ppermute | solution.py:303
  63.1 1.9 %collective-permute-done.14.refs_5_ = bf16[256,128]{1,0:T(8,128)(2,1)S(1)} collective-permute-done((bf16[256,128]{1,0:T(8,128)(2,1)S(1)}, bf16[256,128]{1,0:T(8,128)(2,1)S(1)}, u32[]{:S(2)}, u32[]{:S(2)}) %collective-permute-start.14) | collective-permute-done | bytes 65568 | tf_op jit(solution)/shard_map/ppermute | solution.py:303
  65.0 1.7 %collective-permute-start.18 = (f32[3,64,128]{2,1,0:T(8,128)S(1)}, f32[3,64,128]{2,1,0:T(8,128)S(1)}, u32[]{:S(2)}, u32[]{:S(2)}) collective-permute-start(f32[3,64,128]{2,1,0:T(8,128)S(1)} %constant_dynamic-slice_fusion), channel_id=1, source_target_pairs={{0,8},{8,0},{16,24},{24,16},{1,9},{9,1},{17,25},{25,17},{2,10},{10... | collective-permute-start | bytes 294920 | tf_op jit(solution)/shard_map/ppermute | solution.py:32
  66.7 0.7 collective-permute-start.16
  67.7 0.8 %collective-permute-start.19 = (bf16[3,64,128]{2,1,0:T(8,128)(2,1)S(1)}, bf16[3,64,128]{2,1,0:T(8,128)(2,1)S(1)}, u32[]{:S(2)}, u32[]{:S(2)}) collective-permute-start(bf16[3,64,128]{2,1,0:T(8,128)(2,1)S(1)} %add_convert_fusion.1), channel_id=1, source_target_pairs={{0,16},{8,24},{16,0},{24,8},{1,17},{9,25},{17,1},{25,9},{2,18},{10... | collective-permute-start | bytes 147464 | tf_op jit(solution)/shard_map/ppermute | solution.py:387
  68.4 2.3 %collective-permute-done.16 = bf16[5,64,128]{2,1,0:T(8,128)(2,1)S(1)} collective-permute-done((bf16[5,64,128]{2,1,0:T(8,128)(2,1)S(1)}, bf16[5,64,128]{2,1,0:T(8,128)(2,1)S(1)}, u32[]{:S(2)}, u32[]{:S(2)}) %collective-permute-start.16) | collective-permute-done | bytes 81952 | tf_op jit(solution)/shard_map/ppermute | solution.py:387
  70.7 1.4 %collective-permute-start.17 = (f32[5,64,128]{2,1,0:T(8,128)S(1)}, f32[5,64,128]{2,1,0:T(8,128)S(1)}, u32[]{:S(2)}, u32[]{:S(2)}) collective-permute-start(f32[5,64,128]{2,1,0:T(8,128)S(1)} %convert_add_fusion.refs_0_), channel_id=1, source_target_pairs={{0,8},{8,0},{16,24},{24,16},{1,9},{9,1},{17,25},{25,17},{2,10},{10... | collective-permute-start | bytes 491528 | tf_op jit(solution)/shard_map/ppermute | solution.py:32
  72.7 1.3 %shard_map.66 = bf16[128,1024]{1,0:T(8,128)(2,1)} custom-call(s32[8]{0:T(128)S(1)} %compare_select_fusion.2.where, bf16[1024,128]{1,0:T(8,128)(2,1)S(1)} %shard_map.62.mine, bf16[1024,128]{1,0:T(8,128)(2,1)S(1)} %collective-permute-done.8.refs_0_, bf16[1024,128]{1,0:T(8,128)(2,1)S(1)} %collective-permute-done.9.refs_1_, ...), custom_call_target="tpu_custom_call" | custom-call | tf_op jit(solution)/shard_map/pallas_call | solution.py:352
  74.0 1.4 %shard_map.67 = f32[128,1024]{1,0:T(8,128)} custom-call(s32[8]{0:T(128)S(1)} %compare_select_fusion.2.where, s32[1]{0:T(128)} %bitcast.odd, f32[5,64,128]{2,1,0:T(8,128)S(1)} %convert_add_fusion.refs_0_, f32[5,64,128]{2,1,0:T(8,128)S(1)} %collective-permute-done.17.refs_1_, f32[3,64,128]{2,1,0:T(8,128)S(1)} %convert_add_fusion.1.refs_2_, ...), custom_call_target="tpu_custom_call" | custom-call | tf_op jit(solution)/shard_map/pallas_call | solution.py:361
  (46 shorter events, 3.3 us)
Async XLA Ops:
  0.6 4.7 %copy-start = (bf16[128,1024]{1,0:T(8,128)(2,1)S(1)}, bf16[128,1024]{1,0:T(8,128)(2,1)}, u32[]{:S(2)}) copy-start(bf16[128,1024]{1,0:T(8,128)(2,1)} %param.4) | copy-start | bytes 786436
  0.6 22.2 %collective-permute-start.3 = (bf16[16,64,512]{2,1,0:T(8,128)(2,1)}, bf16[16,64,512]{2,1,0:T(8,128)(2,1)S(1)}, u32[]{:S(2)}, u32[]{:S(2)}) collective-permute-start(bf16[16,64,512]{2,1,0:T(8,128)(2,1)} %tiles.1), channel_id=1, source_target_pairs={{8,16},{16,8},{9,17},{17,9},{10,18},{18,10},{11,19},{19,11},{12,20... | collective-permute-start | bytes 3145736 | tf_op jit(solution)/shard_map/ppermute | solution.py:37
  6.1 13.3 %all-to-all-start = ((bf16[128,8,128]{2,0,1:T(8,128)(2,1)}), bf16[128,8,128]{2,0,1:T(8,128)(2,1)S(1)}, u32[]{:S(2)}, u32[]{:S(2)}) async-start(bf16[128,8,128]{2,0,1:T(8,128)(2,1)} %copy_bitcast_fusion), calls=%async_computation | async-start | bytes 524288 | tf_op jit(solution)/shard_map/all_to_all | solution.py:404
  12.3 1.2 %copy-start.1 = (bf16[16,64,512]{2,1,0:T(8,128)(2,1)S(1)}, bf16[16,64,512]{2,1,0:T(8,128)(2,1)}, u32[]{:S(2)}) copy-start(bf16[16,64,512]{2,1,0:T(8,128)(2,1)} %tiles.1) | copy-start | bytes 3145732
  13.5 0.7 copy-start.2
  16.6 6.3 %collective-permute-start.2 = (bf16[12,64,512]{2,1,0:T(8,128)(2,1)}, bf16[12,64,512]{2,1,0:T(8,128)(2,1)}, u32[]{:S(2)}, u32[]{:S(2)}) collective-permute-start(bf16[12,64,512]{2,1,0:T(8,128)(2,1)} %get-tuple-element.19), channel_id=1, source_target_pairs={{0,8},{8,0},{16,24},{24,16},{1,9},{9,1},{17,25},{25,17},{2,10},{10... | collective-permute-start | bytes 2359304 | tf_op jit(solution)/shard_map/ppermute | solution.py:32
  16.6 2.8 %collective-permute-start = (s32[8,16]{1,0:T(8,128)S(1)}, s32[8,16]{1,0:T(8,128)S(1)}, u32[]{:S(2)}, u32[]{:S(2)}) collective-permute-start(s32[8,16]{1,0:T(8,128)S(1)} %get-tuple-element.18), channel_id=1, source_target_pairs={{0,8},{8,0},{16,24},{24,16},{1,9},{9,1},{17,25},{25,17},{2,10},{10... | collective-permute-start | bytes 1544 | tf_op jit(solution)/shard_map/ppermute | solution.py:32
  17.1 5.7 %collective-permute-start.1 = (s32[8,16]{1,0:T(8,128)S(1)}, s32[8,16]{1,0:T(8,128)S(1)}, u32[]{:S(2)}, u32[]{:S(2)}) collective-permute-start(s32[8,16]{1,0:T(8,128)S(1)} %get-tuple-element.18), channel_id=1, source_target_pairs={{8,16},{16,8},{9,17},{17,9},{10,18},{18,10},{11,19},{19,11},{12,20... | collective-permute-start | bytes 1544 | tf_op jit(solution)/shard_map/ppermute | solution.py:37
  19.3 5.9 %collective-permute-start.4 = (bf16[1024,128]{1,0:T(8,128)(2,1)S(1)}, bf16[1024,128]{1,0:T(8,128)(2,1)S(1)}, u32[]{:S(2)}, u32[]{:S(2)}) collective-permute-start(bf16[1024,128]{1,0:T(8,128)(2,1)S(1)} %bitcast.17), channel_id=1, source_target_pairs={{0,8},{8,0},{16,24},{24,16},{1,9},{9,1},{17,25},{25,17},{2,10},{10... | collective-permute-start | bytes 786440 | tf_op jit(solution)/shard_map/ppermute | solution.py:32
  19.4 7.7 %collective-permute-start.5 = (bf16[1024,128]{1,0:T(8,128)(2,1)S(1)}, bf16[1024,128]{1,0:T(8,128)(2,1)S(1)}, u32[]{:S(2)}, u32[]{:S(2)}) collective-permute-start(bf16[1024,128]{1,0:T(8,128)(2,1)S(1)} %bitcast.18), channel_id=1, source_target_pairs={{8,16},{16,8},{9,17},{17,9},{10,18},{18,10},{11,19},{19,11},{12,20... | collective-permute-start | bytes 786440 | tf_op jit(solution)/shard_map/ppermute | solution.py:37
  30.3 3.5 %collective-permute-start.6 = (bf16[1536,128]{1,0:T(8,128)(2,1)S(1)}, bf16[1536,128]{1,0:T(8,128)(2,1)S(1)}, u32[]{:S(2)}, u32[]{:S(2)}) collective-permute-start(bf16[1536,128]{1,0:T(8,128)(2,1)S(1)} %get-tuple-element.22), channel_id=1, source_target_pairs={{0,8},{8,0},{16,24},{24,16},{1,9},{9,1},{17,25},{25,17},{2,10},{10... | collective-permute-start | bytes 1179656 | tf_op jit(solution)/shard_map/ppermute | solution.py:32
  30.4 9.4 %collective-permute-start.7 = (bf16[1536,128]{1,0:T(8,128)(2,1)S(1)}, bf16[1536,128]{1,0:T(8,128)(2,1)S(1)}, u32[]{:S(2)}, u32[]{:S(2)}) collective-permute-start(bf16[1536,128]{1,0:T(8,128)(2,1)S(1)} %get-tuple-element.22), channel_id=1, source_target_pairs={{8,16},{16,8},{9,17},{17,9},{10,18},{18,10},{11,19},{19,11},{12,20... | collective-permute-start | bytes 1179656 | tf_op jit(solution)/shard_map/ppermute | solution.py:37
  39.8 7.6 %copy-start.3 = (s32[8]{0:T(128)S(1)}, s32[8]{0:T(128)}, u32[]{:S(2)}) copy-start(s32[8]{0:T(128)} %constant.68.clone) | copy-start | bytes 100
  43.2 6.6 %collective-permute-start.8 = (bf16[1024,128]{1,0:T(8,128)(2,1)S(1)}, bf16[1024,128]{1,0:T(8,128)(2,1)S(1)}, u32[]{:S(2)}, u32[]{:S(2)}) collective-permute-start(bf16[1024,128]{1,0:T(8,128)(2,1)S(1)} %shard_map.62.mine), channel_id=1, source_target_pairs={{0,2},{2,4},{4,6},{6,7},{7,5},{5,3},{3,1},{1,0},{8,10},{10,12},{12... | collective-permute-start | bytes 786440 | tf_op jit(solution)/shard_map/ppermute | solution.py:303
  45.0 7.0 %collective-permute-start.9 = (bf16[1024,128]{1,0:T(8,128)(2,1)S(1)}, bf16[1024,128]{1,0:T(8,128)(2,1)S(1)}, u32[]{:S(2)}, u32[]{:S(2)}) collective-permute-start(bf16[1024,128]{1,0:T(8,128)(2,1)S(1)} %shard_map.62.mine), channel_id=1, source_target_pairs={{0,1},{2,0},{4,2},{6,4},{7,6},{5,7},{3,5},{1,3},{8,9},{10,8},{12,1... | collective-permute-start | bytes 786440 | tf_op jit(solution)/shard_map/ppermute | solution.py:303
  45.0 10.5 %collective-permute-start.10 = (bf16[1024,128]{1,0:T(8,128)(2,1)S(1)}, bf16[1024,128]{1,0:T(8,128)(2,1)S(1)}, u32[]{:S(2)}, u32[]{:S(2)}) collective-permute-start(bf16[1024,128]{1,0:T(8,128)(2,1)S(1)} %shard_map.62.mine), channel_id=1, source_target_pairs={{0,4},{2,6},{4,7},{6,5},{7,3},{5,1},{3,0},{1,2},{8,12},{10,14},{12... | collective-permute-start | bytes 786440 | tf_op jit(solution)/shard_map/ppermute | solution.py:303
  47.4 9.2 %collective-permute-start.11 = (bf16[1024,128]{1,0:T(8,128)(2,1)S(1)}, bf16[1024,128]{1,0:T(8,128)(2,1)S(1)}, u32[]{:S(2)}, u32[]{:S(2)}) collective-permute-start(bf16[1024,128]{1,0:T(8,128)(2,1)S(1)} %shard_map.62.mine), channel_id=1, source_target_pairs={{0,3},{2,1},{4,0},{6,2},{7,4},{5,6},{3,7},{1,5},{8,11},{10,9},{12,... | collective-permute-start | bytes 786440 | tf_op jit(solution)/shard_map/ppermute | solution.py:303
  57.8 3.6 %collective-permute-start.12 = (f32[5,64,128]{2,1,0:T(8,128)S(1)}, f32[5,64,128]{2,1,0:T(8,128)S(1)}, u32[]{:S(2)}, u32[]{:S(2)}) collective-permute-start(f32[5,64,128]{2,1,0:T(8,128)S(1)} %constant_dynamic-slice_fusion.1), channel_id=1, source_target_pairs={{0,8},{8,0},{16,24},{24,16},{1,9},{9,1},{17,25},{25,17},{2,10},{10... | collective-permute-start | bytes 491528 | tf_op jit(solution)/shard_map/ppermute | solution.py:32
  57.8 7.1 %collective-permute-start.15 = (bf16[256,128]{1,0:T(8,128)(2,1)S(1)}, bf16[256,128]{1,0:T(8,128)(2,1)S(1)}, u32[]{:S(2)}, u32[]{:S(2)}) collective-permute-start(bf16[256,128]{1,0:T(8,128)(2,1)S(1)} %get-tuple-element.25._), channel_id=1, source_target_pairs={{0,3},{2,1},{4,0},{6,2},{7,4},{5,6},{3,7},{1,5},{8,11},{10,9},{12,... | collective-permute-start | bytes 196616 | tf_op jit(solution)/shard_map/ppermute | solution.py:303
  59.6 3.5 %collective-permute-start.13 = (bf16[256,128]{1,0:T(8,128)(2,1)S(1)}, bf16[256,128]{1,0:T(8,128)(2,1)S(1)}, u32[]{:S(2)}, u32[]{:S(2)}) collective-permute-start(bf16[256,128]{1,0:T(8,128)(2,1)S(1)} %get-tuple-element.26), channel_id=1, source_target_pairs={{0,2},{2,4},{4,6},{6,7},{7,5},{5,3},{3,1},{1,0},{8,10},{10,12},{12... | collective-permute-start | bytes 196616 | tf_op jit(solution)/shard_map/ppermute | solution.py:303
  61.3 3.7 %collective-permute-start.14 = (bf16[256,128]{1,0:T(8,128)(2,1)S(1)}, bf16[256,128]{1,0:T(8,128)(2,1)S(1)}, u32[]{:S(2)}, u32[]{:S(2)}) collective-permute-start(bf16[256,128]{1,0:T(8,128)(2,1)S(1)} %get-tuple-element.27), channel_id=1, source_target_pairs={{0,1},{2,0},{4,2},{6,4},{7,6},{5,7},{3,5},{1,3},{8,9},{10,8},{12,1... | collective-permute-start | bytes 196616 | tf_op jit(solution)/shard_map/ppermute | solution.py:303
  65.0 2.6 %collective-permute-start.18 = (f32[3,64,128]{2,1,0:T(8,128)S(1)}, f32[3,64,128]{2,1,0:T(8,128)S(1)}, u32[]{:S(2)}, u32[]{:S(2)}) collective-permute-start(f32[3,64,128]{2,1,0:T(8,128)S(1)} %constant_dynamic-slice_fusion), channel_id=1, source_target_pairs={{0,8},{8,0},{16,24},{24,16},{1,9},{9,1},{17,25},{25,17},{2,10},{10... | collective-permute-start | bytes 294920 | tf_op jit(solution)/shard_map/ppermute | solution.py:32
  66.7 4.0 %collective-permute-start.16 = (bf16[5,64,128]{2,1,0:T(8,128)(2,1)S(1)}, bf16[5,64,128]{2,1,0:T(8,128)(2,1)S(1)}, u32[]{:S(2)}, u32[]{:S(2)}) collective-permute-start(bf16[5,64,128]{2,1,0:T(8,128)(2,1)S(1)} %add_convert_fusion), channel_id=1, source_target_pairs={{0,16},{8,24},{16,0},{24,8},{1,17},{9,25},{17,1},{25,9},{2,18},{10... | collective-permute-start | bytes 245768 | tf_op jit(solution)/shard_map/ppermute | solution.py:387
  67.7 4.5 %collective-permute-start.19 = (bf16[3,64,128]{2,1,0:T(8,128)(2,1)S(1)}, bf16[3,64,128]{2,1,0:T(8,128)(2,1)S(1)}, u32[]{:S(2)}, u32[]{:S(2)}) collective-permute-start(bf16[3,64,128]{2,1,0:T(8,128)(2,1)S(1)} %add_convert_fusion.1), channel_id=1, source_target_pairs={{0,16},{8,24},{16,0},{24,8},{1,17},{9,25},{17,1},{25,9},{2,18},{10... | collective-permute-start | bytes 147464 | tf_op jit(solution)/shard_map/ppermute | solution.py:387
  70.7 3.3 %collective-permute-start.17 = (f32[5,64,128]{2,1,0:T(8,128)S(1)}, f32[5,64,128]{2,1,0:T(8,128)S(1)}, u32[]{:S(2)}, u32[]{:S(2)}) collective-permute-start(f32[5,64,128]{2,1,0:T(8,128)S(1)} %convert_add_fusion.refs_0_), channel_id=1, source_target_pairs={{0,8},{8,0},{16,24},{24,16},{1,9},{9,1},{17,25},{25,17},{2,10},{10... | collective-permute-start | bytes 491528 | tf_op jit(solution)/shard_map/ppermute | solution.py:32
  72.1 1.9 %collective-permute-start.20 = (f32[3,64,128]{2,1,0:T(8,128)S(1)}, f32[3,64,128]{2,1,0:T(8,128)S(1)}, u32[]{:S(2)}, u32[]{:S(2)}) collective-permute-start(f32[3,64,128]{2,1,0:T(8,128)S(1)} %convert_add_fusion.1.refs_2_), channel_id=1, source_target_pairs={{0,8},{8,0},{16,24},{24,16},{1,9},{9,1},{17,25},{25,17},{2,10},{10... | collective-permute-start | bytes 294920 | tf_op jit(solution)/shard_map/ppermute | solution.py:32

commit v7 on v6

--- a/solution.py
+++ b/solution.py
@@ -127,11 +127,11 @@
         copy.wait()
 
 
-def own_bands(odd, offsets, columns, tiles, bands, to_first, columns_out, doubled, slot):
+def own_bands(odd, offsets, to_send, tiles, bands, to_first, offsets_out, doubled, slot):
     count = tiles.shape[0]
     sent = to_first.shape[0]
     to_first[...] = tiles[pl.ds((1 - odd[0]) * (count - sent), sent)]
-    columns_out[...] = columns[...]
+    offsets_out[...] = to_send[...]
     clear(doubled)
 
     @pl.loop(0, count // HALO)
@@ -408,14 +408,13 @@
     block_columns = block_columns.T
     inner = jnp.arange(count, dtype=jnp.int32)
 
-    def offsets_of(columns, part):
-        return jnp.clip(columns - (part * count + inner), -HALO, HALO)
+    offsets = block_columns - (row_part * count + inner)
 
     scratch = [
         pltpu.VMEM((HALO, kt + 1, tile, 2 * tile), jnp.bfloat16),
         pltpu.SMEM((HALO, 2 * HALO + 1), jnp.int32),
     ]
-    bands, to_first, sent_columns = pl.pallas_call(
+    bands, to_first, sent_offsets = pl.pallas_call(
         own_bands,
         out_shape=(
             jax.ShapeDtypeStruct((count // HALO, size, SPAN * size), jnp.bfloat16),
@@ -426,10 +425,10 @@
         out_specs=(VMEM,) * 3,
         scratch_shapes=scratch,
         compiler_params=params(16),
-    )(odd[None], offsets_of(block_columns, row_part), block_columns, tile_values)
+    )(odd[None], offsets, offsets, tile_values)
     first = with_core(to_first)
-    at_first = with_core(sent_columns)
-    at_second = with_chip(sent_columns)
+    at_first = with_core(sent_offsets)
+    at_second = with_chip(sent_offsets)
     edges = pl.pallas_call(
         edge_bands,
         out_shape=jax.ShapeDtypeStruct(
@@ -441,8 +440,8 @@
         compiler_params=params(16),
     )(
         odd[None],
-        offsets_of(at_first, row_part ^ 1),
-        offsets_of(at_second, row_part - 1 + 2 * odd),
+        jnp.clip(at_first, -HALO, HALO),
+        jnp.clip(at_second, -HALO, HALO),
         first,
         second,
     )

time: 75.8 us -> 75.1 us (level)
  starting transfers between devices: 32.6 us -> 31 us
  waiting for transfers between devices: 22.8 us -> 24.4 us
    ppermute x4, starting transfers between devices: 13.6 us -> 12.3 us  [with_chip(): lax.ppermute(value, 'rows', [p for k in odds for p in ((k, k + 1), (k + 1...]
    ppermute x4, waiting for transfers between devices: 7.9 us -> 9.14 us  [with_chip(): lax.ppermute(value, 'rows', [p for k in odds for p in ((k, k + 1), (k + 1...]
    unnamed x8 -> x6, local copies, waits for them, and re-layouts: 1.92 us -> 1.24 us
  transfers between devices with their start and end apart: 22 -> 22, of which waited for: 10 -> 11; matrix products, arithmetic and copies ran while one was open for 2% -> 2% of each run, Pallas kernels for 9% -> 9%
where the time goes in v7:
time: 75.1 us; the launch traced here: 74.7 us
  starting transfers between devices  31 us (41%)
  waiting for transfers between devices  24.4 us (32%)
  Pallas kernels  15.6 us (21%)
  local copies, waits for them, and re-layouts  2.03 us (3%)
  between operations  0.85 us (1%)
  other arithmetic  0.81 us (1%)
    ppermute x4, starting transfers between devices, with_chip(): lax.ppermute(value, 'rows', [p for k in odds for p in ((k, k + 1), (k + 1...  12.3 us
    ppermute x7, waiting for transfers between devices, move(): lax.ppermute(value, 'cols', [(order[i], order[(i + by) % size]) for i in...  12 us
    ppermute x4, waiting for transfers between devices, with_chip(): lax.ppermute(value, 'rows', [p for k in odds for p in ((k, k + 1), (k + 1...  9.14 us
    ppermute x7, starting transfers between devices, move(): lax.ppermute(value, 'cols', [(order[i], order[(i + by) % size]) for i in...  7.37 us
    all_to_all x1, starting transfers between devices, per_device(): lax.all_to_all(search_vectors, 'cols', split_axis=1, concat_axis=0, tiled...  5.55 us
    ppermute x8, starting transfers between devices, with_core(): lax.ppermute(value, 'rows', [(i, i ^ 1) for i in range(lax.axis_size('row...  4.26 us
    pallas_call x1, Pallas kernels, per_device(): pl.pallas_call(second_stage, out_shape=jax.ShapeDtypeStruct((rows, width)...  3.38 us
    pallas_call x1, Pallas kernels, per_device(): pl.pallas_call(first_stage, out_shape=(jax.ShapeDtypeStruct((rows, width)...  3.24 us
  transfers between devices with their start and end apart: 22, of which 11 were waited for; matrix products, arithmetic and copies ran while one was open for 2% of the time, Pallas kernels for 9%

profile of v7, /device:TPU:1, one launch (start us, length us, event | category | flops | bytes accessed | tf_op | source)
XLA Modules:
  0.0 74.7 jit_solution(16967388180634683565)
XLA Ops:
  0.6 4.6 %collective-permute-start.3 = (bf16[16,64,512]{2,1,0:T(8,128)(2,1)}, bf16[16,64,512]{2,1,0:T(8,128)(2,1)S(1)}, u32[]{:S(2)}, u32[]{:S(2)}) collective-permute-start(bf16[16,64,512]{2,1,0:T(8,128)(2,1)} %tiles.1), channel_id=1, source_target_pairs={{8,16},{16,8},{9,17},{17,9},{10,18},{18,10},{11,19},{19,11},{12,20... | collective-permute-start | bytes 3145736 | tf_op jit(solution)/shard_map/ppermute | solution.py:37
  5.3 0.8 %copy_bitcast_fusion = bf16[128,8,128]{2,0,1:T(8,128)(2,1)} fusion(bf16[128,1024]{1,0:T(8,128)(2,1)S(1)} %copy-done), kind=kLoop, calls=%fused_computation | loop fusion | bytes 524288 | tf_op jit(solution)/shard_map/all_to_all | solution.py:404
  6.1 5.6 %all-to-all-start = ((bf16[128,8,128]{2,0,1:T(8,128)(2,1)}), bf16[128,8,128]{2,0,1:T(8,128)(2,1)S(1)}, u32[]{:S(2)}, u32[]{:S(2)}) async-start(bf16[128,8,128]{2,0,1:T(8,128)(2,1)} %copy_bitcast_fusion), calls=%async_computation | async-start | bytes 524288 | tf_op jit(solution)/shard_map/all_to_all | solution.py:404
  12.3 1.2 %copy-done.1 = bf16[16,64,512]{2,1,0:T(8,128)(2,1)S(1)} copy-done((bf16[16,64,512]{2,1,0:T(8,128)(2,1)S(1)}, bf16[16,64,512]{2,1,0:T(8,128)(2,1)}, u32[]{:S(2)}) %copy-start.1) | copy-done | bytes 1048600
  13.5 2.4 %shard_map.59 = (bf16[4,256,768]{2,1,0:T(8,128)(2,1)S(1)}, bf16[12,64,512]{2,1,0:T(8,128)(2,1)}, s32[8,16]{1,0:T(8,128)S(1)}) custom-call(s32[1]{0:T(128)} %bitcast.odd, s32[8,16]{1,0:T(8,128)S(1)} %subtract_bitcast_fusion.offsets.to_send, s32[8,16]{1,0:T(8,128)S(1)} %subtract_bitcast_fusion.offsets.to_send, bf16[16,64,512]{2,1,0:T(8,128)(2,1)S(1)} %copy-done.1), custom_call_target="tpu_custom_call" | custom-call | tf_op jit(solution)/shard_map/pallas_call | solution.py:417
  16.4 2.2 %collective-permute-start.1 = (s32[8,16]{1,0:T(8,128)S(1)}, s32[8,16]{1,0:T(8,128)S(1)}, u32[]{:S(2)}, u32[]{:S(2)}) collective-permute-start(s32[8,16]{1,0:T(8,128)S(1)} %get-tuple-element.18), channel_id=1, source_target_pairs={{8,16},{16,8},{9,17},{17,9},{10,18},{18,10},{11,19},{19,11},{12,20... | collective-permute-start | bytes 1544 | tf_op jit(solution)/shard_map/ppermute | solution.py:37
  18.6 0.7 all-to-all-done
  19.3 2.7 %collective-permute-start.5 = (bf16[1024,128]{1,0:T(8,128)(2,1)S(1)}, bf16[1024,128]{1,0:T(8,128)(2,1)S(1)}, u32[]{:S(2)}, u32[]{:S(2)}) collective-permute-start(bf16[1024,128]{1,0:T(8,128)(2,1)S(1)} %bitcast.18), channel_id=1, source_target_pairs={{8,16},{16,8},{9,17},{17,9},{10,18},{18,10},{11,19},{19,11},{12,20... | collective-permute-start | bytes 786440 | tf_op jit(solution)/shard_map/ppermute | solution.py:37
  22.1 2.4 %shard_map.60.edges = bf16[6,256,768]{2,1,0:T(8,128)(2,1)S(1)} custom-call(s32[1]{0:T(128)} %bitcast.odd, s32[8,16]{1,0:T(8,128)S(1)} %broadcast_clamp_fusion.1.at_first, s32[8,16]{1,0:T(8,128)S(1)} %broadcast_clamp_fusion.at_second, bf16[12,64,512]{2,1,0:T(8,128)(2,1)} %collective-permute-done.2.first, bf16[16,64,512]{2,1,0:T(8,128)(2,1)S(1)} %collective-permute-done.3.second), custom_call_target="tpu_custom_call" | custom-call | tf_op jit(solution)/shard_map/pallas_call | solution.py:432
  24.5 2.5 %collective-permute-done.5.x_second = bf16[1024,128]{1,0:T(8,128)(2,1)S(1)} collective-permute-done((bf16[1024,128]{1,0:T(8,128)(2,1)S(1)}, bf16[1024,128]{1,0:T(8,128)(2,1)S(1)}, u32[]{:S(2)}, u32[]{:S(2)}) %collective-permute-start.5) | collective-permute-done | bytes 262176 | tf_op jit(solution)/shard_map/ppermute | solution.py:37
  27.0 3.2 %shard_map.61 = (f32[1024,128]{1,0:T(8,128)S(1)}, f32[1536,128]{1,0:T(8,128)S(1)}, bf16[1536,128]{1,0:T(8,128)(2,1)S(1)}) custom-call(s32[1]{0:T(128)} %bitcast.odd, bf16[4,256,768]{2,1,0:T(8,128)(2,1)S(1)} %get-tuple-element.17.own, bf16[6,256,768]{2,1,0:T(8,128)(2,1)S(1)} %shard_map.60.edges, bf16[1024,128]{1,0:T(8,128)(2,1)S(1)} %collective-permute-done.4.x_first, ...), custom_call_target="tpu_custom_call" | custom-call | tf_op jit(solution)/shard_map/pallas_call | solution.py:455
  30.3 2.7 %collective-permute-start.7 = (bf16[1536,128]{1,0:T(8,128)(2,1)S(1)}, bf16[1536,128]{1,0:T(8,128)(2,1)S(1)}, u32[]{:S(2)}, u32[]{:S(2)}) collective-permute-start(bf16[1536,128]{1,0:T(8,128)(2,1)S(1)} %get-tuple-element.22), channel_id=1, source_target_pairs={{8,16},{16,8},{9,17},{17,9},{10,18},{18,10},{11,19},{19,11},{12,20... | collective-permute-start | bytes 1179656 | tf_op jit(solution)/shard_map/ppermute | solution.py:37
  33.1 6.6 %collective-permute-done.7.got_second = bf16[1536,128]{1,0:T(8,128)(2,1)S(1)} collective-permute-done((bf16[1536,128]{1,0:T(8,128)(2,1)S(1)}, bf16[1536,128]{1,0:T(8,128)(2,1)S(1)}, u32[]{:S(2)}, u32[]{:S(2)}) %collective-permute-start.7) | collective-permute-done | bytes 393248 | tf_op jit(solution)/shard_map/ppermute | solution.py:37
  39.7 3.4 %shard_map.62.mine = bf16[1024,128]{1,0:T(8,128)(2,1)S(1)} custom-call(s32[1]{0:T(128)} %bitcast.odd, bf16[4,256,768]{2,1,0:T(8,128)(2,1)S(1)} %get-tuple-element.17.own, bf16[6,256,768]{2,1,0:T(8,128)(2,1)S(1)} %shard_map.60.edges, f32[1024,128]{1,0:T(8,128)S(1)} %get-tuple-element.20.now, f32[1536,128]{1,0:T(8,128)S(1)} %get-tuple-element.21.last, ...), custom_call_target="tpu_custom_call" | custom-call | tf_op jit(solution)/shard_map/pallas_call | solution.py:469
  43.1 1.2 %collective-permute-start.8 = (bf16[1024,128]{1,0:T(8,128)(2,1)S(1)}, bf16[1024,128]{1,0:T(8,128)(2,1)S(1)}, u32[]{:S(2)}, u32[]{:S(2)}) collective-permute-start(bf16[1024,128]{1,0:T(8,128)(2,1)S(1)} %shard_map.62.mine), channel_id=1, source_target_pairs={{0,2},{2,4},{4,6},{6,7},{7,5},{5,3},{3,1},{1,0},{8,10},{10,12},{12... | collective-permute-start | bytes 786440 | tf_op jit(solution)/shard_map/ppermute | solution.py:303
  44.6 2.0 %collective-permute-start.10 = (bf16[1024,128]{1,0:T(8,128)(2,1)S(1)}, bf16[1024,128]{1,0:T(8,128)(2,1)S(1)}, u32[]{:S(2)}, u32[]{:S(2)}) collective-permute-start(bf16[1024,128]{1,0:T(8,128)(2,1)S(1)} %shard_map.62.mine), channel_id=1, source_target_pairs={{0,4},{2,6},{4,7},{6,5},{7,3},{5,1},{3,0},{1,2},{8,12},{10,14},{12... | collective-permute-start | bytes 786440 | tf_op jit(solution)/shard_map/ppermute | solution.py:303
  47.0 2.1 %collective-permute-done.8.refs_0_ = bf16[1024,128]{1,0:T(8,128)(2,1)S(1)} collective-permute-done((bf16[1024,128]{1,0:T(8,128)(2,1)S(1)}, bf16[1024,128]{1,0:T(8,128)(2,1)S(1)}, u32[]{:S(2)}, u32[]{:S(2)}) %collective-permute-start.8) | collective-permute-done | bytes 262176 | tf_op jit(solution)/shard_map/ppermute | solution.py:303
  49.1 2.1 %collective-permute-done.9.refs_1_ = bf16[1024,128]{1,0:T(8,128)(2,1)S(1)} collective-permute-done((bf16[1024,128]{1,0:T(8,128)(2,1)S(1)}, bf16[1024,128]{1,0:T(8,128)(2,1)S(1)}, u32[]{:S(2)}, u32[]{:S(2)}) %collective-permute-start.9) | collective-permute-done | bytes 262176 | tf_op jit(solution)/shard_map/ppermute | solution.py:303
  51.6 3.2 %collective-permute-done.10.back.refs_2_ = bf16[1024,128]{1,0:T(8,128)(2,1)S(1)} collective-permute-done((bf16[1024,128]{1,0:T(8,128)(2,1)S(1)}, bf16[1024,128]{1,0:T(8,128)(2,1)S(1)}, u32[]{:S(2)}, u32[]{:S(2)}) %collective-permute-start.10) | collective-permute-done | bytes 262176 | tf_op jit(solution)/shard_map/ppermute | solution.py:303
  54.9 0.9 %collective-permute-done.11.front.refs_3_ = bf16[1024,128]{1,0:T(8,128)(2,1)S(1)} collective-permute-done((bf16[1024,128]{1,0:T(8,128)(2,1)S(1)}, bf16[1024,128]{1,0:T(8,128)(2,1)S(1)}, u32[]{:S(2)}, u32[]{:S(2)}) %collective-permute-start.11) | collective-permute-done | bytes 262176 | tf_op jit(solution)/shard_map/ppermute | solution.py:303
  55.8 0.9 %shard_map.64 = (bf16[256,128]{1,0:T(8,128)(2,1)S(1)}, bf16[256,128]{1,0:T(8,128)(2,1)S(1)}, bf16[256,128]{1,0:T(8,128)(2,1)S(1)}) custom-call(s32[8]{0:T(128)S(1)} %compare_select_fusion.2.where, bf16[3,128,1024]{2,1,0:T(8,128)(2,1)S(1)} %get-tuple-element.23.lefts, bf16[1024,128]{1,0:T(8,128)(2,1)S(1)} %collective-permute-done.10.back.refs_2_, ...), custom_call_target="tpu_custom_call" | custom-call | tf_op jit(solution)/shard_map/pallas_call | solution.py:331
  57.1 1.8 %collective-permute-start.15 = (bf16[256,128]{1,0:T(8,128)(2,1)S(1)}, bf16[256,128]{1,0:T(8,128)(2,1)S(1)}, u32[]{:S(2)}, u32[]{:S(2)}) collective-permute-start(bf16[256,128]{1,0:T(8,128)(2,1)S(1)} %get-tuple-element.25._), channel_id=1, source_target_pairs={{0,3},{2,1},{4,0},{6,2},{7,4},{5,6},{3,7},{1,5},{8,11},{10,9},{12,... | collective-permute-start | bytes 196616 | tf_op jit(solution)/shard_map/ppermute | solution.py:303
  58.9 1.7 %collective-permute-start.13 = (bf16[256,128]{1,0:T(8,128)(2,1)S(1)}, bf16[256,128]{1,0:T(8,128)(2,1)S(1)}, u32[]{:S(2)}, u32[]{:S(2)}) collective-permute-start(bf16[256,128]{1,0:T(8,128)(2,1)S(1)} %get-tuple-element.26), channel_id=1, source_target_pairs={{0,2},{2,4},{4,6},{6,7},{7,5},{5,3},{3,1},{1,0},{8,10},{10,12},{12... | collective-permute-start | bytes 196616 | tf_op jit(solution)/shard_map/ppermute | solution.py:303
  60.7 1.7 %collective-permute-done.13.refs_4_ = bf16[256,128]{1,0:T(8,128)(2,1)S(1)} collective-permute-done((bf16[256,128]{1,0:T(8,128)(2,1)S(1)}, bf16[256,128]{1,0:T(8,128)(2,1)S(1)}, u32[]{:S(2)}, u32[]{:S(2)}) %collective-permute-start.13) | collective-permute-done | bytes 65568 | tf_op jit(solution)/shard_map/ppermute | solution.py:303
  62.4 1.9 %collective-permute-done.14.refs_5_ = bf16[256,128]{1,0:T(8,128)(2,1)S(1)} collective-permute-done((bf16[256,128]{1,0:T(8,128)(2,1)S(1)}, bf16[256,128]{1,0:T(8,128)(2,1)S(1)}, u32[]{:S(2)}, u32[]{:S(2)}) %collective-permute-start.14) | collective-permute-done | bytes 65568 | tf_op jit(solution)/shard_map/ppermute | solution.py:303
  64.3 1.7 %collective-permute-start.18 = (f32[3,64,128]{2,1,0:T(8,128)S(1)}, f32[3,64,128]{2,1,0:T(8,128)S(1)}, u32[]{:S(2)}, u32[]{:S(2)}) collective-permute-start(f32[3,64,128]{2,1,0:T(8,128)S(1)} %constant_dynamic-slice_fusion), channel_id=1, source_target_pairs={{0,8},{8,0},{16,24},{24,16},{1,9},{9,1},{17,25},{25,17},{2,10},{10... | collective-permute-start | bytes 294920 | tf_op jit(solution)/shard_map/ppermute | solution.py:32
  66.0 0.7 collective-permute-start.16
  66.9 0.8 %collective-permute-start.19 = (bf16[3,64,128]{2,1,0:T(8,128)(2,1)S(1)}, bf16[3,64,128]{2,1,0:T(8,128)(2,1)S(1)}, u32[]{:S(2)}, u32[]{:S(2)}) collective-permute-start(bf16[3,64,128]{2,1,0:T(8,128)(2,1)S(1)} %add_convert_fusion.1), channel_id=1, source_target_pairs={{0,16},{8,24},{16,0},{24,8},{1,17},{9,25},{17,1},{25,9},{2,18},{10... | collective-permute-start | bytes 147464 | tf_op jit(solution)/shard_map/ppermute | solution.py:387
  67.7 2.3 %collective-permute-done.16 = bf16[5,64,128]{2,1,0:T(8,128)(2,1)S(1)} collective-permute-done((bf16[5,64,128]{2,1,0:T(8,128)(2,1)S(1)}, bf16[5,64,128]{2,1,0:T(8,128)(2,1)S(1)}, u32[]{:S(2)}, u32[]{:S(2)}) %collective-permute-start.16) | collective-permute-done | bytes 81952 | tf_op jit(solution)/shard_map/ppermute | solution.py:387
  70.0 1.4 %collective-permute-start.17 = (f32[5,64,128]{2,1,0:T(8,128)S(1)}, f32[5,64,128]{2,1,0:T(8,128)S(1)}, u32[]{:S(2)}, u32[]{:S(2)}) collective-permute-start(f32[5,64,128]{2,1,0:T(8,128)S(1)} %convert_add_fusion.refs_0_), channel_id=1, source_target_pairs={{0,8},{8,0},{16,24},{24,16},{1,9},{9,1},{17,25},{25,17},{2,10},{10... | collective-permute-start | bytes 491528 | tf_op jit(solution)/shard_map/ppermute | solution.py:32
  72.0 1.3 %shard_map.66 = bf16[128,1024]{1,0:T(8,128)(2,1)} custom-call(s32[8]{0:T(128)S(1)} %compare_select_fusion.2.where, bf16[1024,128]{1,0:T(8,128)(2,1)S(1)} %shard_map.62.mine, bf16[1024,128]{1,0:T(8,128)(2,1)S(1)} %collective-permute-done.8.refs_0_, bf16[1024,128]{1,0:T(8,128)(2,1)S(1)} %collective-permute-done.9.refs_1_, ...), custom_call_target="tpu_custom_call" | custom-call | tf_op jit(solution)/shard_map/pallas_call | solution.py:352
  73.3 1.4 %shard_map.67 = f32[128,1024]{1,0:T(8,128)} custom-call(s32[8]{0:T(128)S(1)} %compare_select_fusion.2.where, s32[1]{0:T(128)} %bitcast.odd, f32[5,64,128]{2,1,0:T(8,128)S(1)} %convert_add_fusion.refs_0_, f32[5,64,128]{2,1,0:T(8,128)S(1)} %collective-permute-done.17.refs_1_, f32[3,64,128]{2,1,0:T(8,128)S(1)} %convert_add_fusion.1.refs_2_, ...), custom_call_target="tpu_custom_call" | custom-call | tf_op jit(solution)/shard_map/pallas_call | solution.py:361
  (42 shorter events, 3.8 us)
Async XLA Ops:
  0.6 4.7 %copy-start = (bf16[128,1024]{1,0:T(8,128)(2,1)S(1)}, bf16[128,1024]{1,0:T(8,128)(2,1)}, u32[]{:S(2)}) copy-start(bf16[128,1024]{1,0:T(8,128)(2,1)} %param.4) | copy-start | bytes 786436
  0.6 21.5 %collective-permute-start.3 = (bf16[16,64,512]{2,1,0:T(8,128)(2,1)}, bf16[16,64,512]{2,1,0:T(8,128)(2,1)S(1)}, u32[]{:S(2)}, u32[]{:S(2)}) collective-permute-start(bf16[16,64,512]{2,1,0:T(8,128)(2,1)} %tiles.1), channel_id=1, source_target_pairs={{8,16},{16,8},{9,17},{17,9},{10,18},{18,10},{11,19},{19,11},{12,20... | collective-permute-start | bytes 3145736 | tf_op jit(solution)/shard_map/ppermute | solution.py:37
  6.1 13.3 %all-to-all-start = ((bf16[128,8,128]{2,0,1:T(8,128)(2,1)}), bf16[128,8,128]{2,0,1:T(8,128)(2,1)S(1)}, u32[]{:S(2)}, u32[]{:S(2)}) async-start(bf16[128,8,128]{2,0,1:T(8,128)(2,1)} %copy_bitcast_fusion), calls=%async_computation | async-start | bytes 524288 | tf_op jit(solution)/shard_map/all_to_all | solution.py:404
  12.3 1.2 %copy-start.1 = (bf16[16,64,512]{2,1,0:T(8,128)(2,1)S(1)}, bf16[16,64,512]{2,1,0:T(8,128)(2,1)}, u32[]{:S(2)}) copy-start(bf16[16,64,512]{2,1,0:T(8,128)(2,1)} %tiles.1) | copy-start | bytes 3145732
  15.9 6.2 %collective-permute-start.2 = (bf16[12,64,512]{2,1,0:T(8,128)(2,1)}, bf16[12,64,512]{2,1,0:T(8,128)(2,1)}, u32[]{:S(2)}, u32[]{:S(2)}) collective-permute-start(bf16[12,64,512]{2,1,0:T(8,128)(2,1)} %get-tuple-element.19), channel_id=1, source_target_pairs={{0,8},{8,0},{16,24},{24,16},{1,9},{9,1},{17,25},{25,17},{2,10},{10... | collective-permute-start | bytes 2359304 | tf_op jit(solution)/shard_map/ppermute | solution.py:32
  15.9 3.4 %collective-permute-start = (s32[8,16]{1,0:T(8,128)S(1)}, s32[8,16]{1,0:T(8,128)S(1)}, u32[]{:S(2)}, u32[]{:S(2)}) collective-permute-start(s32[8,16]{1,0:T(8,128)S(1)} %get-tuple-element.18), channel_id=1, source_target_pairs={{0,8},{8,0},{16,24},{24,16},{1,9},{9,1},{17,25},{25,17},{2,10},{10... | collective-permute-start | bytes 1544 | tf_op jit(solution)/shard_map/ppermute | solution.py:32
  16.4 5.7 %collective-permute-start.1 = (s32[8,16]{1,0:T(8,128)S(1)}, s32[8,16]{1,0:T(8,128)S(1)}, u32[]{:S(2)}, u32[]{:S(2)}) collective-permute-start(s32[8,16]{1,0:T(8,128)S(1)} %get-tuple-element.18), channel_id=1, source_target_pairs={{8,16},{16,8},{9,17},{17,9},{10,18},{18,10},{11,19},{19,11},{12,20... | collective-permute-start | bytes 1544 | tf_op jit(solution)/shard_map/ppermute | solution.py:37
  19.3 5.2 %collective-permute-start.4 = (bf16[1024,128]{1,0:T(8,128)(2,1)S(1)}, bf16[1024,128]{1,0:T(8,128)(2,1)S(1)}, u32[]{:S(2)}, u32[]{:S(2)}) collective-permute-start(bf16[1024,128]{1,0:T(8,128)(2,1)S(1)} %bitcast.17), channel_id=1, source_target_pairs={{0,8},{8,0},{16,24},{24,16},{1,9},{9,1},{17,25},{25,17},{2,10},{10... | collective-permute-start | bytes 786440 | tf_op jit(solution)/shard_map/ppermute | solution.py:32
  19.3 7.7 %collective-permute-start.5 = (bf16[1024,128]{1,0:T(8,128)(2,1)S(1)}, bf16[1024,128]{1,0:T(8,128)(2,1)S(1)}, u32[]{:S(2)}, u32[]{:S(2)}) collective-permute-start(bf16[1024,128]{1,0:T(8,128)(2,1)S(1)} %bitcast.18), channel_id=1, source_target_pairs={{8,16},{16,8},{9,17},{17,9},{10,18},{18,10},{11,19},{19,11},{12,20... | collective-permute-start | bytes 786440 | tf_op jit(solution)/shard_map/ppermute | solution.py:37
  30.2 2.8 %collective-permute-start.6 = (bf16[1536,128]{1,0:T(8,128)(2,1)S(1)}, bf16[1536,128]{1,0:T(8,128)(2,1)S(1)}, u32[]{:S(2)}, u32[]{:S(2)}) collective-permute-start(bf16[1536,128]{1,0:T(8,128)(2,1)S(1)} %get-tuple-element.22), channel_id=1, source_target_pairs={{0,8},{8,0},{16,24},{24,16},{1,9},{9,1},{17,25},{25,17},{2,10},{10... | collective-permute-start | bytes 1179656 | tf_op jit(solution)/shard_map/ppermute | solution.py:32
  30.3 9.4 %collective-permute-start.7 = (bf16[1536,128]{1,0:T(8,128)(2,1)S(1)}, bf16[1536,128]{1,0:T(8,128)(2,1)S(1)}, u32[]{:S(2)}, u32[]{:S(2)}) collective-permute-start(bf16[1536,128]{1,0:T(8,128)(2,1)S(1)} %get-tuple-element.22), channel_id=1, source_target_pairs={{8,16},{16,8},{9,17},{17,9},{10,18},{18,10},{11,19},{19,11},{12,20... | collective-permute-start | bytes 1179656 | tf_op jit(solution)/shard_map/ppermute | solution.py:37
  39.7 7.3 %copy-start.2 = (s32[8]{0:T(128)S(1)}, s32[8]{0:T(128)}, u32[]{:S(2)}) copy-start(s32[8]{0:T(128)} %constant.67.clone) | copy-start | bytes 100
  43.1 6.0 %collective-permute-start.8 = (bf16[1024,128]{1,0:T(8,128)(2,1)S(1)}, bf16[1024,128]{1,0:T(8,128)(2,1)S(1)}, u32[]{:S(2)}, u32[]{:S(2)}) collective-permute-start(bf16[1024,128]{1,0:T(8,128)(2,1)S(1)} %shard_map.62.mine), channel_id=1, source_target_pairs={{0,2},{2,4},{4,6},{6,7},{7,5},{5,3},{3,1},{1,0},{8,10},{10,12},{12... | collective-permute-start | bytes 786440 | tf_op jit(solution)/shard_map/ppermute | solution.py:303
  44.3 7.0 %collective-permute-start.9 = (bf16[1024,128]{1,0:T(8,128)(2,1)S(1)}, bf16[1024,128]{1,0:T(8,128)(2,1)S(1)}, u32[]{:S(2)}, u32[]{:S(2)}) collective-permute-start(bf16[1024,128]{1,0:T(8,128)(2,1)S(1)} %shard_map.62.mine), channel_id=1, source_target_pairs={{0,1},{2,0},{4,2},{6,4},{7,6},{5,7},{3,5},{1,3},{8,9},{10,8},{12,1... | collective-permute-start | bytes 786440 | tf_op jit(solution)/shard_map/ppermute | solution.py:303
  44.6 10.3 %collective-permute-start.10 = (bf16[1024,128]{1,0:T(8,128)(2,1)S(1)}, bf16[1024,128]{1,0:T(8,128)(2,1)S(1)}, u32[]{:S(2)}, u32[]{:S(2)}) collective-permute-start(bf16[1024,128]{1,0:T(8,128)(2,1)S(1)} %shard_map.62.mine), channel_id=1, source_target_pairs={{0,4},{2,6},{4,7},{6,5},{7,3},{5,1},{3,0},{1,2},{8,12},{10,14},{12... | collective-permute-start | bytes 786440 | tf_op jit(solution)/shard_map/ppermute | solution.py:303
  46.6 9.2 %collective-permute-start.11 = (bf16[1024,128]{1,0:T(8,128)(2,1)S(1)}, bf16[1024,128]{1,0:T(8,128)(2,1)S(1)}, u32[]{:S(2)}, u32[]{:S(2)}) collective-permute-start(bf16[1024,128]{1,0:T(8,128)(2,1)S(1)} %shard_map.62.mine), channel_id=1, source_target_pairs={{0,3},{2,1},{4,0},{6,2},{7,4},{5,6},{3,7},{1,5},{8,11},{10,9},{12,... | collective-permute-start | bytes 786440 | tf_op jit(solution)/shard_map/ppermute | solution.py:303
  57.0 3.6 %collective-permute-start.12 = (f32[5,64,128]{2,1,0:T(8,128)S(1)}, f32[5,64,128]{2,1,0:T(8,128)S(1)}, u32[]{:S(2)}, u32[]{:S(2)}) collective-permute-start(f32[5,64,128]{2,1,0:T(8,128)S(1)} %constant_dynamic-slice_fusion.1), channel_id=1, source_target_pairs={{0,8},{8,0},{16,24},{24,16},{1,9},{9,1},{17,25},{25,17},{2,10},{10... | collective-permute-start | bytes 491528 | tf_op jit(solution)/shard_map/ppermute | solution.py:32
  57.1 7.1 %collective-permute-start.15 = (bf16[256,128]{1,0:T(8,128)(2,1)S(1)}, bf16[256,128]{1,0:T(8,128)(2,1)S(1)}, u32[]{:S(2)}, u32[]{:S(2)}) collective-permute-start(bf16[256,128]{1,0:T(8,128)(2,1)S(1)} %get-tuple-element.25._), channel_id=1, source_target_pairs={{0,3},{2,1},{4,0},{6,2},{7,4},{5,6},{3,7},{1,5},{8,11},{10,9},{12,... | collective-permute-start | bytes 196616 | tf_op jit(solution)/shard_map/ppermute | solution.py:303
  58.9 3.5 %collective-permute-start.13 = (bf16[256,128]{1,0:T(8,128)(2,1)S(1)}, bf16[256,128]{1,0:T(8,128)(2,1)S(1)}, u32[]{:S(2)}, u32[]{:S(2)}) collective-permute-start(bf16[256,128]{1,0:T(8,128)(2,1)S(1)} %get-tuple-element.26), channel_id=1, source_target_pairs={{0,2},{2,4},{4,6},{6,7},{7,5},{5,3},{3,1},{1,0},{8,10},{10,12},{12... | collective-permute-start | bytes 196616 | tf_op jit(solution)/shard_map/ppermute | solution.py:303
  60.6 3.7 %collective-permute-start.14 = (bf16[256,128]{1,0:T(8,128)(2,1)S(1)}, bf16[256,128]{1,0:T(8,128)(2,1)S(1)}, u32[]{:S(2)}, u32[]{:S(2)}) collective-permute-start(bf16[256,128]{1,0:T(8,128)(2,1)S(1)} %get-tuple-element.27), channel_id=1, source_target_pairs={{0,1},{2,0},{4,2},{6,4},{7,6},{5,7},{3,5},{1,3},{8,9},{10,8},{12,1... | collective-permute-start | bytes 196616 | tf_op jit(solution)/shard_map/ppermute | solution.py:303
  64.3 2.6 %collective-permute-start.18 = (f32[3,64,128]{2,1,0:T(8,128)S(1)}, f32[3,64,128]{2,1,0:T(8,128)S(1)}, u32[]{:S(2)}, u32[]{:S(2)}) collective-permute-start(f32[3,64,128]{2,1,0:T(8,128)S(1)} %constant_dynamic-slice_fusion), channel_id=1, source_target_pairs={{0,8},{8,0},{16,24},{24,16},{1,9},{9,1},{17,25},{25,17},{2,10},{10... | collective-permute-start | bytes 294920 | tf_op jit(solution)/shard_map/ppermute | solution.py:32
  66.0 4.0 %collective-permute-start.16 = (bf16[5,64,128]{2,1,0:T(8,128)(2,1)S(1)}, bf16[5,64,128]{2,1,0:T(8,128)(2,1)S(1)}, u32[]{:S(2)}, u32[]{:S(2)}) collective-permute-start(bf16[5,64,128]{2,1,0:T(8,128)(2,1)S(1)} %add_convert_fusion), channel_id=1, source_target_pairs={{0,16},{8,24},{16,0},{24,8},{1,17},{9,25},{17,1},{25,9},{2,18},{10... | collective-permute-start | bytes 245768 | tf_op jit(solution)/shard_map/ppermute | solution.py:387
  66.9 4.5 %collective-permute-start.19 = (bf16[3,64,128]{2,1,0:T(8,128)(2,1)S(1)}, bf16[3,64,128]{2,1,0:T(8,128)(2,1)S(1)}, u32[]{:S(2)}, u32[]{:S(2)}) collective-permute-start(bf16[3,64,128]{2,1,0:T(8,128)(2,1)S(1)} %add_convert_fusion.1), channel_id=1, source_target_pairs={{0,16},{8,24},{16,0},{24,8},{1,17},{9,25},{17,1},{25,9},{2,18},{10... | collective-permute-start | bytes 147464 | tf_op jit(solution)/shard_map/ppermute | solution.py:387
  70.0 3.3 %collective-permute-start.17 = (f32[5,64,128]{2,1,0:T(8,128)S(1)}, f32[5,64,128]{2,1,0:T(8,128)S(1)}, u32[]{:S(2)}, u32[]{:S(2)}) collective-permute-start(f32[5,64,128]{2,1,0:T(8,128)S(1)} %convert_add_fusion.refs_0_), channel_id=1, source_target_pairs={{0,8},{8,0},{16,24},{24,16},{1,9},{9,1},{17,25},{25,17},{2,10},{10... | collective-permute-start | bytes 491528 | tf_op jit(solution)/shard_map/ppermute | solution.py:32
  71.4 1.9 %collective-permute-start.20 = (f32[3,64,128]{2,1,0:T(8,128)S(1)}, f32[3,64,128]{2,1,0:T(8,128)S(1)}, u32[]{:S(2)}, u32[]{:S(2)}) collective-permute-start(f32[3,64,128]{2,1,0:T(8,128)S(1)} %convert_add_fusion.1.refs_2_), channel_id=1, source_target_pairs={{0,8},{8,0},{16,24},{24,16},{1,9},{9,1},{17,25},{25,17},{2,10},{10... | collective-permute-start | bytes 294920 | tf_op jit(solution)/shard_map/ppermute | solution.py:32

commit v8 on v7

--- a/solution.py
+++ b/solution.py
@@ -348,7 +348,7 @@
 
     flat = width % 128 == 0
     shape = (lambda n: (n, size * width)) if flat else (lambda n: (size, n, width))
-    far = sum_of_cores(far)
+    far, messages = lax.optimization_barrier((sum_of_cores(far), messages))
     rowwise = pl.pallas_call(
         functools.partial(filtered_rows, len(blocks)),
         out_shape=jax.ShapeDtypeStruct(shape(share), mine.dtype),
@@ -356,8 +356,8 @@
         out_specs=VMEM,
         compiler_params=params(16),
     )(where, mine, *blocks, *messages)
-    own = sum_of_chips(own)
-    far = sum_of_chips(far)
+    own, _ = sum_of_chips(own)
+    far, rowwise = sum_of_chips(far, rowwise)
     gram = pl.pallas_call(
         functools.partial(place_blocks, 1.0 / (rows * lax.axis_size("rows"))),
         out_shape=jax.ShapeDtypeStruct(shape(width), jnp.float32),
@@ -379,16 +379,18 @@
     return (keep + with_core(give)).astype(jnp.bfloat16)
 
 
-def sum_of_chips(sent):
+def sum_of_chips(sent, beside=None):
     size = lax.axis_size("rows")
     total = sent.astype(jnp.float32)
     bit = 2
     while bit < size:
         got = lax.ppermute(sent, "rows", [(i, i ^ bit) for i in range(size)])
+        if beside is not None:
+            got, beside = lax.optimization_barrier((got, beside))
         total = sent.astype(jnp.float32) + got.astype(jnp.float32)
         sent = total.astype(jnp.bfloat16)
         bit *= 2
-    return total
+    return total, beside
 
 
 def per_device(search_vectors, tile_values, block_columns):

time: 75.1 us -> 76 us (1.012)
  waiting for transfers between devices: 24.4 us -> 25.7 us
    ppermute x8, waiting for transfers between devices: 0.25 us -> 1.52 us  [with_core(): lax.ppermute(value, 'rows', [(i, i ^ 1) for i in range(lax.axis_size('row...]
  transfers between devices with their start and end apart: 22 -> 22, of which waited for: 11 -> 12; matrix products, arithmetic and copies ran while one was open for 2% -> 2% of each run, Pallas kernels for 9% -> 9%
where the time goes in v8:
time: 76 us; the launch traced here: 75.5 us
  starting transfers between devices  30.5 us (40%)
  waiting for transfers between devices  25.7 us (34%)
  Pallas kernels  15.6 us (21%)
  local copies, waits for them, and re-layouts  2.03 us (3%)
  between operations  0.85 us (1%)
  other arithmetic  0.81 us (1%)
    ppermute x4, starting transfers between devices, with_chip(): lax.ppermute(value, 'rows', [p for k in odds for p in ((k, k + 1), (k + 1...  12.3 us
    ppermute x7, waiting for transfers between devices, move(): lax.ppermute(value, 'cols', [(order[i], order[(i + by) % size]) for i in...  12 us
    ppermute x4, waiting for transfers between devices, with_chip(): lax.ppermute(value, 'rows', [p for k in odds for p in ((k, k + 1), (k + 1...  9.14 us
    ppermute x7, starting transfers between devices, move(): lax.ppermute(value, 'cols', [(order[i], order[(i + by) % size]) for i in...  7.37 us
    all_to_all x1, starting transfers between devices, per_device(): lax.all_to_all(search_vectors, 'cols', split_axis=1, concat_axis=0, tiled...  5.55 us
    ppermute x8, starting transfers between devices, with_core(): lax.ppermute(value, 'rows', [(i, i ^ 1) for i in range(lax.axis_size('row...  3.76 us
    pallas_call x1, Pallas kernels, per_device(): pl.pallas_call(second_stage, out_shape=jax.ShapeDtypeStruct((rows, width)...  3.38 us
    pallas_call x1, Pallas kernels, per_device(): pl.pallas_call(first_stage, out_shape=(jax.ShapeDtypeStruct((rows, width)...  3.24 us
  transfers between devices with their start and end apart: 22, of which 12 were waited for; matrix products, arithmetic and copies ran while one was open for 2% of the time, Pallas kernels for 9%

profile of v8, /device:TPU:1, one launch (start us, length us, event | category | flops | bytes accessed | tf_op | source)
XLA Modules:
  0.0 75.5 jit_solution(10961354695274216953)
XLA Ops:
  0.6 4.6 %collective-permute-start.3 = (bf16[16,64,512]{2,1,0:T(8,128)(2,1)}, bf16[16,64,512]{2,1,0:T(8,128)(2,1)S(1)}, u32[]{:S(2)}, u32[]{:S(2)}) collective-permute-start(bf16[16,64,512]{2,1,0:T(8,128)(2,1)} %tiles.1), channel_id=1, source_target_pairs={{8,16},{16,8},{9,17},{17,9},{10,18},{18,10},{11,19},{19,11},{12,20... | collective-permute-start | bytes 3145736 | tf_op jit(solution)/shard_map/ppermute | solution.py:37
  5.3 0.8 copy_bitcast_fusion
  6.1 5.6 %all-to-all-start = ((bf16[128,8,128]{2,0,1:T(8,128)(2,1)}), bf16[128,8,128]{2,0,1:T(8,128)(2,1)S(1)}, u32[]{:S(2)}, u32[]{:S(2)}) async-start(bf16[128,8,128]{2,0,1:T(8,128)(2,1)} %copy_bitcast_fusion), calls=%async_computation | async-start | bytes 524288 | tf_op jit(solution)/shard_map/all_to_all | solution.py:406
  12.3 1.2 %copy-done.1 = bf16[16,64,512]{2,1,0:T(8,128)(2,1)S(1)} copy-done((bf16[16,64,512]{2,1,0:T(8,128)(2,1)S(1)}, bf16[16,64,512]{2,1,0:T(8,128)(2,1)}, u32[]{:S(2)}) %copy-start.1) | copy-done | bytes 1048600
  13.5 2.4 %shard_map.59 = (bf16[4,256,768]{2,1,0:T(8,128)(2,1)S(1)}, bf16[12,64,512]{2,1,0:T(8,128)(2,1)}, s32[8,16]{1,0:T(8,128)S(1)}) custom-call(s32[1]{0:T(128)} %bitcast.odd, s32[8,16]{1,0:T(8,128)S(1)} %subtract_bitcast_fusion.offsets.to_send, s32[8,16]{1,0:T(8,128)S(1)} %subtract_bitcast_fusion.offsets.to_send, bf16[16,64,512]{2,1,0:T(8,128)(2,1)S(1)} %copy-done.1), custom_call_target="tpu_custom_call" | custom-call | tf_op jit(solution)/shard_map/pallas_call | solution.py:419
  16.4 2.2 %collective-permute-start.1 = (s32[8,16]{1,0:T(8,128)S(1)}, s32[8,16]{1,0:T(8,128)S(1)}, u32[]{:S(2)}, u32[]{:S(2)}) collective-permute-start(s32[8,16]{1,0:T(8,128)S(1)} %get-tuple-element.24), channel_id=1, source_target_pairs={{8,16},{16,8},{9,17},{17,9},{10,18},{18,10},{11,19},{19,11},{12,20... | collective-permute-start | bytes 1544 | tf_op jit(solution)/shard_map/ppermute | solution.py:37
  18.6 0.7 all-to-all-done
  19.3 2.7 %collective-permute-start.5 = (bf16[1024,128]{1,0:T(8,128)(2,1)S(1)}, bf16[1024,128]{1,0:T(8,128)(2,1)S(1)}, u32[]{:S(2)}, u32[]{:S(2)}) collective-permute-start(bf16[1024,128]{1,0:T(8,128)(2,1)S(1)} %bitcast.18), channel_id=1, source_target_pairs={{8,16},{16,8},{9,17},{17,9},{10,18},{18,10},{11,19},{19,11},{12,20... | collective-permute-start | bytes 786440 | tf_op jit(solution)/shard_map/ppermute | solution.py:37
  22.1 2.4 %shard_map.60.edges = bf16[6,256,768]{2,1,0:T(8,128)(2,1)S(1)} custom-call(s32[1]{0:T(128)} %bitcast.odd, s32[8,16]{1,0:T(8,128)S(1)} %broadcast_clamp_fusion.1.at_first, s32[8,16]{1,0:T(8,128)S(1)} %broadcast_clamp_fusion.at_second, bf16[12,64,512]{2,1,0:T(8,128)(2,1)} %collective-permute-done.2.first, bf16[16,64,512]{2,1,0:T(8,128)(2,1)S(1)} %collective-permute-done.3.second), custom_call_target="tpu_custom_call" | custom-call | tf_op jit(solution)/shard_map/pallas_call | solution.py:434
  24.5 2.5 %collective-permute-done.5.x_second = bf16[1024,128]{1,0:T(8,128)(2,1)S(1)} collective-permute-done((bf16[1024,128]{1,0:T(8,128)(2,1)S(1)}, bf16[1024,128]{1,0:T(8,128)(2,1)S(1)}, u32[]{:S(2)}, u32[]{:S(2)}) %collective-permute-start.5) | collective-permute-done | bytes 262176 | tf_op jit(solution)/shard_map/ppermute | solution.py:37
  27.0 3.2 %shard_map.61 = (f32[1024,128]{1,0:T(8,128)S(1)}, f32[1536,128]{1,0:T(8,128)S(1)}, bf16[1536,128]{1,0:T(8,128)(2,1)S(1)}) custom-call(s32[1]{0:T(128)} %bitcast.odd, bf16[4,256,768]{2,1,0:T(8,128)(2,1)S(1)} %get-tuple-element.23.own, bf16[6,256,768]{2,1,0:T(8,128)(2,1)S(1)} %shard_map.60.edges, bf16[1024,128]{1,0:T(8,128)(2,1)S(1)} %collective-permute-done.4.x_first, ...), custom_call_target="tpu_custom_call" | custom-call | tf_op jit(solution)/shard_map/pallas_call | solution.py:457
  30.3 2.7 %collective-permute-start.7 = (bf16[1536,128]{1,0:T(8,128)(2,1)S(1)}, bf16[1536,128]{1,0:T(8,128)(2,1)S(1)}, u32[]{:S(2)}, u32[]{:S(2)}) collective-permute-start(bf16[1536,128]{1,0:T(8,128)(2,1)S(1)} %get-tuple-element.28), channel_id=1, source_target_pairs={{8,16},{16,8},{9,17},{17,9},{10,18},{18,10},{11,19},{19,11},{12,20... | collective-permute-start | bytes 1179656 | tf_op jit(solution)/shard_map/ppermute | solution.py:37
  33.1 6.6 %collective-permute-done.7.got_second = bf16[1536,128]{1,0:T(8,128)(2,1)S(1)} collective-permute-done((bf16[1536,128]{1,0:T(8,128)(2,1)S(1)}, bf16[1536,128]{1,0:T(8,128)(2,1)S(1)}, u32[]{:S(2)}, u32[]{:S(2)}) %collective-permute-start.7) | collective-permute-done | bytes 393248 | tf_op jit(solution)/shard_map/ppermute | solution.py:37
  39.7 3.4 %shard_map.62.mine = bf16[1024,128]{1,0:T(8,128)(2,1)S(1)} custom-call(s32[1]{0:T(128)} %bitcast.odd, bf16[4,256,768]{2,1,0:T(8,128)(2,1)S(1)} %get-tuple-element.23.own, bf16[6,256,768]{2,1,0:T(8,128)(2,1)S(1)} %shard_map.60.edges, f32[1024,128]{1,0:T(8,128)S(1)} %get-tuple-element.26.now, f32[1536,128]{1,0:T(8,128)S(1)} %get-tuple-element.27.last, ...), custom_call_target="tpu_custom_call" | custom-call | tf_op jit(solution)/shard_map/pallas_call | solution.py:471
  43.1 1.2 %collective-permute-start.8 = (bf16[1024,128]{1,0:T(8,128)(2,1)S(1)}, bf16[1024,128]{1,0:T(8,128)(2,1)S(1)}, u32[]{:S(2)}, u32[]{:S(2)}) collective-permute-start(bf16[1024,128]{1,0:T(8,128)(2,1)S(1)} %shard_map.62.mine), channel_id=1, source_target_pairs={{0,2},{2,4},{4,6},{6,7},{7,5},{5,3},{3,1},{1,0},{8,10},{10,12},{12... | collective-permute-start | bytes 786440 | tf_op jit(solution)/shard_map/ppermute | solution.py:303
  44.6 2.0 %collective-permute-start.10 = (bf16[1024,128]{1,0:T(8,128)(2,1)S(1)}, bf16[1024,128]{1,0:T(8,128)(2,1)S(1)}, u32[]{:S(2)}, u32[]{:S(2)}) collective-permute-start(bf16[1024,128]{1,0:T(8,128)(2,1)S(1)} %shard_map.62.mine), channel_id=1, source_target_pairs={{0,4},{2,6},{4,7},{6,5},{7,3},{5,1},{3,0},{1,2},{8,12},{10,14},{12... | collective-permute-start | bytes 786440 | tf_op jit(solution)/shard_map/ppermute | solution.py:303
  47.0 2.1 %collective-permute-done.8.refs_0_ = bf16[1024,128]{1,0:T(8,128)(2,1)S(1)} collective-permute-done((bf16[1024,128]{1,0:T(8,128)(2,1)S(1)}, bf16[1024,128]{1,0:T(8,128)(2,1)S(1)}, u32[]{:S(2)}, u32[]{:S(2)}) %collective-permute-start.8) | collective-permute-done | bytes 262176 | tf_op jit(solution)/shard_map/ppermute | solution.py:303
  49.1 2.1 %collective-permute-done.9.refs_1_ = bf16[1024,128]{1,0:T(8,128)(2,1)S(1)} collective-permute-done((bf16[1024,128]{1,0:T(8,128)(2,1)S(1)}, bf16[1024,128]{1,0:T(8,128)(2,1)S(1)}, u32[]{:S(2)}, u32[]{:S(2)}) %collective-permute-start.9) | collective-permute-done | bytes 262176 | tf_op jit(solution)/shard_map/ppermute | solution.py:303
  51.6 3.2 %collective-permute-done.10.back.refs_2_ = bf16[1024,128]{1,0:T(8,128)(2,1)S(1)} collective-permute-done((bf16[1024,128]{1,0:T(8,128)(2,1)S(1)}, bf16[1024,128]{1,0:T(8,128)(2,1)S(1)}, u32[]{:S(2)}, u32[]{:S(2)}) %collective-permute-start.10) | collective-permute-done | bytes 262176 | tf_op jit(solution)/shard_map/ppermute | solution.py:303
  54.9 0.9 %collective-permute-done.11.front.refs_3_ = bf16[1024,128]{1,0:T(8,128)(2,1)S(1)} collective-permute-done((bf16[1024,128]{1,0:T(8,128)(2,1)S(1)}, bf16[1024,128]{1,0:T(8,128)(2,1)S(1)}, u32[]{:S(2)}, u32[]{:S(2)}) %collective-permute-start.11) | collective-permute-done | bytes 262176 | tf_op jit(solution)/shard_map/ppermute | solution.py:303
  55.8 0.9 %shard_map.64 = (bf16[256,128]{1,0:T(8,128)(2,1)S(1)}, bf16[256,128]{1,0:T(8,128)(2,1)S(1)}, bf16[256,128]{1,0:T(8,128)(2,1)S(1)}) custom-call(s32[8]{0:T(128)S(1)} %compare_select_fusion.2.where, bf16[3,128,1024]{2,1,0:T(8,128)(2,1)S(1)} %get-tuple-element.29.lefts, bf16[1024,128]{1,0:T(8,128)(2,1)S(1)} %collective-permute-done.10.back.refs_2_, ...), custom_call_target="tpu_custom_call" | custom-call | tf_op jit(solution)/shard_map/pallas_call | solution.py:331
  57.1 1.8 %collective-permute-start.15 = (bf16[256,128]{1,0:T(8,128)(2,1)S(1)}, bf16[256,128]{1,0:T(8,128)(2,1)S(1)}, u32[]{:S(2)}, u32[]{:S(2)}) collective-permute-start(bf16[256,128]{1,0:T(8,128)(2,1)S(1)} %get-tuple-element.31._), channel_id=1, source_target_pairs={{0,3},{2,1},{4,0},{6,2},{7,4},{5,6},{3,7},{1,5},{8,11},{10,9},{12,... | collective-permute-start | bytes 196616 | tf_op jit(solution)/shard_map/ppermute | solution.py:303
  58.9 1.7 %collective-permute-start.13 = (bf16[256,128]{1,0:T(8,128)(2,1)S(1)}, bf16[256,128]{1,0:T(8,128)(2,1)S(1)}, u32[]{:S(2)}, u32[]{:S(2)}) collective-permute-start(bf16[256,128]{1,0:T(8,128)(2,1)S(1)} %get-tuple-element.32), channel_id=1, source_target_pairs={{0,2},{2,4},{4,6},{6,7},{7,5},{5,3},{3,1},{1,0},{8,10},{10,12},{12... | collective-permute-start | bytes 196616 | tf_op jit(solution)/shard_map/ppermute | solution.py:303
  60.7 1.7 %collective-permute-done.13.refs_4_ = bf16[256,128]{1,0:T(8,128)(2,1)S(1)} collective-permute-done((bf16[256,128]{1,0:T(8,128)(2,1)S(1)}, bf16[256,128]{1,0:T(8,128)(2,1)S(1)}, u32[]{:S(2)}, u32[]{:S(2)}) %collective-permute-start.13) | collective-permute-done | bytes 65568 | tf_op jit(solution)/shard_map/ppermute | solution.py:303
  62.4 1.9 %collective-permute-done.14.refs_5_ = bf16[256,128]{1,0:T(8,128)(2,1)S(1)} collective-permute-done((bf16[256,128]{1,0:T(8,128)(2,1)S(1)}, bf16[256,128]{1,0:T(8,128)(2,1)S(1)}, u32[]{:S(2)}, u32[]{:S(2)}) %collective-permute-start.14) | collective-permute-done | bytes 65568 | tf_op jit(solution)/shard_map/ppermute | solution.py:303
  64.3 1.7 %collective-permute-start.16 = (f32[3,64,128]{2,1,0:T(8,128)S(1)}, f32[3,64,128]{2,1,0:T(8,128)S(1)}, u32[]{:S(2)}, u32[]{:S(2)}) collective-permute-start(f32[3,64,128]{2,1,0:T(8,128)S(1)} %constant_dynamic-slice_fusion), channel_id=1, source_target_pairs={{0,8},{8,0},{16,24},{24,16},{1,9},{9,1},{17,25},{25,17},{2,10},{10... | collective-permute-start | bytes 294920 | tf_op jit(solution)/shard_map/ppermute | solution.py:32
  66.9 0.8 %collective-permute-start.17 = (bf16[3,64,128]{2,1,0:T(8,128)(2,1)S(1)}, bf16[3,64,128]{2,1,0:T(8,128)(2,1)S(1)}, u32[]{:S(2)}, u32[]{:S(2)}) collective-permute-start(bf16[3,64,128]{2,1,0:T(8,128)(2,1)S(1)} %add_convert_fusion.1), channel_id=1, source_target_pairs={{0,16},{8,24},{16,0},{24,8},{1,17},{9,25},{17,1},{25,9},{2,18},{10... | collective-permute-start | bytes 147464 | tf_op jit(solution)/shard_map/ppermute | solution.py:387
  67.7 2.3 %collective-permute-done.18 = bf16[5,64,128]{2,1,0:T(8,128)(2,1)S(1)} collective-permute-done((bf16[5,64,128]{2,1,0:T(8,128)(2,1)S(1)}, bf16[5,64,128]{2,1,0:T(8,128)(2,1)S(1)}, u32[]{:S(2)}, u32[]{:S(2)}) %collective-permute-start.18) | collective-permute-done | bytes 81952 | tf_op jit(solution)/shard_map/ppermute | solution.py:387
  70.0 1.4 %collective-permute-start.19 = (f32[5,64,128]{2,1,0:T(8,128)S(1)}, f32[5,64,128]{2,1,0:T(8,128)S(1)}, u32[]{:S(2)}, u32[]{:S(2)}) collective-permute-start(f32[5,64,128]{2,1,0:T(8,128)S(1)} %convert_add_fusion.refs_0_), channel_id=1, source_target_pairs={{0,8},{8,0},{16,24},{24,16},{1,9},{9,1},{17,25},{25,17},{2,10},{10... | collective-permute-start | bytes 491528 | tf_op jit(solution)/shard_map/ppermute | solution.py:32
  71.4 1.3 %shard_map.66 = bf16[128,1024]{1,0:T(8,128)(2,1)} custom-call(s32[8]{0:T(128)S(1)} %compare_select_fusion.2.where, bf16[1024,128]{1,0:T(8,128)(2,1)S(1)} %shard_map.62.mine, bf16[1024,128]{1,0:T(8,128)(2,1)S(1)} %collective-permute-done.8.refs_0_, bf16[1024,128]{1,0:T(8,128)(2,1)S(1)} %collective-permute-done.9.refs_1_, ...), custom_call_target="tpu_custom_call" | custom-call | tf_op jit(solution)/shard_map/pallas_call | solution.py:352
  72.8 1.3 %collective-permute-done.20.refs_3_ = f32[3,64,128]{2,1,0:T(8,128)S(1)} collective-permute-done((f32[3,64,128]{2,1,0:T(8,128)S(1)}, f32[3,64,128]{2,1,0:T(8,128)S(1)}, u32[]{:S(2)}, u32[]{:S(2)}) %collective-permute-start.20) | collective-permute-done | bytes 98336 | tf_op jit(solution)/shard_map/ppermute | solution.py:32
  74.1 1.4 %shard_map.67 = f32[128,1024]{1,0:T(8,128)} custom-call(s32[8]{0:T(128)S(1)} %compare_select_fusion.2.where, s32[1]{0:T(128)} %bitcast.odd, f32[5,64,128]{2,1,0:T(8,128)S(1)} %convert_add_fusion.refs_0_, f32[5,64,128]{2,1,0:T(8,128)S(1)} %collective-permute-done.19.refs_1_, f32[3,64,128]{2,1,0:T(8,128)S(1)} %convert_add_fusion.1.refs_2_, ...), custom_call_target="tpu_custom_call" | custom-call | tf_op jit(solution)/shard_map/pallas_call | solution.py:361
  (42 shorter events, 4.0 us)
Async XLA Ops:
  0.6 4.7 %copy-start = (bf16[128,1024]{1,0:T(8,128)(2,1)S(1)}, bf16[128,1024]{1,0:T(8,128)(2,1)}, u32[]{:S(2)}) copy-start(bf16[128,1024]{1,0:T(8,128)(2,1)} %param.4) | copy-start | bytes 786436
  0.6 21.5 %collective-permute-start.3 = (bf16[16,64,512]{2,1,0:T(8,128)(2,1)}, bf16[16,64,512]{2,1,0:T(8,128)(2,1)S(1)}, u32[]{:S(2)}, u32[]{:S(2)}) collective-permute-start(bf16[16,64,512]{2,1,0:T(8,128)(2,1)} %tiles.1), channel_id=1, source_target_pairs={{8,16},{16,8},{9,17},{17,9},{10,18},{18,10},{11,19},{19,11},{12,20... | collective-permute-start | bytes 3145736 | tf_op jit(solution)/shard_map/ppermute | solution.py:37
  6.1 13.3 %all-to-all-start = ((bf16[128,8,128]{2,0,1:T(8,128)(2,1)}), bf16[128,8,128]{2,0,1:T(8,128)(2,1)S(1)}, u32[]{:S(2)}, u32[]{:S(2)}) async-start(bf16[128,8,128]{2,0,1:T(8,128)(2,1)} %copy_bitcast_fusion), calls=%async_computation | async-start | bytes 524288 | tf_op jit(solution)/shard_map/all_to_all | solution.py:406
  12.3 1.2 %copy-start.1 = (bf16[16,64,512]{2,1,0:T(8,128)(2,1)S(1)}, bf16[16,64,512]{2,1,0:T(8,128)(2,1)}, u32[]{:S(2)}) copy-start(bf16[16,64,512]{2,1,0:T(8,128)(2,1)} %tiles.1) | copy-start | bytes 3145732
  15.9 6.2 %collective-permute-start.2 = (bf16[12,64,512]{2,1,0:T(8,128)(2,1)}, bf16[12,64,512]{2,1,0:T(8,128)(2,1)}, u32[]{:S(2)}, u32[]{:S(2)}) collective-permute-start(bf16[12,64,512]{2,1,0:T(8,128)(2,1)} %get-tuple-element.25), channel_id=1, source_target_pairs={{0,8},{8,0},{16,24},{24,16},{1,9},{9,1},{17,25},{25,17},{2,10},{10... | collective-permute-start | bytes 2359304 | tf_op jit(solution)/shard_map/ppermute | solution.py:32
  15.9 3.4 %collective-permute-start = (s32[8,16]{1,0:T(8,128)S(1)}, s32[8,16]{1,0:T(8,128)S(1)}, u32[]{:S(2)}, u32[]{:S(2)}) collective-permute-start(s32[8,16]{1,0:T(8,128)S(1)} %get-tuple-element.24), channel_id=1, source_target_pairs={{0,8},{8,0},{16,24},{24,16},{1,9},{9,1},{17,25},{25,17},{2,10},{10... | collective-permute-start | bytes 1544 | tf_op jit(solution)/shard_map/ppermute | solution.py:32
  16.4 5.7 %collective-permute-start.1 = (s32[8,16]{1,0:T(8,128)S(1)}, s32[8,16]{1,0:T(8,128)S(1)}, u32[]{:S(2)}, u32[]{:S(2)}) collective-permute-start(s32[8,16]{1,0:T(8,128)S(1)} %get-tuple-element.24), channel_id=1, source_target_pairs={{8,16},{16,8},{9,17},{17,9},{10,18},{18,10},{11,19},{19,11},{12,20... | collective-permute-start | bytes 1544 | tf_op jit(solution)/shard_map/ppermute | solution.py:37
  19.3 5.2 %collective-permute-start.4 = (bf16[1024,128]{1,0:T(8,128)(2,1)S(1)}, bf16[1024,128]{1,0:T(8,128)(2,1)S(1)}, u32[]{:S(2)}, u32[]{:S(2)}) collective-permute-start(bf16[1024,128]{1,0:T(8,128)(2,1)S(1)} %bitcast.17), channel_id=1, source_target_pairs={{0,8},{8,0},{16,24},{24,16},{1,9},{9,1},{17,25},{25,17},{2,10},{10... | collective-permute-start | bytes 786440 | tf_op jit(solution)/shard_map/ppermute | solution.py:32
  19.3 7.7 %collective-permute-start.5 = (bf16[1024,128]{1,0:T(8,128)(2,1)S(1)}, bf16[1024,128]{1,0:T(8,128)(2,1)S(1)}, u32[]{:S(2)}, u32[]{:S(2)}) collective-permute-start(bf16[1024,128]{1,0:T(8,128)(2,1)S(1)} %bitcast.18), channel_id=1, source_target_pairs={{8,16},{16,8},{9,17},{17,9},{10,18},{18,10},{11,19},{19,11},{12,20... | collective-permute-start | bytes 786440 | tf_op jit(solution)/shard_map/ppermute | solution.py:37
  30.2 2.8 %collective-permute-start.6 = (bf16[1536,128]{1,0:T(8,128)(2,1)S(1)}, bf16[1536,128]{1,0:T(8,128)(2,1)S(1)}, u32[]{:S(2)}, u32[]{:S(2)}) collective-permute-start(bf16[1536,128]{1,0:T(8,128)(2,1)S(1)} %get-tuple-element.28), channel_id=1, source_target_pairs={{0,8},{8,0},{16,24},{24,16},{1,9},{9,1},{17,25},{25,17},{2,10},{10... | collective-permute-start | bytes 1179656 | tf_op jit(solution)/shard_map/ppermute | solution.py:32
  30.3 9.4 %collective-permute-start.7 = (bf16[1536,128]{1,0:T(8,128)(2,1)S(1)}, bf16[1536,128]{1,0:T(8,128)(2,1)S(1)}, u32[]{:S(2)}, u32[]{:S(2)}) collective-permute-start(bf16[1536,128]{1,0:T(8,128)(2,1)S(1)} %get-tuple-element.28), channel_id=1, source_target_pairs={{8,16},{16,8},{9,17},{17,9},{10,18},{18,10},{11,19},{19,11},{12,20... | collective-permute-start | bytes 1179656 | tf_op jit(solution)/shard_map/ppermute | solution.py:37
  39.7 7.3 %copy-start.2 = (s32[8]{0:T(128)S(1)}, s32[8]{0:T(128)}, u32[]{:S(2)}) copy-start(s32[8]{0:T(128)} %constant.67.clone) | copy-start | bytes 100
  43.1 6.0 %collective-permute-start.8 = (bf16[1024,128]{1,0:T(8,128)(2,1)S(1)}, bf16[1024,128]{1,0:T(8,128)(2,1)S(1)}, u32[]{:S(2)}, u32[]{:S(2)}) collective-permute-start(bf16[1024,128]{1,0:T(8,128)(2,1)S(1)} %shard_map.62.mine), channel_id=1, source_target_pairs={{0,2},{2,4},{4,6},{6,7},{7,5},{5,3},{3,1},{1,0},{8,10},{10,12},{12... | collective-permute-start | bytes 786440 | tf_op jit(solution)/shard_map/ppermute | solution.py:303
  44.3 7.0 %collective-permute-start.9 = (bf16[1024,128]{1,0:T(8,128)(2,1)S(1)}, bf16[1024,128]{1,0:T(8,128)(2,1)S(1)}, u32[]{:S(2)}, u32[]{:S(2)}) collective-permute-start(bf16[1024,128]{1,0:T(8,128)(2,1)S(1)} %shard_map.62.mine), channel_id=1, source_target_pairs={{0,1},{2,0},{4,2},{6,4},{7,6},{5,7},{3,5},{1,3},{8,9},{10,8},{12,1... | collective-permute-start | bytes 786440 | tf_op jit(solution)/shard_map/ppermute | solution.py:303
  44.6 10.3 %collective-permute-start.10 = (bf16[1024,128]{1,0:T(8,128)(2,1)S(1)}, bf16[1024,128]{1,0:T(8,128)(2,1)S(1)}, u32[]{:S(2)}, u32[]{:S(2)}) collective-permute-start(bf16[1024,128]{1,0:T(8,128)(2,1)S(1)} %shard_map.62.mine), channel_id=1, source_target_pairs={{0,4},{2,6},{4,7},{6,5},{7,3},{5,1},{3,0},{1,2},{8,12},{10,14},{12... | collective-permute-start | bytes 786440 | tf_op jit(solution)/shard_map/ppermute | solution.py:303
  46.6 9.2 %collective-permute-start.11 = (bf16[1024,128]{1,0:T(8,128)(2,1)S(1)}, bf16[1024,128]{1,0:T(8,128)(2,1)S(1)}, u32[]{:S(2)}, u32[]{:S(2)}) collective-permute-start(bf16[1024,128]{1,0:T(8,128)(2,1)S(1)} %shard_map.62.mine), channel_id=1, source_target_pairs={{0,3},{2,1},{4,0},{6,2},{7,4},{5,6},{3,7},{1,5},{8,11},{10,9},{12,... | collective-permute-start | bytes 786440 | tf_op jit(solution)/shard_map/ppermute | solution.py:303
  57.0 3.6 %collective-permute-start.12 = (f32[5,64,128]{2,1,0:T(8,128)S(1)}, f32[5,64,128]{2,1,0:T(8,128)S(1)}, u32[]{:S(2)}, u32[]{:S(2)}) collective-permute-start(f32[5,64,128]{2,1,0:T(8,128)S(1)} %constant_dynamic-slice_fusion.1), channel_id=1, source_target_pairs={{0,8},{8,0},{16,24},{24,16},{1,9},{9,1},{17,25},{25,17},{2,10},{10... | collective-permute-start | bytes 491528 | tf_op jit(solution)/shard_map/ppermute | solution.py:32
  57.1 7.1 %collective-permute-start.15 = (bf16[256,128]{1,0:T(8,128)(2,1)S(1)}, bf16[256,128]{1,0:T(8,128)(2,1)S(1)}, u32[]{:S(2)}, u32[]{:S(2)}) collective-permute-start(bf16[256,128]{1,0:T(8,128)(2,1)S(1)} %get-tuple-element.31._), channel_id=1, source_target_pairs={{0,3},{2,1},{4,0},{6,2},{7,4},{5,6},{3,7},{1,5},{8,11},{10,9},{12,... | collective-permute-start | bytes 196616 | tf_op jit(solution)/shard_map/ppermute | solution.py:303
  58.9 3.5 %collective-permute-start.13 = (bf16[256,128]{1,0:T(8,128)(2,1)S(1)}, bf16[256,128]{1,0:T(8,128)(2,1)S(1)}, u32[]{:S(2)}, u32[]{:S(2)}) collective-permute-start(bf16[256,128]{1,0:T(8,128)(2,1)S(1)} %get-tuple-element.32), channel_id=1, source_target_pairs={{0,2},{2,4},{4,6},{6,7},{7,5},{5,3},{3,1},{1,0},{8,10},{10,12},{12... | collective-permute-start | bytes 196616 | tf_op jit(solution)/shard_map/ppermute | solution.py:303
  60.6 3.7 %collective-permute-start.14 = (bf16[256,128]{1,0:T(8,128)(2,1)S(1)}, bf16[256,128]{1,0:T(8,128)(2,1)S(1)}, u32[]{:S(2)}, u32[]{:S(2)}) collective-permute-start(bf16[256,128]{1,0:T(8,128)(2,1)S(1)} %get-tuple-element.33), channel_id=1, source_target_pairs={{0,1},{2,0},{4,2},{6,4},{7,6},{5,7},{3,5},{1,3},{8,9},{10,8},{12,1... | collective-permute-start | bytes 196616 | tf_op jit(solution)/shard_map/ppermute | solution.py:303
  64.3 2.6 %collective-permute-start.16 = (f32[3,64,128]{2,1,0:T(8,128)S(1)}, f32[3,64,128]{2,1,0:T(8,128)S(1)}, u32[]{:S(2)}, u32[]{:S(2)}) collective-permute-start(f32[3,64,128]{2,1,0:T(8,128)S(1)} %constant_dynamic-slice_fusion), channel_id=1, source_target_pairs={{0,8},{8,0},{16,24},{24,16},{1,9},{9,1},{17,25},{25,17},{2,10},{10... | collective-permute-start | bytes 294920 | tf_op jit(solution)/shard_map/ppermute | solution.py:32
  66.0 4.0 %collective-permute-start.18 = (bf16[5,64,128]{2,1,0:T(8,128)(2,1)S(1)}, bf16[5,64,128]{2,1,0:T(8,128)(2,1)S(1)}, u32[]{:S(2)}, u32[]{:S(2)}) collective-permute-start(bf16[5,64,128]{2,1,0:T(8,128)(2,1)S(1)} %add_convert_fusion), channel_id=1, source_target_pairs={{0,16},{8,24},{16,0},{24,8},{1,17},{9,25},{17,1},{25,9},{2,18},{10... | collective-permute-start | bytes 245768 | tf_op jit(solution)/shard_map/ppermute | solution.py:387
  66.9 5.8 %collective-permute-start.17 = (bf16[3,64,128]{2,1,0:T(8,128)(2,1)S(1)}, bf16[3,64,128]{2,1,0:T(8,128)(2,1)S(1)}, u32[]{:S(2)}, u32[]{:S(2)}) collective-permute-start(bf16[3,64,128]{2,1,0:T(8,128)(2,1)S(1)} %add_convert_fusion.1), channel_id=1, source_target_pairs={{0,16},{8,24},{16,0},{24,8},{1,17},{9,25},{17,1},{25,9},{2,18},{10... | collective-permute-start | bytes 147464 | tf_op jit(solution)/shard_map/ppermute | solution.py:387
  70.0 2.8 %collective-permute-start.19 = (f32[5,64,128]{2,1,0:T(8,128)S(1)}, f32[5,64,128]{2,1,0:T(8,128)S(1)}, u32[]{:S(2)}, u32[]{:S(2)}) collective-permute-start(f32[5,64,128]{2,1,0:T(8,128)S(1)} %convert_add_fusion.refs_0_), channel_id=1, source_target_pairs={{0,8},{8,0},{16,24},{24,16},{1,9},{9,1},{17,25},{25,17},{2,10},{10... | collective-permute-start | bytes 491528 | tf_op jit(solution)/shard_map/ppermute | solution.py:32
  72.7 1.4 %collective-permute-start.20 = (f32[3,64,128]{2,1,0:T(8,128)S(1)}, f32[3,64,128]{2,1,0:T(8,128)S(1)}, u32[]{:S(2)}, u32[]{:S(2)}) collective-permute-start(f32[3,64,128]{2,1,0:T(8,128)S(1)} %convert_add_fusion.1.refs_2_), channel_id=1, source_target_pairs={{0,8},{8,0},{16,24},{24,16},{1,9},{9,1},{17,25},{25,17},{2,10},{10... | collective-permute-start | bytes 294920 | tf_op jit(solution)/shard_map/ppermute | solution.py:32

commit v9 on v7

--- a/solution.py
+++ b/solution.py
@@ -154,7 +154,7 @@
                         doubled, slot)
 
 
-def run_steps(own, edges, w, y, degree):
+def run_steps(own, edges, w, y, degree, now=None):
     middle, size, span = own.shape
     edge = edges.shape[0] // 2
     bands = [edges.at[j] for j in range(edge)]
@@ -168,12 +168,17 @@
             start = j * size
             here = slice(start + size, start + 2 * size)
             product = dot(bands[j][...], src[start:start + span])
+            k = j - edge
+            mine = now is not None and 0 <= k < middle
+            given = src if step == 0 else dst
+            start_value = (
+                now[k * size:(k + 1) * size] if mine else given[here].astype(jnp.float32)
+            )
+            value = product - shift_value * (start_value if step == 0 else cur[here])
             if degree + step == 0:
-                value = (product - shift_value * src[here].astype(jnp.float32)) / half_width
-            elif degree + step == 1:
-                value = product - shift_value * cur[here] - dst[here].astype(jnp.float32)
+                value = value / half_width
             else:
-                value = product - shift_value * cur[here] - new[here]
+                value = value - (start_value if step == 1 else new[here])
             new[here] = value
             dst[here] = value.astype(jnp.bfloat16)
         cur, new = new, cur
@@ -204,16 +209,14 @@
     size = own.shape[1]
     here = slice(rows, 2 * rows)
     w0[here] = now[...].astype(jnp.bfloat16)
-    y0[here] = now[...]
     y1[rows - size:2 * rows + size] = last[...]
     for got, behind in ((got_first, odd[0]), (got_second, 1 - odd[0])):
         start = placed(behind, rows)
         w0[pl.ds(start, rows)] = got[:rows]
-        y0[pl.ds(start, rows)] = got[:rows].astype(jnp.float32)
         y1[pl.ds(pl.multiple_of(start + size, size), rows - 2 * size)] = (
             got[rows:].astype(jnp.float32)
         )
-    _, _, rounded = run_steps(own, edges, (w0, w1), (y0, y1), STAGE)
+    _, _, rounded = run_steps(own, edges, (w0, w1), (y0, y1), STAGE, now)
     out[...] = rounded[here]
 
 

time: 75.1 us -> 75 us (level)
  no operation moved by 1% of the time
where the time goes in v9:
time: 75 us; the launch traced here: 74.6 us
  starting transfers between devices  31 us (41%)
  waiting for transfers between devices  24.4 us (33%)
  Pallas kernels  15.5 us (21%)
  local copies, waits for them, and re-layouts  2.03 us (3%)
  between operations  0.85 us (1%)
  other arithmetic  0.81 us (1%)
    ppermute x4, starting transfers between devices, with_chip(): lax.ppermute(value, 'rows', [p for k in odds for p in ((k, k + 1), (k + 1...  12.3 us
    ppermute x7, waiting for transfers between devices, move(): lax.ppermute(value, 'cols', [(order[i], order[(i + by) % size]) for i in...  12 us
    ppermute x4, waiting for transfers between devices, with_chip(): lax.ppermute(value, 'rows', [p for k in odds for p in ((k, k + 1), (k + 1...  9.14 us
    ppermute x7, starting transfers between devices, move(): lax.ppermute(value, 'cols', [(order[i], order[(i + by) % size]) for i in...  7.37 us
    all_to_all x1, starting transfers between devices, per_device(): lax.all_to_all(search_vectors, 'cols', split_axis=1, concat_axis=0, tiled...  5.55 us
    ppermute x8, starting transfers between devices, with_core(): lax.ppermute(value, 'rows', [(i, i ^ 1) for i in range(lax.axis_size('row...  4.25 us
    pallas_call x1, Pallas kernels, per_device(): pl.pallas_call(second_stage, out_shape=jax.ShapeDtypeStruct((rows, width)...  3.28 us
    pallas_call x1, Pallas kernels, per_device(): pl.pallas_call(first_stage, out_shape=(jax.ShapeDtypeStruct((rows, width)...  3.24 us
  transfers between devices with their start and end apart: 22, of which 11 were waited for; matrix products, arithmetic and copies ran while one was open for 2% of the time, Pallas kernels for 9%

profile of v9, /device:TPU:1, one launch (start us, length us, event | category | flops | bytes accessed | tf_op | source)
XLA Modules:
  0.0 74.6 jit_solution(11150821381964017995)
XLA Ops:
  0.6 4.6 %collective-permute-start.3 = (bf16[16,64,512]{2,1,0:T(8,128)(2,1)}, bf16[16,64,512]{2,1,0:T(8,128)(2,1)S(1)}, u32[]{:S(2)}, u32[]{:S(2)}) collective-permute-start(bf16[16,64,512]{2,1,0:T(8,128)(2,1)} %tiles.1), channel_id=1, source_target_pairs={{8,16},{16,8},{9,17},{17,9},{10,18},{18,10},{11,19},{19,11},{12,20... | collective-permute-start | bytes 3145736 | tf_op jit(solution)/shard_map/ppermute | solution.py:37
  5.3 0.8 %copy_bitcast_fusion = bf16[128,8,128]{2,0,1:T(8,128)(2,1)} fusion(bf16[128,1024]{1,0:T(8,128)(2,1)S(1)} %copy-done), kind=kLoop, calls=%fused_computation | loop fusion | bytes 524288 | tf_op jit(solution)/shard_map/all_to_all | solution.py:407
  6.1 5.6 %all-to-all-start = ((bf16[128,8,128]{2,0,1:T(8,128)(2,1)}), bf16[128,8,128]{2,0,1:T(8,128)(2,1)S(1)}, u32[]{:S(2)}, u32[]{:S(2)}) async-start(bf16[128,8,128]{2,0,1:T(8,128)(2,1)} %copy_bitcast_fusion), calls=%async_computation | async-start | bytes 524288 | tf_op jit(solution)/shard_map/all_to_all | solution.py:407
  12.3 1.2 %copy-done.1 = bf16[16,64,512]{2,1,0:T(8,128)(2,1)S(1)} copy-done((bf16[16,64,512]{2,1,0:T(8,128)(2,1)S(1)}, bf16[16,64,512]{2,1,0:T(8,128)(2,1)}, u32[]{:S(2)}) %copy-start.1) | copy-done | bytes 1048600
  13.5 2.4 %shard_map.59 = (bf16[4,256,768]{2,1,0:T(8,128)(2,1)S(1)}, bf16[12,64,512]{2,1,0:T(8,128)(2,1)}, s32[8,16]{1,0:T(8,128)S(1)}) custom-call(s32[1]{0:T(128)} %bitcast.odd, s32[8,16]{1,0:T(8,128)S(1)} %subtract_bitcast_fusion.offsets.to_send, s32[8,16]{1,0:T(8,128)S(1)} %subtract_bitcast_fusion.offsets.to_send, bf16[16,64,512]{2,1,0:T(8,128)(2,1)S(1)} %copy-done.1), custom_call_target="tpu_custom_call" | custom-call | tf_op jit(solution)/shard_map/pallas_call | solution.py:420
  16.4 2.2 %collective-permute-start.1 = (s32[8,16]{1,0:T(8,128)S(1)}, s32[8,16]{1,0:T(8,128)S(1)}, u32[]{:S(2)}, u32[]{:S(2)}) collective-permute-start(s32[8,16]{1,0:T(8,128)S(1)} %get-tuple-element.18), channel_id=1, source_target_pairs={{8,16},{16,8},{9,17},{17,9},{10,18},{18,10},{11,19},{19,11},{12,20... | collective-permute-start | bytes 1544 | tf_op jit(solution)/shard_map/ppermute | solution.py:37
  18.6 0.7 all-to-all-done
  19.3 2.7 %collective-permute-start.5 = (bf16[1024,128]{1,0:T(8,128)(2,1)S(1)}, bf16[1024,128]{1,0:T(8,128)(2,1)S(1)}, u32[]{:S(2)}, u32[]{:S(2)}) collective-permute-start(bf16[1024,128]{1,0:T(8,128)(2,1)S(1)} %bitcast.18), channel_id=1, source_target_pairs={{8,16},{16,8},{9,17},{17,9},{10,18},{18,10},{11,19},{19,11},{12,20... | collective-permute-start | bytes 786440 | tf_op jit(solution)/shard_map/ppermute | solution.py:37
  22.1 2.4 %shard_map.60.edges = bf16[6,256,768]{2,1,0:T(8,128)(2,1)S(1)} custom-call(s32[1]{0:T(128)} %bitcast.odd, s32[8,16]{1,0:T(8,128)S(1)} %broadcast_clamp_fusion.1.at_first, s32[8,16]{1,0:T(8,128)S(1)} %broadcast_clamp_fusion.at_second, bf16[12,64,512]{2,1,0:T(8,128)(2,1)} %collective-permute-done.2.first, bf16[16,64,512]{2,1,0:T(8,128)(2,1)S(1)} %collective-permute-done.3.second), custom_call_target="tpu_custom_call" | custom-call | tf_op jit(solution)/shard_map/pallas_call | solution.py:435
  24.5 2.5 %collective-permute-done.5.x_second = bf16[1024,128]{1,0:T(8,128)(2,1)S(1)} collective-permute-done((bf16[1024,128]{1,0:T(8,128)(2,1)S(1)}, bf16[1024,128]{1,0:T(8,128)(2,1)S(1)}, u32[]{:S(2)}, u32[]{:S(2)}) %collective-permute-start.5) | collective-permute-done | bytes 262176 | tf_op jit(solution)/shard_map/ppermute | solution.py:37
  27.0 3.2 %shard_map.61 = (f32[1024,128]{1,0:T(8,128)S(1)}, f32[1536,128]{1,0:T(8,128)S(1)}, bf16[1536,128]{1,0:T(8,128)(2,1)S(1)}) custom-call(s32[1]{0:T(128)} %bitcast.odd, bf16[4,256,768]{2,1,0:T(8,128)(2,1)S(1)} %get-tuple-element.17.own, bf16[6,256,768]{2,1,0:T(8,128)(2,1)S(1)} %shard_map.60.edges, bf16[1024,128]{1,0:T(8,128)(2,1)S(1)} %collective-permute-done.4.x_first, ...), custom_call_target="tpu_custom_call" | custom-call | tf_op jit(solution)/shard_map/pallas_call | solution.py:458
  30.3 2.7 %collective-permute-start.7 = (bf16[1536,128]{1,0:T(8,128)(2,1)S(1)}, bf16[1536,128]{1,0:T(8,128)(2,1)S(1)}, u32[]{:S(2)}, u32[]{:S(2)}) collective-permute-start(bf16[1536,128]{1,0:T(8,128)(2,1)S(1)} %get-tuple-element.22), channel_id=1, source_target_pairs={{8,16},{16,8},{9,17},{17,9},{10,18},{18,10},{11,19},{19,11},{12,20... | collective-permute-start | bytes 1179656 | tf_op jit(solution)/shard_map/ppermute | solution.py:37
  33.1 6.6 %collective-permute-done.7.got_second = bf16[1536,128]{1,0:T(8,128)(2,1)S(1)} collective-permute-done((bf16[1536,128]{1,0:T(8,128)(2,1)S(1)}, bf16[1536,128]{1,0:T(8,128)(2,1)S(1)}, u32[]{:S(2)}, u32[]{:S(2)}) %collective-permute-start.7) | collective-permute-done | bytes 393248 | tf_op jit(solution)/shard_map/ppermute | solution.py:37
  39.7 3.3 %shard_map.62.mine = bf16[1024,128]{1,0:T(8,128)(2,1)S(1)} custom-call(s32[1]{0:T(128)} %bitcast.odd, bf16[4,256,768]{2,1,0:T(8,128)(2,1)S(1)} %get-tuple-element.17.own, bf16[6,256,768]{2,1,0:T(8,128)(2,1)S(1)} %shard_map.60.edges, f32[1024,128]{1,0:T(8,128)S(1)} %get-tuple-element.20.now, f32[1536,128]{1,0:T(8,128)S(1)} %get-tuple-element.21.last, ...), custom_call_target="tpu_custom_call" | custom-call | tf_op jit(solution)/shard_map/pallas_call | solution.py:472
  43.0 1.2 %collective-permute-start.8 = (bf16[1024,128]{1,0:T(8,128)(2,1)S(1)}, bf16[1024,128]{1,0:T(8,128)(2,1)S(1)}, u32[]{:S(2)}, u32[]{:S(2)}) collective-permute-start(bf16[1024,128]{1,0:T(8,128)(2,1)S(1)} %shard_map.62.mine), channel_id=1, source_target_pairs={{0,2},{2,4},{4,6},{6,7},{7,5},{5,3},{3,1},{1,0},{8,10},{10,12},{12... | collective-permute-start | bytes 786440 | tf_op jit(solution)/shard_map/ppermute | solution.py:306
  44.5 2.0 %collective-permute-start.10 = (bf16[1024,128]{1,0:T(8,128)(2,1)S(1)}, bf16[1024,128]{1,0:T(8,128)(2,1)S(1)}, u32[]{:S(2)}, u32[]{:S(2)}) collective-permute-start(bf16[1024,128]{1,0:T(8,128)(2,1)S(1)} %shard_map.62.mine), channel_id=1, source_target_pairs={{0,4},{2,6},{4,7},{6,5},{7,3},{5,1},{3,0},{1,2},{8,12},{10,14},{12... | collective-permute-start | bytes 786440 | tf_op jit(solution)/shard_map/ppermute | solution.py:306
  46.9 2.1 %collective-permute-done.8.refs_0_ = bf16[1024,128]{1,0:T(8,128)(2,1)S(1)} collective-permute-done((bf16[1024,128]{1,0:T(8,128)(2,1)S(1)}, bf16[1024,128]{1,0:T(8,128)(2,1)S(1)}, u32[]{:S(2)}, u32[]{:S(2)}) %collective-permute-start.8) | collective-permute-done | bytes 262176 | tf_op jit(solution)/shard_map/ppermute | solution.py:306
  49.0 2.1 %collective-permute-done.9.refs_1_ = bf16[1024,128]{1,0:T(8,128)(2,1)S(1)} collective-permute-done((bf16[1024,128]{1,0:T(8,128)(2,1)S(1)}, bf16[1024,128]{1,0:T(8,128)(2,1)S(1)}, u32[]{:S(2)}, u32[]{:S(2)}) %collective-permute-start.9) | collective-permute-done | bytes 262176 | tf_op jit(solution)/shard_map/ppermute | solution.py:306
  51.6 3.2 %collective-permute-done.10.back.refs_2_ = bf16[1024,128]{1,0:T(8,128)(2,1)S(1)} collective-permute-done((bf16[1024,128]{1,0:T(8,128)(2,1)S(1)}, bf16[1024,128]{1,0:T(8,128)(2,1)S(1)}, u32[]{:S(2)}, u32[]{:S(2)}) %collective-permute-start.10) | collective-permute-done | bytes 262176 | tf_op jit(solution)/shard_map/ppermute | solution.py:306
  54.8 0.9 %collective-permute-done.11.front.refs_3_ = bf16[1024,128]{1,0:T(8,128)(2,1)S(1)} collective-permute-done((bf16[1024,128]{1,0:T(8,128)(2,1)S(1)}, bf16[1024,128]{1,0:T(8,128)(2,1)S(1)}, u32[]{:S(2)}, u32[]{:S(2)}) %collective-permute-start.11) | collective-permute-done | bytes 262176 | tf_op jit(solution)/shard_map/ppermute | solution.py:306
  55.7 0.9 %shard_map.64 = (bf16[256,128]{1,0:T(8,128)(2,1)S(1)}, bf16[256,128]{1,0:T(8,128)(2,1)S(1)}, bf16[256,128]{1,0:T(8,128)(2,1)S(1)}) custom-call(s32[8]{0:T(128)S(1)} %compare_select_fusion.2.where, bf16[3,128,1024]{2,1,0:T(8,128)(2,1)S(1)} %get-tuple-element.23.lefts, bf16[1024,128]{1,0:T(8,128)(2,1)S(1)} %collective-permute-done.10.back.refs_2_, ...), custom_call_target="tpu_custom_call" | custom-call | tf_op jit(solution)/shard_map/pallas_call | solution.py:334
  57.0 1.8 %collective-permute-start.15 = (bf16[256,128]{1,0:T(8,128)(2,1)S(1)}, bf16[256,128]{1,0:T(8,128)(2,1)S(1)}, u32[]{:S(2)}, u32[]{:S(2)}) collective-permute-start(bf16[256,128]{1,0:T(8,128)(2,1)S(1)} %get-tuple-element.25._), channel_id=1, source_target_pairs={{0,3},{2,1},{4,0},{6,2},{7,4},{5,6},{3,7},{1,5},{8,11},{10,9},{12,... | collective-permute-start | bytes 196616 | tf_op jit(solution)/shard_map/ppermute | solution.py:306
  58.8 1.7 %collective-permute-start.13 = (bf16[256,128]{1,0:T(8,128)(2,1)S(1)}, bf16[256,128]{1,0:T(8,128)(2,1)S(1)}, u32[]{:S(2)}, u32[]{:S(2)}) collective-permute-start(bf16[256,128]{1,0:T(8,128)(2,1)S(1)} %get-tuple-element.26), channel_id=1, source_target_pairs={{0,2},{2,4},{4,6},{6,7},{7,5},{5,3},{3,1},{1,0},{8,10},{10,12},{12... | collective-permute-start | bytes 196616 | tf_op jit(solution)/shard_map/ppermute | solution.py:306
  60.5 1.7 %collective-permute-done.13.refs_4_ = bf16[256,128]{1,0:T(8,128)(2,1)S(1)} collective-permute-done((bf16[256,128]{1,0:T(8,128)(2,1)S(1)}, bf16[256,128]{1,0:T(8,128)(2,1)S(1)}, u32[]{:S(2)}, u32[]{:S(2)}) %collective-permute-start.13) | collective-permute-done | bytes 65568 | tf_op jit(solution)/shard_map/ppermute | solution.py:306
  62.3 1.9 %collective-permute-done.14.refs_5_ = bf16[256,128]{1,0:T(8,128)(2,1)S(1)} collective-permute-done((bf16[256,128]{1,0:T(8,128)(2,1)S(1)}, bf16[256,128]{1,0:T(8,128)(2,1)S(1)}, u32[]{:S(2)}, u32[]{:S(2)}) %collective-permute-start.14) | collective-permute-done | bytes 65568 | tf_op jit(solution)/shard_map/ppermute | solution.py:306
  64.2 1.7 %collective-permute-start.18 = (f32[3,64,128]{2,1,0:T(8,128)S(1)}, f32[3,64,128]{2,1,0:T(8,128)S(1)}, u32[]{:S(2)}, u32[]{:S(2)}) collective-permute-start(f32[3,64,128]{2,1,0:T(8,128)S(1)} %constant_dynamic-slice_fusion), channel_id=1, source_target_pairs={{0,8},{8,0},{16,24},{24,16},{1,9},{9,1},{17,25},{25,17},{2,10},{10... | collective-permute-start | bytes 294920 | tf_op jit(solution)/shard_map/ppermute | solution.py:32
  65.9 0.7 collective-permute-start.16
  66.8 0.8 %collective-permute-start.19 = (bf16[3,64,128]{2,1,0:T(8,128)(2,1)S(1)}, bf16[3,64,128]{2,1,0:T(8,128)(2,1)S(1)}, u32[]{:S(2)}, u32[]{:S(2)}) collective-permute-start(bf16[3,64,128]{2,1,0:T(8,128)(2,1)S(1)} %add_convert_fusion.1), channel_id=1, source_target_pairs={{0,16},{8,24},{16,0},{24,8},{1,17},{9,25},{17,1},{25,9},{2,18},{10... | collective-permute-start | bytes 147464 | tf_op jit(solution)/shard_map/ppermute | solution.py:390
  67.6 2.3 %collective-permute-done.16 = bf16[5,64,128]{2,1,0:T(8,128)(2,1)S(1)} collective-permute-done((bf16[5,64,128]{2,1,0:T(8,128)(2,1)S(1)}, bf16[5,64,128]{2,1,0:T(8,128)(2,1)S(1)}, u32[]{:S(2)}, u32[]{:S(2)}) %collective-permute-start.16) | collective-permute-done | bytes 81952 | tf_op jit(solution)/shard_map/ppermute | solution.py:390
  69.9 1.4 %collective-permute-start.17 = (f32[5,64,128]{2,1,0:T(8,128)S(1)}, f32[5,64,128]{2,1,0:T(8,128)S(1)}, u32[]{:S(2)}, u32[]{:S(2)}) collective-permute-start(f32[5,64,128]{2,1,0:T(8,128)S(1)} %convert_add_fusion.refs_0_), channel_id=1, source_target_pairs={{0,8},{8,0},{16,24},{24,16},{1,9},{9,1},{17,25},{25,17},{2,10},{10... | collective-permute-start | bytes 491528 | tf_op jit(solution)/shard_map/ppermute | solution.py:32
  71.9 1.3 %shard_map.66 = bf16[128,1024]{1,0:T(8,128)(2,1)} custom-call(s32[8]{0:T(128)S(1)} %compare_select_fusion.2.where, bf16[1024,128]{1,0:T(8,128)(2,1)S(1)} %shard_map.62.mine, bf16[1024,128]{1,0:T(8,128)(2,1)S(1)} %collective-permute-done.8.refs_0_, bf16[1024,128]{1,0:T(8,128)(2,1)S(1)} %collective-permute-done.9.refs_1_, ...), custom_call_target="tpu_custom_call" | custom-call | tf_op jit(solution)/shard_map/pallas_call | solution.py:355
  73.2 1.4 %shard_map.67 = f32[128,1024]{1,0:T(8,128)} custom-call(s32[8]{0:T(128)S(1)} %compare_select_fusion.2.where, s32[1]{0:T(128)} %bitcast.odd, f32[5,64,128]{2,1,0:T(8,128)S(1)} %convert_add_fusion.refs_0_, f32[5,64,128]{2,1,0:T(8,128)S(1)} %collective-permute-done.17.refs_1_, f32[3,64,128]{2,1,0:T(8,128)S(1)} %convert_add_fusion.1.refs_2_, ...), custom_call_target="tpu_custom_call" | custom-call | tf_op jit(solution)/shard_map/pallas_call | solution.py:364
  (42 shorter events, 3.8 us)
Async XLA Ops:
  0.6 4.7 %copy-start = (bf16[128,1024]{1,0:T(8,128)(2,1)S(1)}, bf16[128,1024]{1,0:T(8,128)(2,1)}, u32[]{:S(2)}) copy-start(bf16[128,1024]{1,0:T(8,128)(2,1)} %param.4) | copy-start | bytes 786436
  0.6 21.5 %collective-permute-start.3 = (bf16[16,64,512]{2,1,0:T(8,128)(2,1)}, bf16[16,64,512]{2,1,0:T(8,128)(2,1)S(1)}, u32[]{:S(2)}, u32[]{:S(2)}) collective-permute-start(bf16[16,64,512]{2,1,0:T(8,128)(2,1)} %tiles.1), channel_id=1, source_target_pairs={{8,16},{16,8},{9,17},{17,9},{10,18},{18,10},{11,19},{19,11},{12,20... | collective-permute-start | bytes 3145736 | tf_op jit(solution)/shard_map/ppermute | solution.py:37
  6.1 13.3 %all-to-all-start = ((bf16[128,8,128]{2,0,1:T(8,128)(2,1)}), bf16[128,8,128]{2,0,1:T(8,128)(2,1)S(1)}, u32[]{:S(2)}, u32[]{:S(2)}) async-start(bf16[128,8,128]{2,0,1:T(8,128)(2,1)} %copy_bitcast_fusion), calls=%async_computation | async-start | bytes 524288 | tf_op jit(solution)/shard_map/all_to_all | solution.py:407
  12.3 1.2 %copy-start.1 = (bf16[16,64,512]{2,1,0:T(8,128)(2,1)S(1)}, bf16[16,64,512]{2,1,0:T(8,128)(2,1)}, u32[]{:S(2)}) copy-start(bf16[16,64,512]{2,1,0:T(8,128)(2,1)} %tiles.1) | copy-start | bytes 3145732
  15.9 6.2 %collective-permute-start.2 = (bf16[12,64,512]{2,1,0:T(8,128)(2,1)}, bf16[12,64,512]{2,1,0:T(8,128)(2,1)}, u32[]{:S(2)}, u32[]{:S(2)}) collective-permute-start(bf16[12,64,512]{2,1,0:T(8,128)(2,1)} %get-tuple-element.19), channel_id=1, source_target_pairs={{0,8},{8,0},{16,24},{24,16},{1,9},{9,1},{17,25},{25,17},{2,10},{10... | collective-permute-start | bytes 2359304 | tf_op jit(solution)/shard_map/ppermute | solution.py:32
  15.9 3.4 %collective-permute-start = (s32[8,16]{1,0:T(8,128)S(1)}, s32[8,16]{1,0:T(8,128)S(1)}, u32[]{:S(2)}, u32[]{:S(2)}) collective-permute-start(s32[8,16]{1,0:T(8,128)S(1)} %get-tuple-element.18), channel_id=1, source_target_pairs={{0,8},{8,0},{16,24},{24,16},{1,9},{9,1},{17,25},{25,17},{2,10},{10... | collective-permute-start | bytes 1544 | tf_op jit(solution)/shard_map/ppermute | solution.py:32
  16.4 5.7 %collective-permute-start.1 = (s32[8,16]{1,0:T(8,128)S(1)}, s32[8,16]{1,0:T(8,128)S(1)}, u32[]{:S(2)}, u32[]{:S(2)}) collective-permute-start(s32[8,16]{1,0:T(8,128)S(1)} %get-tuple-element.18), channel_id=1, source_target_pairs={{8,16},{16,8},{9,17},{17,9},{10,18},{18,10},{11,19},{19,11},{12,20... | collective-permute-start | bytes 1544 | tf_op jit(solution)/shard_map/ppermute | solution.py:37
  19.3 5.2 %collective-permute-start.4 = (bf16[1024,128]{1,0:T(8,128)(2,1)S(1)}, bf16[1024,128]{1,0:T(8,128)(2,1)S(1)}, u32[]{:S(2)}, u32[]{:S(2)}) collective-permute-start(bf16[1024,128]{1,0:T(8,128)(2,1)S(1)} %bitcast.17), channel_id=1, source_target_pairs={{0,8},{8,0},{16,24},{24,16},{1,9},{9,1},{17,25},{25,17},{2,10},{10... | collective-permute-start | bytes 786440 | tf_op jit(solution)/shard_map/ppermute | solution.py:32
  19.3 7.7 %collective-permute-start.5 = (bf16[1024,128]{1,0:T(8,128)(2,1)S(1)}, bf16[1024,128]{1,0:T(8,128)(2,1)S(1)}, u32[]{:S(2)}, u32[]{:S(2)}) collective-permute-start(bf16[1024,128]{1,0:T(8,128)(2,1)S(1)} %bitcast.18), channel_id=1, source_target_pairs={{8,16},{16,8},{9,17},{17,9},{10,18},{18,10},{11,19},{19,11},{12,20... | collective-permute-start | bytes 786440 | tf_op jit(solution)/shard_map/ppermute | solution.py:37
  30.2 2.8 %collective-permute-start.6 = (bf16[1536,128]{1,0:T(8,128)(2,1)S(1)}, bf16[1536,128]{1,0:T(8,128)(2,1)S(1)}, u32[]{:S(2)}, u32[]{:S(2)}) collective-permute-start(bf16[1536,128]{1,0:T(8,128)(2,1)S(1)} %get-tuple-element.22), channel_id=1, source_target_pairs={{0,8},{8,0},{16,24},{24,16},{1,9},{9,1},{17,25},{25,17},{2,10},{10... | collective-permute-start | bytes 1179656 | tf_op jit(solution)/shard_map/ppermute | solution.py:32
  30.3 9.4 %collective-permute-start.7 = (bf16[1536,128]{1,0:T(8,128)(2,1)S(1)}, bf16[1536,128]{1,0:T(8,128)(2,1)S(1)}, u32[]{:S(2)}, u32[]{:S(2)}) collective-permute-start(bf16[1536,128]{1,0:T(8,128)(2,1)S(1)} %get-tuple-element.22), channel_id=1, source_target_pairs={{8,16},{16,8},{9,17},{17,9},{10,18},{18,10},{11,19},{19,11},{12,20... | collective-permute-start | bytes 1179656 | tf_op jit(solution)/shard_map/ppermute | solution.py:37
  39.7 7.2 %copy-start.2 = (s32[8]{0:T(128)S(1)}, s32[8]{0:T(128)}, u32[]{:S(2)}) copy-start(s32[8]{0:T(128)} %constant.67.clone) | copy-start | bytes 100
  43.0 6.0 %collective-permute-start.8 = (bf16[1024,128]{1,0:T(8,128)(2,1)S(1)}, bf16[1024,128]{1,0:T(8,128)(2,1)S(1)}, u32[]{:S(2)}, u32[]{:S(2)}) collective-permute-start(bf16[1024,128]{1,0:T(8,128)(2,1)S(1)} %shard_map.62.mine), channel_id=1, source_target_pairs={{0,2},{2,4},{4,6},{6,7},{7,5},{5,3},{3,1},{1,0},{8,10},{10,12},{12... | collective-permute-start | bytes 786440 | tf_op jit(solution)/shard_map/ppermute | solution.py:306
  44.2 7.0 %collective-permute-start.9 = (bf16[1024,128]{1,0:T(8,128)(2,1)S(1)}, bf16[1024,128]{1,0:T(8,128)(2,1)S(1)}, u32[]{:S(2)}, u32[]{:S(2)}) collective-permute-start(bf16[1024,128]{1,0:T(8,128)(2,1)S(1)} %shard_map.62.mine), channel_id=1, source_target_pairs={{0,1},{2,0},{4,2},{6,4},{7,6},{5,7},{3,5},{1,3},{8,9},{10,8},{12,1... | collective-permute-start | bytes 786440 | tf_op jit(solution)/shard_map/ppermute | solution.py:306
  44.5 10.3 %collective-permute-start.10 = (bf16[1024,128]{1,0:T(8,128)(2,1)S(1)}, bf16[1024,128]{1,0:T(8,128)(2,1)S(1)}, u32[]{:S(2)}, u32[]{:S(2)}) collective-permute-start(bf16[1024,128]{1,0:T(8,128)(2,1)S(1)} %shard_map.62.mine), channel_id=1, source_target_pairs={{0,4},{2,6},{4,7},{6,5},{7,3},{5,1},{3,0},{1,2},{8,12},{10,14},{12... | collective-permute-start | bytes 786440 | tf_op jit(solution)/shard_map/ppermute | solution.py:306
  46.5 9.2 %collective-permute-start.11 = (bf16[1024,128]{1,0:T(8,128)(2,1)S(1)}, bf16[1024,128]{1,0:T(8,128)(2,1)S(1)}, u32[]{:S(2)}, u32[]{:S(2)}) collective-permute-start(bf16[1024,128]{1,0:T(8,128)(2,1)S(1)} %shard_map.62.mine), channel_id=1, source_target_pairs={{0,3},{2,1},{4,0},{6,2},{7,4},{5,6},{3,7},{1,5},{8,11},{10,9},{12,... | collective-permute-start | bytes 786440 | tf_op jit(solution)/shard_map/ppermute | solution.py:306
  56.9 3.6 %collective-permute-start.12 = (f32[5,64,128]{2,1,0:T(8,128)S(1)}, f32[5,64,128]{2,1,0:T(8,128)S(1)}, u32[]{:S(2)}, u32[]{:S(2)}) collective-permute-start(f32[5,64,128]{2,1,0:T(8,128)S(1)} %constant_dynamic-slice_fusion.1), channel_id=1, source_target_pairs={{0,8},{8,0},{16,24},{24,16},{1,9},{9,1},{17,25},{25,17},{2,10},{10... | collective-permute-start | bytes 491528 | tf_op jit(solution)/shard_map/ppermute | solution.py:32
  57.0 7.1 %collective-permute-start.15 = (bf16[256,128]{1,0:T(8,128)(2,1)S(1)}, bf16[256,128]{1,0:T(8,128)(2,1)S(1)}, u32[]{:S(2)}, u32[]{:S(2)}) collective-permute-start(bf16[256,128]{1,0:T(8,128)(2,1)S(1)} %get-tuple-element.25._), channel_id=1, source_target_pairs={{0,3},{2,1},{4,0},{6,2},{7,4},{5,6},{3,7},{1,5},{8,11},{10,9},{12,... | collective-permute-start | bytes 196616 | tf_op jit(solution)/shard_map/ppermute | solution.py:306
  58.8 3.5 %collective-permute-start.13 = (bf16[256,128]{1,0:T(8,128)(2,1)S(1)}, bf16[256,128]{1,0:T(8,128)(2,1)S(1)}, u32[]{:S(2)}, u32[]{:S(2)}) collective-permute-start(bf16[256,128]{1,0:T(8,128)(2,1)S(1)} %get-tuple-element.26), channel_id=1, source_target_pairs={{0,2},{2,4},{4,6},{6,7},{7,5},{5,3},{3,1},{1,0},{8,10},{10,12},{12... | collective-permute-start | bytes 196616 | tf_op jit(solution)/shard_map/ppermute | solution.py:306
  60.5 3.7 %collective-permute-start.14 = (bf16[256,128]{1,0:T(8,128)(2,1)S(1)}, bf16[256,128]{1,0:T(8,128)(2,1)S(1)}, u32[]{:S(2)}, u32[]{:S(2)}) collective-permute-start(bf16[256,128]{1,0:T(8,128)(2,1)S(1)} %get-tuple-element.27), channel_id=1, source_target_pairs={{0,1},{2,0},{4,2},{6,4},{7,6},{5,7},{3,5},{1,3},{8,9},{10,8},{12,1... | collective-permute-start | bytes 196616 | tf_op jit(solution)/shard_map/ppermute | solution.py:306
  64.2 2.6 %collective-permute-start.18 = (f32[3,64,128]{2,1,0:T(8,128)S(1)}, f32[3,64,128]{2,1,0:T(8,128)S(1)}, u32[]{:S(2)}, u32[]{:S(2)}) collective-permute-start(f32[3,64,128]{2,1,0:T(8,128)S(1)} %constant_dynamic-slice_fusion), channel_id=1, source_target_pairs={{0,8},{8,0},{16,24},{24,16},{1,9},{9,1},{17,25},{25,17},{2,10},{10... | collective-permute-start | bytes 294920 | tf_op jit(solution)/shard_map/ppermute | solution.py:32
  65.9 4.0 %collective-permute-start.16 = (bf16[5,64,128]{2,1,0:T(8,128)(2,1)S(1)}, bf16[5,64,128]{2,1,0:T(8,128)(2,1)S(1)}, u32[]{:S(2)}, u32[]{:S(2)}) collective-permute-start(bf16[5,64,128]{2,1,0:T(8,128)(2,1)S(1)} %add_convert_fusion), channel_id=1, source_target_pairs={{0,16},{8,24},{16,0},{24,8},{1,17},{9,25},{17,1},{25,9},{2,18},{10... | collective-permute-start | bytes 245768 | tf_op jit(solution)/shard_map/ppermute | solution.py:390
  66.8 4.5 %collective-permute-start.19 = (bf16[3,64,128]{2,1,0:T(8,128)(2,1)S(1)}, bf16[3,64,128]{2,1,0:T(8,128)(2,1)S(1)}, u32[]{:S(2)}, u32[]{:S(2)}) collective-permute-start(bf16[3,64,128]{2,1,0:T(8,128)(2,1)S(1)} %add_convert_fusion.1), channel_id=1, source_target_pairs={{0,16},{8,24},{16,0},{24,8},{1,17},{9,25},{17,1},{25,9},{2,18},{10... | collective-permute-start | bytes 147464 | tf_op jit(solution)/shard_map/ppermute | solution.py:390
  69.9 3.3 %collective-permute-start.17 = (f32[5,64,128]{2,1,0:T(8,128)S(1)}, f32[5,64,128]{2,1,0:T(8,128)S(1)}, u32[]{:S(2)}, u32[]{:S(2)}) collective-permute-start(f32[5,64,128]{2,1,0:T(8,128)S(1)} %convert_add_fusion.refs_0_), channel_id=1, source_target_pairs={{0,8},{8,0},{16,24},{24,16},{1,9},{9,1},{17,25},{25,17},{2,10},{10... | collective-permute-start | bytes 491528 | tf_op jit(solution)/shard_map/ppermute | solution.py:32
  71.3 1.9 %collective-permute-start.20 = (f32[3,64,128]{2,1,0:T(8,128)S(1)}, f32[3,64,128]{2,1,0:T(8,128)S(1)}, u32[]{:S(2)}, u32[]{:S(2)}) collective-permute-start(f32[3,64,128]{2,1,0:T(8,128)S(1)} %convert_add_fusion.1.refs_2_), channel_id=1, source_target_pairs={{0,8},{8,0},{16,24},{24,16},{1,9},{9,1},{17,25},{25,17},{2,10},{10... | collective-permute-start | bytes 294920 | tf_op jit(solution)/shard_map/ppermute | solution.py:32
